TPU v7x, 32 devices: a whole 2x2x4 slice. The times are simulated.
32 devices in a mesh: bins: 8 (over z, y), chan: 4 (over x, core).
Axes of the slice: x: 2, y: 2, z: 4, core: 2. Of those that a mesh axis runs over, the one named last changes fastest.
Arguments:
- tokens_in: bfloat16 [4096, 2048], P('bins', 'chan'), may hold values from -6 to 6
- filters: bfloat16 [4096, 2048], P('bins', 'chan'), may hold values from -0.09375 to 0.09375
- gate: bfloat16 [4096, 2048], P('bins', 'chan'), may hold values from -6 to 6
- skip: float32 [2048], P('chan'), may hold values from 0.5 to 1.5
- out_grad: bfloat16 [4096, 4096], P('bins', 'chan'), may hold values from -6 to 6
- out_weight: bfloat16 [2048, 4096], P('chan'), may hold values from -0.09375 to 0.09375
- owner: int32 [8, 512], P(None, 'bins'), may hold values from 0 to 7, as said below
- slot: int32 [8, 512], P(None, 'bins'), may hold values from 0 to 1023, as said below
Outputs:
- gate_grad: bfloat16 [8, 512, 2048], P(None, 'bins', 'chan')
- filter_grad: float32 [8, 512, 2048], P(None, 'bins', 'chan')
- grad_rows: bfloat16 [8192, 2048], P('bins', 'chan')
Inputs may be any that keep to these rules, and one draw needn't show every extreme that they name: Let the column group j be the entries [i, r] with j * 64 <= r < (j + 1) * 64, all i. Within one column group at most 128 entries name the same owner, and in every draw some owner is named exactly 128 times by every column group. An entry of column group j (as for owner) lies in j * 128 to (j + 1) * 128 - 1; no two tokens share an owner and a slot; in every draw some owner has all 1024 slots used.
All inputs are finite; a program needn't handle non-finite values.
Results may differ from a plain program's by a relative error of at most 0.012.
Values may be sent and summed in bfloat16 or wider, within the bound.
No kernel may reach another device: no remote copies, remote signals or barrier semaphores. Data moves between devices by JAX's collectives and lax.ppermute only.
A program may use at most 128 MiB of HBM per device.

v0:
```python
import math

import jax
import jax.numpy as jnp
from jax import lax
from jax.sharding import PartitionSpec as P

exact_mode = lax.Precision.HIGHEST


def angles(index, period):
    return 2.0 * math.pi / period * (index % period).astype(jnp.float32)


def contract(table, values, form):
    return jnp.einsum(form, table, values, precision=exact_mode)


def product(left_re, left_im, right_re, right_im):
    return (left_re * right_re - left_im * right_im, left_re * right_im + left_im * right_re)


def shards(tokens_in, filters, gate, skip, out_grad, out_weight, owner, slot):
    blocks = lax.axis_size("bins")
    my_index = lax.axis_index("bins")
    tok_rows, channels = tokens_in.shape
    col_rows = tok_rows // blocks
    length = 2 * blocks * tok_rows
    block_ids = jnp.arange(blocks, dtype=jnp.int32)
    bin_order = jnp.stack(
        [block_ids, jnp.where(block_ids == 0, blocks, 2 * blocks - block_ids)], axis=1
    ).reshape(2 * blocks)
    block_angle = angles(bin_order[:, None] * block_ids[None, :], 2 * blocks)
    block_cos = jnp.cos(block_angle)
    block_sin = jnp.sin(block_angle)
    back_cos = block_cos.T
    back_sin = block_sin.T
    column_ids = my_index * col_rows + jnp.arange(col_rows, dtype=jnp.int32)
    ahead_angle = angles(bin_order[:, None] * column_ids[None, :], length)[:, :, None]
    ahead_cos = jnp.cos(ahead_angle)
    ahead_sin = jnp.sin(ahead_angle)
    own_bins = lax.dynamic_slice_in_dim(bin_order, 2 * my_index, 2)
    positions = jnp.arange(tok_rows, dtype=jnp.int32)
    return_angle = angles(own_bins[:, None] * positions[None, :], length)[:, :, None]
    return_cos = jnp.cos(return_angle)
    return_sin = jnp.sin(return_angle)
    inner_angle = angles(positions[:, None] * positions[None, :], tok_rows)
    inner_cos = jnp.cos(inner_angle)
    inner_sin = jnp.sin(inner_angle)
    upstream = lax.dot_general(
        lax.all_gather(out_grad, "chan", axis=1, tiled=True),
        out_weight,
        (((1,), (1,)), ((), ())),
        preferred_element_type=jnp.float32,
    )
    g_rounded = upstream.astype(jnp.bfloat16)
    grad_in = (g_rounded.astype(jnp.float32) * gate.astype(jnp.float32)).astype(jnp.bfloat16)
    grid_shape = (blocks, col_rows, channels)
    tok_cols, filt_cols, grad_cols, gout_cols = (
        lax.all_to_all(
            tokens_in.reshape(grid_shape), "bins", split_axis=0, concat_axis=0, tiled=True
        ),
        lax.all_to_all(
            filters.reshape(grid_shape), "bins", split_axis=0, concat_axis=0, tiled=True
        ),
        lax.all_to_all(
            grad_in.reshape(grid_shape), "bins", split_axis=0, concat_axis=0, tiled=True
        ),
        lax.all_to_all(
            g_rounded.reshape(grid_shape), "bins", split_axis=0, concat_axis=0, tiled=True
        ),
    )
    tok_real = tok_cols.astype(jnp.float32)
    filt_real = filt_cols.astype(jnp.float32)
    grad_real = grad_cols.astype(jnp.float32)
    real_stack = jnp.stack([tok_real, filt_real, grad_real])
    part_re = contract(block_cos, real_stack, "ki,sirc->skrc")
    part_im = -contract(block_sin, real_stack, "ki,sirc->skrc")
    turned = jnp.stack(
        [part_re * ahead_cos + part_im * ahead_sin, part_im * ahead_cos - part_re * ahead_sin],
        axis=1,
    )
    arrived = lax.all_to_all(turned, "bins", split_axis=2, concat_axis=3, tiled=True)
    came_re = arrived[:, 0]
    came_im = arrived[:, 1]
    spec_re = contract(inner_cos, came_re, "kr,slrc->slkc") + contract(
        inner_sin, came_im, "kr,slrc->slkc"
    )
    spec_im = contract(inner_cos, came_im, "kr,slrc->slkc") - contract(
        inner_sin, came_re, "kr,slrc->slkc"
    )
    spec_re, spec_im = (spec_re, spec_im)
    x_re, x_im = (spec_re[0], spec_im[0])
    h_re, h_im = (spec_re[1], spec_im[1])
    y_re, y_im = (spec_re[2], spec_im[2])
    conv_re, conv_im = product(x_re, x_im, h_re, h_im)
    back_re, back_im = product(h_re, -h_im, y_re, y_im)
    lag_re, lag_im = product(y_re, y_im, x_re, -x_im)
    freq_re = jnp.stack([conv_re, back_re, lag_re])
    freq_im = jnp.stack([conv_im, back_im, lag_im])
    sum_re = contract(inner_cos, freq_re, "rk,slkc->slrc") - contract(
        inner_sin, freq_im, "rk,slkc->slrc"
    )
    sum_im = contract(inner_cos, freq_im, "rk,slkc->slrc") + contract(
        inner_sin, freq_re, "rk,slkc->slrc"
    )
    twist_re = sum_re * return_cos - sum_im * return_sin
    twist_im = sum_re * return_sin + sum_im * return_cos
    turned = jnp.stack([twist_re, twist_im], axis=1)
    arrived = lax.all_to_all(turned, "bins", split_axis=3, concat_axis=2, tiled=True)
    came_re = arrived[:, 0]
    came_im = arrived[:, 1]
    out_re = contract(back_cos, came_re, "ik,skrc->sirc") - contract(
        back_sin, came_im, "ik,skrc->sirc"
    )
    result_re = out_re / length
    conv = result_re[0]
    backward = result_re[1]
    lagged = result_re[2]
    gate_grad = (gout_cols.astype(jnp.float32) * (conv + skip * tok_real)).astype(jnp.bfloat16)
    filter_grad = lagged / math.sqrt(blocks * tok_rows)
    token_grad = (backward + skip * grad_real).astype(jnp.bfloat16)
    send_rows = 2 * tok_rows // blocks
    targets = owner.reshape(-1) * send_rows + slot.reshape(-1) - my_index * send_rows
    outbox = (
        jnp.zeros((blocks * send_rows, channels), jnp.bfloat16)
        .at[targets]
        .set(token_grad.reshape(tok_rows, channels))
    )
    inbox = lax.all_to_all(
        outbox.reshape(blocks, send_rows, channels), "bins", split_axis=0, concat_axis=0, tiled=True
    )
    grad_rows = inbox.reshape(blocks * send_rows, channels)
    return (gate_grad, filter_grad, grad_rows)


def solution(mesh):
    return jax.shard_map(
        shards,
        mesh=mesh,
        in_specs=(
            P("bins", "chan"),
            P("bins", "chan"),
            P("bins", "chan"),
            P("chan"),
            P("bins", "chan"),
            P("chan", None),
            P(None, "bins"),
            P(None, "bins"),
        ),
        out_specs=(P(None, "bins", "chan"), P(None, "bins", "chan"), P("bins", "chan")),
        check_vma=False,
    )
```

profile of v0, /device:TPU:0, one launch (start us, length us, event | category | flops | bytes accessed | tf_op | source)
XLA Modules:
  0.0 1024.5 jit_solution(9164600726779022838)
XLA Ops:
  7.9 21.8 %all_to_all.61 = bf16[8,64,512]{2,1,0:T(8,128)(2,1)S(1)} all-to-all(bf16[8,64,512]{2,1,0:T(8,128)(2,1)} %bitcast.142), channel_id=1, replica_groups=mesh['bins'=8,'chan'=4] {'bins'}, dimensions={0} | all-to-all | bytes 1048576 | tf_op jit(solution)/shard_map/all_to_all | solution.py:60
  33.3 13.5 %all-gather.2.cloned.1.call-done = bf16[512,4096]{1,0:T(8,128)(2,1)} async-done(((bf16[512,1024]{1,0:T(8,128)(2,1)}), bf16[512,4096]{1,0:T(8,128)(2,1)}) %all-gather.2.cloned.1.call-update) | async-done | bytes 4194320 | tf_op jit(solution)/shard_map/all_gather | solution.py:51
  46.8 6.8 multiply_convert_fusion
  60.4 13.8 %all-to-all-done.3 = bf16[8,64,512]{2,1,0:T(8,128)(2,1)S(1)} async-done(((bf16[8,64,512]{2,1,0:T(8,128)(2,1)}), bf16[8,64,512]{2,1,0:T(8,128)(2,1)S(1)}, u32[]{:S(2)}, u32[]{:S(2)}) %all-to-all-start.3) | async-done | bytes 524320 | tf_op jit(solution)/shard_map/all_to_all | solution.py:66
  80.7 10.8 %fusion.3 = (f32[3,1,16,64,512]{4,2,3,0,1:T(8,128)S(1)}, f32[3,1,16,64,512]{4,2,3,0,1:T(8,128)}) fusion(f32[3,64,512,16]{2,3,1,0:T(8,128)S(1)} %fusion.14, f32[16,64]{0,1:T(8,128)S(1)} %get-tuple-element.28, f32[16,64]{0,1:T(8,128)S(1)} %get-tuple-element.27, s32[16]{0:T(128)S(1)} %mul.319, f32[1,8,64,512]{3,1,2,0:T(8,128)S(1)} %convert_bitcast_fusion, ...), kind=kOutput, calls=%fused_computation.14 | convolution fusion | flops 163579648 | bytes 22028352 | tf_op jit(solution)/shard_map/ki,sirc->skrc/dot_general | solution.py:16
  91.5 9.5 pad_maximum_fusion
  101.1 16.4 %copy.48 = f32[3,2,16,64,512]{4,3,0,1,2:T(8,128)} copy(f32[3,2,16,64,512]{4,2,3,0,1:T(8,128)} %pad_maximum_fusion) | data formatting | bytes 25165824 | tf_op jit(solution)/shard_map/stack | solution.py:79
  123.5 271.6 %all-to-all-done.4 = f32[3,2,16,64,512]{4,3,0,1,2:T(8,128)} async-done(((f32[3,2,16,64,512]{4,3,0,1,2:T(8,128)}), f32[3,2,16,64,512]{4,3,0,1,2:T(8,128)}, u32[]{:S(2)}, u32[]{:S(2)}) %all-to-all-start.4) | async-done | bytes 12582944 | tf_op jit(solution)/shard_map/all_to_all | solution.py:83
  395.0 12.0 %copy.50 = f32[3,2,2,8,64,512]{5,4,3,2,1,0:T(8,128)} copy(f32[3,2,2,8,64,512]{5,4,0,1,2,3:T(8,128)} %bitcast.17) | data formatting | bytes 25165824 | tf_op jit(solution)/shard_map/all_to_all | solution.py:83
  407.0 26.4 %fusion.7 = f32[3,2,512,512]{3,2,1,0:T(8,128)S(1)} fusion(f32[3,2,2,512,512]{4,3,2,1,0:T(8,128)} %bitcast.136), kind=kOutput, calls=%fused_computation.24 | convolution fusion | flops 9667346432 | bytes 12582912 | tf_op jit(solution)/shard_map/kr,slrc->slkc/dot_general | solution.py:16
  433.4 27.5 %fusion.6 = f32[3,2,512,512]{3,2,1,0:T(8,128)} fusion(f32[3,2,2,512,512]{4,3,2,1,0:T(8,128)S(1)} %bitcast.137), kind=kOutput, calls=%fused_computation.23 | convolution fusion | flops 9667346432 | bytes 12582912 | tf_op jit(solution)/shard_map/kr,slrc->slkc/dot_general | solution.py:16
  460.9 25.5 %add_bitcast_fusion.1 = f32[3,2,512,512]{2,3,1,0:T(8,128)S(1)} fusion(f32[3,2,512,512]{3,2,1,0:T(8,128)S(1)} %fusion.7, f32[3,2,2,512,512]{4,3,2,1,0:T(8,128)S(1)} %bitcast.138), kind=kOutput, calls=%fused_computation.22 | convolution fusion | flops 9668919296 | bytes 18874368 | tf_op jit(solution)/shard_map/kr,slrc->slkc/dot_general | solution.py:16
  486.4 30.3 %subtract_bitcast_fusion.1 = f32[3,2,512,512]{2,3,1,0:T(8,128)S(1)} fusion(f32[3,2,512,512]{3,2,1,0:T(8,128)} %fusion.6, f32[3,2,2,512,512]{4,3,2,1,0:T(8,128)S(1)} %bitcast.139), kind=kOutput, calls=%fused_computation.21 | convolution fusion | flops 9668919296 | bytes 18874368 | tf_op jit(solution)/shard_map/kr,slrc->slkc/dot_general | solution.py:16
  525.7 18.9 %fusion.11 = f32[3,2,512,512]{3,2,1,0:T(8,128)} fusion(f32[1,2,512,512]{2,3,1,0:T(8,128)} %get-tuple-element.22, f32[1,2,512,512]{2,3,1,0:T(8,128)} %get-tuple-element.21, f32[1,2,512,512]{2,3,1,0:T(8,128)} %get-tuple-element.24), kind=kOutput, calls=%fused_computation.28 | convolution fusion | flops 9670492160 | bytes 12582912 | tf_op jit(solution)/shard_map/rk,slkc->slrc/dot_general | solution.py:16
  544.6 16.1 %fusion.10 = f32[3,2,512,512]{3,2,1,0:T(8,128)} fusion(f32[1,2,512,512]{2,3,1,0:T(8,128)S(1)} %copy-done.10, f32[1,2,512,512]{2,3,1,0:T(8,128)S(1)} %copy-done.9, f32[1,2,512,512]{2,3,1,0:T(8,128)S(1)} %copy-done.11), kind=kOutput, calls=%fused_computation.27 | convolution fusion | flops 9670492160 | bytes 12582912 | tf_op jit(solution)/shard_map/rk,slkc->slrc/dot_general | solution.py:16
  560.8 15.9 %fusion.12 = f32[3,2,512,512]{3,2,1,0:T(8,128)} fusion(f32[1,2,512,512]{2,3,1,0:T(8,128)S(1)} %copy-done.5, f32[1,2,512,512]{2,3,1,0:T(8,128)S(1)} %copy-done.6, f32[1,2,512,512]{2,3,1,0:T(8,128)S(1)} %copy-done.4), kind=kOutput, calls=%fused_computation.29 | convolution fusion | flops 9670492160 | bytes 12582912 | tf_op jit(solution)/shard_map/rk,slkc->slrc/dot_general | solution.py:16
  576.6 27.5 %subtract_bitcast_fusion = (f32[3,1,2,512,512]{3,4,2,0,1:T(8,128)S(1)}, f32[3,1,2,512,512]{3,4,2,0,1:T(8,128)}) fusion(f32[2,512]{1,0:T(2,128)S(1)} %get-tuple-element.30, f32[2,512]{1,0:T(2,128)S(1)} %get-tuple-element.29, f32[3,2,512,512]{3,2,1,0:T(8,128)} %fusion.10, f32[3,2,512,512]{3,2,1,0:T(8,128)} %fusion.12, f32[3,2,512,512]{3,2,1,0:T(8,128)} %fusion.11, ...), kind=kOutput, calls=%fused_computation.20 | convolution fusion | flops 9683075072 | bytes 37756928 | tf_op jit(solution)/shard_map/rk,slkc->slrc/dot_general | solution.py:16
  604.1 8.8 pad_maximum_fusion.1
  612.9 19.3 %copy.53 = f32[3,2,2,512,512]{4,2,0,1,3:T(2,128)} copy(f32[3,2,2,512,512]{3,4,2,0,1:T(8,128)} %pad_maximum_fusion.1) | data formatting | bytes 25165824 | tf_op jit(solution)/shard_map/stack | solution.py:109
  637.8 271.3 %all-to-all-done.5 = f32[3,2,2,512,512]{4,2,0,1,3:T(2,128)} async-done(((f32[3,2,2,512,512]{4,2,0,1,3:T(2,128)}), f32[3,2,2,512,512]{4,2,0,1,3:T(2,128)}, u32[]{:S(2)}, u32[]{:S(2)}) %all-to-all-start.5) | async-done | bytes 12582944 | tf_op jit(solution)/shard_map/all_to_all | solution.py:110
  913.8 13.2 %copy.54 = f32[3,2,2,512,512]{4,3,2,1,0:T(8,128)} copy(f32[3,2,2,512,512]{4,2,0,1,3:T(2,128)} %all-to-all-done.5) | data formatting | bytes 25165824 | tf_op jit(solution)/shard_map/all_to_all | solution.py:110
  927.0 22.1 %copy.55 = f32[3,2,8,2,64,512]{5,3,2,4,0,1:T(2,128)} copy(f32[3,2,8,2,64,512]{5,4,2,3,1,0:T(8,128)} %bitcast.140) | data formatting | bytes 25165824 | tf_op jit(solution)/shard_map/all_to_all | solution.py:110
  949.0 15.8 %all_to_all.52 = f32[3,2,16,64,512]{4,2,3,0,1:T(8,128)} reshape(f32[3,2,8,2,64,512]{5,3,2,4,0,1:T(2,128)} %copy.55) | data formatting | bytes 25165824 | tf_op jit(solution)/shard_map/all_to_all | solution.py:110
  993.2 22.0 %all-to-all-done.6 = bf16[8,128,512]{2,1,0:T(8,128)(2,1)} async-done(((bf16[8,128,512]{2,1,0:T(8,128)(2,1)}), bf16[8,128,512]{2,1,0:T(8,128)(2,1)}, u32[]{:S(2)}, u32[]{:S(2)}) %all-to-all-start.6) | async-done | bytes 1048608 | tf_op jit(solution)/shard_map/all_to_all | solution.py:130
  (67 shorter events, 73.3 us)
Async XLA Ops:
  7.2 39.6 %all-gather.2.cloned.1.call-start = ((), (), s32[]{:S(2)}) async-start(), calls=%async_computation.7 | async-start | bytes 5242880 | tf_op jit(solution)/shard_map/all_gather | solution.py:51
  29.7 30.0 %copy-start.7 = (bf16[8,64,512]{2,1,0:T(8,128)(2,1)}, bf16[8,64,512]{2,1,0:T(8,128)(2,1)S(1)}, u32[]{:S(2)}) copy-start(bf16[8,64,512]{2,1,0:T(8,128)(2,1)S(1)} %all_to_all.61) | copy-start | bytes 1572868
  29.7 23.9 %all-to-all-start.2 = ((bf16[8,64,512]{2,1,0:T(8,128)(2,1)}), bf16[8,64,512]{2,1,0:T(8,128)(2,1)S(1)}, u32[]{:S(2)}, u32[]{:S(2)}) async-start(bf16[8,64,512]{2,1,0:T(8,128)(2,1)} %bitcast.143), calls=%async_computation.2 | async-start | bytes 1048576 | tf_op jit(solution)/shard_map/all_to_all | solution.py:63
  53.6 20.6 %all-to-all-start.3 = ((bf16[8,64,512]{2,1,0:T(8,128)(2,1)}), bf16[8,64,512]{2,1,0:T(8,128)(2,1)S(1)}, u32[]{:S(2)}, u32[]{:S(2)}) async-start(bf16[8,64,512]{2,1,0:T(8,128)(2,1)} %bitcast.5), calls=%async_computation.3 | async-start | bytes 1048576 | tf_op jit(solution)/shard_map/all_to_all | solution.py:66
  60.1 20.6 %copy-start.2 = (f32[1,8,64,512]{3,1,2,0:T(8,128)}, f32[1,8,64,512]{3,1,2,0:T(8,128)S(1)}, u32[]{:S(2)}) copy-start(f32[1,8,64,512]{3,1,2,0:T(8,128)S(1)} %convert_bitcast_fusion.1) | copy-start | bytes 3145732
  60.4 20.3 %copy-start.3 = (f32[1,8,64,512]{3,1,2,0:T(8,128)}, f32[1,8,64,512]{3,1,2,0:T(8,128)S(1)}, u32[]{:S(2)}) copy-start(f32[1,8,64,512]{3,1,2,0:T(8,128)S(1)} %bitcast_convert_fusion) | copy-start | bytes 3145732
  74.2 6.5 copy-start.8
  117.4 277.6 %all-to-all-start.4 = ((f32[3,2,16,64,512]{4,3,0,1,2:T(8,128)}), f32[3,2,16,64,512]{4,3,0,1,2:T(8,128)}, u32[]{:S(2)}, u32[]{:S(2)}) async-start(f32[3,2,16,64,512]{4,3,0,1,2:T(8,128)} %copy.48), calls=%async_computation.4 | async-start | bytes 25165824 | tf_op jit(solution)/shard_map/all_to_all | solution.py:83
  407.0 26.4 %copy-start = (f32[3,2,2,8,64,512]{5,4,3,2,1,0:T(8,128)S(1)}, f32[3,2,2,8,64,512]{5,4,3,2,1,0:T(8,128)}, u32[]{:S(2)}) copy-start(f32[3,2,2,8,64,512]{5,4,3,2,1,0:T(8,128)} %copy.50) | copy-start | bytes 37748740
  525.7 18.9 %copy-start.9 = (f32[1,2,512,512]{2,3,1,0:T(8,128)S(1)}, f32[1,2,512,512]{2,3,1,0:T(8,128)}, u32[]{:S(2)}) copy-start(f32[1,2,512,512]{2,3,1,0:T(8,128)} %get-tuple-element.21) | copy-start | bytes 6291460
  525.7 18.9 %copy-start.10 = (f32[1,2,512,512]{2,3,1,0:T(8,128)S(1)}, f32[1,2,512,512]{2,3,1,0:T(8,128)}, u32[]{:S(2)}) copy-start(f32[1,2,512,512]{2,3,1,0:T(8,128)} %get-tuple-element.22) | copy-start | bytes 6291460
  525.7 18.9 %copy-start.11 = (f32[1,2,512,512]{2,3,1,0:T(8,128)S(1)}, f32[1,2,512,512]{2,3,1,0:T(8,128)}, u32[]{:S(2)}) copy-start(f32[1,2,512,512]{2,3,1,0:T(8,128)} %get-tuple-element.24) | copy-start | bytes 6291460
  544.6 16.2 %copy-start.4 = (f32[1,2,512,512]{2,3,1,0:T(8,128)S(1)}, f32[1,2,512,512]{2,3,1,0:T(8,128)}, u32[]{:S(2)}) copy-start(f32[1,2,512,512]{2,3,1,0:T(8,128)} %get-tuple-element.19) | copy-start | bytes 6291460
  544.6 16.2 %copy-start.5 = (f32[1,2,512,512]{2,3,1,0:T(8,128)S(1)}, f32[1,2,512,512]{2,3,1,0:T(8,128)}, u32[]{:S(2)}) copy-start(f32[1,2,512,512]{2,3,1,0:T(8,128)} %get-tuple-element.20) | copy-start | bytes 6291460
  544.6 16.2 %copy-start.6 = (f32[1,2,512,512]{2,3,1,0:T(8,128)S(1)}, f32[1,2,512,512]{2,3,1,0:T(8,128)}, u32[]{:S(2)}) copy-start(f32[1,2,512,512]{2,3,1,0:T(8,128)} %get-tuple-element.23) | copy-start | bytes 6291460
  632.2 5.5 copy-start.12
  632.2 5.5 copy-start.13
  632.2 277.0 %all-to-all-start.5 = ((f32[3,2,2,512,512]{4,2,0,1,3:T(2,128)}), f32[3,2,2,512,512]{4,2,0,1,3:T(2,128)}, u32[]{:S(2)}, u32[]{:S(2)}) async-start(f32[3,2,2,512,512]{4,2,0,1,3:T(2,128)} %copy.53), calls=%async_computation.5 | async-start | bytes 25165824 | tf_op jit(solution)/shard_map/all_to_all | solution.py:110
  909.2 66.3 %all-to-all-start = ((bf16[8,64,512]{2,1,0:T(8,128)(2,1)}), bf16[8,64,512]{2,1,0:T(8,128)(2,1)}, u32[]{:S(2)}, u32[]{:S(2)}) async-start(bf16[8,64,512]{2,1,0:T(8,128)(2,1)} %bitcast), calls=%async_computation | async-start | bytes 1048576 | tf_op jit(solution)/shard_map/all_to_all | solution.py:69
  964.8 6.4 copy-start.1
  971.3 4.2 copy-start.14
  983.5 31.7 %all-to-all-start.6 = ((bf16[8,128,512]{2,1,0:T(8,128)(2,1)}), bf16[8,128,512]{2,1,0:T(8,128)(2,1)}, u32[]{:S(2)}, u32[]{:S(2)}) async-start(bf16[8,128,512]{2,1,0:T(8,128)(2,1)} %bitcast.141), calls=%async_computation.6 | async-start | bytes 2097152 | tf_op jit(solution)/shard_map/all_to_all | solution.py:130
Sparse Core Ops, SparseCore 0:
  9.6 37.1 all-gather.1
where the time goes:
time: 1030 us; the launch traced here: 1020 us
  waiting for transfers between devices  593 us (58%)
  matrix products  222 us (22%)
  local copies, waits for them, and re-layouts  110 us (11%)
  other arithmetic  31.9 us (3%)
  starting transfers between devices  31.2 us (3%)
  blocking collectives  21.8 us (2%)
  between operations  14.5 us (1%)
    all_to_all x1, waiting for transfers between devices, shards(): lax.all_to_all(turned, 'bins', split_axis=2, concat_axis=3, tiled=True)  272 us
    all_to_all x1, waiting for transfers between devices, shards(): lax.all_to_all(turned, 'bins', split_axis=3, concat_axis=2, tiled=True)  271 us
    dot_general x12, matrix products, contract(): return jnp.einsum(form, table, values, precision=exact_mode)  215 us
    all_to_all x3, local copies, waits for them, and re-layouts, shards(): lax.all_to_all(turned, 'bins', split_axis=3, concat_axis=2, tiled=True)  51 us
    all_to_all x1, waiting for transfers between devices, shards(): lax.all_to_all(outbox.reshape(blocks, send_rows, channels), 'bins', split...  22 us
    all_to_all x1, blocking collectives, shards(): lax.all_to_all(tokens_in.reshape(grid_shape), 'bins', split_axis=0, conca...  21.8 us
  transfers between devices with their start and end apart: 7, of which 5 were waited for; matrix products, arithmetic and copies ran while one was open for 6% of the time, Pallas kernels for 0%

commit v1 on v0

v1 whole, which is shorter than its diff:
```python
import functools
import math

import jax
import jax.numpy as jnp
import numpy as np
from jax import lax
from jax.experimental import pallas as pl
from jax.experimental.pallas import tpu as pltpu
from jax.sharding import PartitionSpec as P

LANES = 128
F32 = jnp.float32
BF16 = jnp.bfloat16
MIB = 1 << 20


class Plan:
    def __init__(self, blocks, tok, chans):
        self.B = blocks
        self.T = tok
        self.C = chans
        self.cb = chans // blocks
        self.G = LANES // self.cb
        self.R = tok // self.G
        self.tiles = chans // LANES
        self.cols = tok // blocks
        self.send = 2 * self.cols
        self.Q = blocks // self.G
        self.N = 2 * blocks * tok
        self.K = blocks + 1


def wave(num, den):
    ang = 2.0 * np.pi * (np.asarray(num) % den) / den
    return np.cos(ang), -np.sin(ang)


def tables(s):
    rows = np.arange(s.R)
    lane_e = np.arange(LANES) // s.cb
    dft_c, dft_s = wave(rows[:, None] * rows[None, :], s.R)
    stacked = np.concatenate([dft_c, -dft_s], axis=0)
    k1 = np.arange(s.K)
    tw = wave(rows[None, :, None] * (k1[:, None, None] + 2 * s.B * lane_e[None, None, :]), s.N)
    tw = np.stack(tw, axis=1)
    pre = np.stack(wave(k1[:, None] * lane_e[None, :], 2 * s.B * s.G), axis=1)
    return (
        jnp.asarray(stacked, BF16),
        jnp.asarray(tw, F32),
        jnp.asarray(pre, F32),
    )


def lane_group(s, rows):
    return lax.broadcasted_iota(jnp.int32, (rows, LANES), 1) // s.cb


def turn(v, shift):
    shift = shift % LANES
    return v if shift == 0 else pltpu.roll(v, shift, 1)


def lane_transpose(s, parts, group):
    out = []
    for a in range(s.G):
        acc = None
        for g in range(s.G):
            moved = turn(parts[g], (g - a) * s.cb)
            acc = moved if acc is None else jnp.where(group == g, moved, acc)
        out.append(acc)
    return out


def lane_dft(s, re, im, group, sign):
    if s.G == 1:
        return re, im
    if s.G == 2:
        flip = jnp.where(group == 0, 1.0, -1.0).astype(F32)
        return turn(re, s.cb) + flip * re, turn(im, s.cb) + flip * im
    out_re = out_im = None
    for d in range(s.G):
        mre, mim = turn(re, d * s.cb), turn(im, d * s.cb)
        source = (group - d + s.G) % s.G
        angle_index = (group * source) % s.G
        cos_t = jnp.zeros_like(re)
        sin_t = jnp.zeros_like(re)
        for a in range(s.G):
            c, w = wave(a, s.G)
            cos_t = jnp.where(angle_index == a, float(c), cos_t)
            sin_t = jnp.where(angle_index == a, float(w) * sign, sin_t)
        add_re = mre * cos_t - mim * sin_t
        add_im = mre * sin_t + mim * cos_t
        out_re = add_re if out_re is None else out_re + add_re
        out_im = add_im if out_im is None else out_im + add_im
    return out_re, out_im


def weighted(values, weights):
    acc = None
    for v, w in zip(values, weights):
        w = float(w)
        if abs(w) < 1e-12:
            continue
        term = v if abs(w - 1) < 1e-12 else (-v if abs(w + 1) < 1e-12 else v * w)
        acc = term if acc is None else acc + term
    return acc


def add(a, b):
    return b if a is None else (a if b is None else a + b)


def sub(a, b):
    return a if b is None else (-b if a is None else a - b)


def block_dft(s, xs):
    even, odd = range(0, s.B, 2), range(1, s.B, 2)
    out = [None] * s.K
    for k in range(s.B // 2 + 1):
        ce, se = wave(np.array(even) * k, 2 * s.B)
        co, so = wave(np.array(odd) * k, 2 * s.B)
        xe, xo = [xs[i] for i in even], [xs[i] for i in odd]
        ere, eim = weighted(xe, ce), weighted(xe, se)
        ore, oim = weighted(xo, co), weighted(xo, so)
        out[k] = (add(ere, ore), add(eim, oim))
        if k != s.B - k:
            out[s.B - k] = (sub(ere, ore), sub(oim, eim))
    return out


def block_back(s, ts):
    half = s.B // 2
    sums = {}
    for k in range(half + 1):
        tre, tim = ts[k]
        if k == half:
            sums[k] = (tre, tre, tim, tim)
        else:
            ure, uim = ts[s.B - k]
            sums[k] = (tre + ure, tre - ure, tim - uim, tim + uim)
    out = []
    for i in range(s.B):
        acc = None
        for k in range(half + 1):
            c, w = wave(i * k, 2 * s.B)
            gain = 1.0 if k == 0 else 2.0
            re = sums[k][i % 2]
            im = sums[k][2 + i % 2]
            acc = add(acc, weighted([re, im], [gain * float(c), gain * float(w)]))
        out.append(acc)
    return out


CHUNK = 16


def forward_rows(s, load, held, tw, pre):
    def body(c, _):
        rows = pl.ds(pl.multiple_of(c * CHUNK, CHUNK), CHUNK)
        group = lane_group(s, CHUNK)
        spec = block_dft(s, [load(i, rows) for i in range(s.B)])
        for k in range(s.K):
            re, im = spec[k]
            pr, pi = pre[k, 0:1, :], pre[k, 1:2, :]
            if k == 0:
                im = jnp.zeros_like(re)
            elif im is None:
                re, im = re * pr, re * pi
            else:
                re, im = re * pr - im * pi, re * pi + im * pr
            re, im = lane_dft(s, re, im, group, 1.0)
            tr, ti = tw[k, 0, rows, :], tw[k, 1, rows, :]
            held[k, rows, 0:LANES] = (re * tr - im * ti).astype(BF16)
            held[k, rows, LANES : 2 * LANES] = (re * ti + im * tr).astype(BF16)
        return 0

    lax.fori_loop(0, s.R // CHUNK, body, 0)


def forward_bins(s, held_k, dft):
    o = jnp.dot(dft[...], held_k, preferred_element_type=F32)
    re = o[: s.R, :LANES] + o[s.R :, LANES:]
    im = o[: s.R, LANES:] - o[s.R :, :LANES]
    return re, im


def inverse_bins(s, re, im, k, dft, tw, pre, back):
    z = jnp.concatenate([re.astype(BF16), im.astype(BF16)], axis=1)
    o = jnp.dot(dft[...], z, preferred_element_type=F32)
    re = o[: s.R, :LANES] - o[s.R :, LANES:]
    im = o[: s.R, LANES:] + o[s.R :, :LANES]
    tr, ti = tw[k, 0], tw[k, 1]
    re, im = re * tr + im * ti, im * tr - re * ti
    re, im = lane_dft(s, re, im, lane_group(s, s.R), -1.0)
    pr, pi = pre[k, 0:1, :], pre[k, 1:2, :]
    back[k, 0] = re * pr + im * pi
    back[k, 1] = im * pr - re * pi


def inverse_rows(s, back, rows):
    return block_back(s, [(back[k, 0, rows, :], back[k, 1, rows, :]) for k in range(s.K)])


def each_chunk(s, body):
    def step(c, _):
        body(pl.ds(pl.multiple_of(c * CHUNK, CHUNK), CHUNK))
        return 0

    lax.fori_loop(0, s.R // CHUNK, step, 0)


def params(limit=40):
    return pltpu.CompilerParams(vmem_limit_bytes=limit * MIB)


def vmem():
    return pl.BlockSpec(memory_space=pltpu.VMEM)


def cost(flops, nbytes):
    return pl.CostEstimate(flops=int(flops), bytes_accessed=int(nbytes), transcendentals=0)


def pack_kernel(s, n, *refs):
    group = lane_group(s, s.R)
    for a in range(n):
        src, dst = refs[a], refs[n + a]
        for m in range(s.tiles):
            parts = [
                src[p * s.R : (p + 1) * s.R, m * LANES : (m + 1) * LANES].astype(F32)
                for p in range(s.G)
            ]
            for q, v in enumerate(lane_transpose(s, parts, group)):
                dst[s.G * m + q] = v.astype(BF16)


def pack(s, *arrays):
    n = len(arrays)
    return pl.pallas_call(
        functools.partial(pack_kernel, s, n),
        out_shape=[jax.ShapeDtypeStruct((s.B, s.R, LANES), BF16)] * n,
        in_specs=[vmem()] * n,
        out_specs=[vmem()] * n,
        compiler_params=params(32),
        cost_estimate=cost(n * s.T * s.C * 4, n * s.T * s.C * 4),
        name="pack_channels",
    )(*arrays)


def project_kernel(s, n, index, *refs):
    pieces, weight, out, acc = refs[:n], refs[n], refs[n + 1], refs[n + 2]
    k = pl.program_id(0)

    @pl.when(k == 0)
    def _():
        acc[...] = jnp.zeros_like(acc)

    for a in range(n):

        @pl.when(k == a)
        def _():
            acc[...] += lax.dot_general(
                pieces[a][...],
                weight[...],
                (((1,), (1,)), ((), ())),
                preferred_element_type=F32,
            )

    @pl.when(k == n - 1)
    def _():
        group = lane_group(s, s.R)
        for m in range(s.tiles):
            parts = [
                acc[p * s.R : (p + 1) * s.R, m * LANES : (m + 1) * LANES] for p in range(s.G)
            ]
            for q, v in enumerate(lane_transpose(s, parts, group)):
                out[s.G * m + q] = v.astype(BF16)


def project(s, pieces, order, weight):
    n = len(pieces)
    feats = pieces[0].shape[1]
    return pl.pallas_call(
        functools.partial(project_kernel, s, n),
        out_shape=jax.ShapeDtypeStruct((s.B, s.R, LANES), BF16),
        grid_spec=pltpu.PrefetchScalarGridSpec(
            num_scalar_prefetch=1,
            grid=(n,),
            in_specs=[pl.BlockSpec((s.T, feats), lambda k, o: (0, 0))] * n
            + [pl.BlockSpec((s.C, feats), lambda k, o: (0, o[k]))],
            out_specs=pl.BlockSpec((s.B, s.R, LANES), lambda k, o: (0, 0, 0)),
            scratch_shapes=[pltpu.VMEM((s.T, s.C), F32)],
        ),
        compiler_params=params(32),
        cost_estimate=cost(2 * s.T * s.C * feats * n, 2 * n * feats * (s.T + s.C)),
        name="project_cotangent",
    )(order, *pieces, weight)


def conv_kernel(s, x, h, skip, dft, tw, pre, x_spec, h_spec, u, held, back):
    forward_rows(s, lambda i, rows: x[i, rows, :].astype(F32), held, tw, pre)

    def x_bins(k, _):
        re, im = forward_bins(s, held[k], dft)
        x_spec[k, 0] = re
        x_spec[k, 1] = im
        return 0

    lax.fori_loop(0, s.K, x_bins, 0)
    forward_rows(s, lambda i, rows: h[i, rows, :].astype(F32), held, tw, pre)

    def h_bins(k, _):
        hre, him = forward_bins(s, held[k], dft)
        h_spec[k, 0] = hre
        h_spec[k, 1] = him
        xre, xim = x_spec[k, 0], x_spec[k, 1]
        inverse_bins(s, xre * hre - xim * him, xre * him + xim * hre, k, dft, tw, pre, back)
        return 0

    lax.fori_loop(0, s.K, h_bins, 0)

    def last(rows):
        conv = inverse_rows(s, back, rows)
        for i in range(s.B):
            u[i, rows, :] = conv[i] * (1.0 / s.N) + skip[...] * x[i, rows, :].astype(F32)

    each_chunk(s, last)


def gate_kernel(s, g, u, out):
    group = lane_group(s, s.cols)
    for q in range(s.Q):
        rows = slice(q * s.cols, (q + 1) * s.cols)
        for i2 in range(s.Q):
            parts = [
                g[s.G * i2 + a, rows, :].astype(F32) * u[s.G * i2 + a, rows, :]
                for a in range(s.G)
            ]
            for p, v in enumerate(lane_transpose(s, parts, group)):
                out[p * s.Q + q, i2] = v.astype(BF16)


def token_kernel(s, g, gate, h_spec, skip, hot, dft, tw, pre, y_spec, out, dy, held, back, tok):
    step = pl.program_id(0)

    @pl.when(step == 0)
    def _():
        def gated(i, rows):
            v = (g[i, rows, :].astype(F32) * gate[i, rows, :].astype(F32)).astype(BF16)
            dy[i, rows, :] = v
            return v.astype(F32)

        forward_rows(s, gated, held, tw, pre)

        def bins(k, _):
            yre, yim = forward_bins(s, held[k], dft)
            y_spec[k, 0] = yre
            y_spec[k, 1] = yim
            hre, him = h_spec[k, 0], h_spec[k, 1]
            inverse_bins(s, hre * yre + him * yim, hre * yim - him * yre, k, dft, tw, pre, back)
            return 0

        lax.fori_loop(0, s.K, bins, 0)

        def last(rows):
            back_rows = inverse_rows(s, back, rows)
            for i in range(s.B):
                v = back_rows[i] * (1.0 / s.N) + skip[...] * dy[i, rows, :].astype(F32)
                tok[i, rows, :] = v.astype(BF16)

        each_chunk(s, last)

    rows = pl.ds(pl.multiple_of(step * s.cols, s.cols), s.cols)
    v = jnp.concatenate([tok[i, rows, :] for i in range(s.B)], axis=0)
    group = lane_group(s, s.B * s.cols)
    zero = jnp.zeros_like(v)
    v = jnp.concatenate([jnp.where(group == p, v, zero) for p in range(s.G)], axis=0)
    o = jnp.dot(hot[0], v, preferred_element_type=F32)
    for b in range(s.B):
        out[b] = o[b * s.send : (b + 1) * s.send].astype(BF16)


def filter_kernel(s, x_spec, y_spec, dft, tw, pre, out, back):
    def bins(k, _):
        xre, xim = x_spec[k, 0], x_spec[k, 1]
        yre, yim = y_spec[k, 0], y_spec[k, 1]
        inverse_bins(s, yre * xre + yim * xim, yim * xre - yre * xim, k, dft, tw, pre, back)
        return 0

    lax.fori_loop(0, s.K, bins, 0)
    scale = 1.0 / (s.N * math.sqrt(s.B * s.T))
    group = lane_group(s, CHUNK)
    per = s.cols // CHUNK

    def body(c, _):
        rows = pl.ds(pl.multiple_of(c * CHUNK, CHUNK), CHUNK)
        lag = inverse_rows(s, back, rows)
        q = c // per
        inner = pl.ds(pl.multiple_of((c % per) * CHUNK, CHUNK), CHUNK)
        for i2 in range(s.Q):
            parts = [lag[s.G * i2 + a] * scale for a in range(s.G)]
            for p, v in enumerate(lane_transpose(s, parts, group)):
                out[p * s.Q + q, i2, inner, :] = v.astype(BF16)
        return 0

    lax.fori_loop(0, s.R // CHUNK, body, 0)


def hot_kernel(s, code, out):
    rows = s.B * s.send
    wide = s.B * s.cols
    target = lax.broadcasted_iota(jnp.int32, (rows, wide), 0)
    for p in range(s.G):
        match = target == code[0, :, p * wide : (p + 1) * wide]
        out[0, :, p * wide : (p + 1) * wide] = jnp.where(match, 1.0, 0.0).astype(BF16)


def columns_kernel(s, src, out):
    group = lane_group(s, s.cols)
    for i2 in range(s.Q):
        for m in range(s.tiles):
            parts = [src[s.G * m + g, i2].astype(F32) for g in range(s.G)]
            for a, v in enumerate(lane_transpose(s, parts, group)):
                out[s.G * i2 + a, :, m * LANES : (m + 1) * LANES] = v.astype(out.dtype)


def columns(s, src, dtype):
    return pl.pallas_call(
        functools.partial(columns_kernel, s),
        out_shape=jax.ShapeDtypeStruct((s.B, s.cols, s.C), dtype),
        in_specs=[vmem()],
        out_specs=vmem(),
        compiler_params=params(16),
        cost_estimate=cost(s.T * s.C * 4, s.T * s.C * 6),
        name="unpack_columns",
    )(src)


def rows_kernel(s, src, out):
    group = lane_group(s, s.send)
    for m in range(s.tiles):
        for q in range(s.Q):
            rows = slice(q * s.send, (q + 1) * s.send)
            parts = [src[s.G * m + g, rows, :].astype(F32) for g in range(s.G)]
            for p, v in enumerate(lane_transpose(s, parts, group)):
                at = (p * s.Q + q) * s.send
                out[at : at + s.send, m * LANES : (m + 1) * LANES] = v.astype(BF16)


def owner_rows(s, src):
    return pl.pallas_call(
        functools.partial(rows_kernel, s),
        out_shape=jax.ShapeDtypeStruct((s.B * s.send, s.C), BF16),
        in_specs=[vmem()],
        out_specs=vmem(),
        compiler_params=params(16),
        cost_estimate=cost(s.T * s.C * 4, s.T * s.C * 8),
        name="unpack_rows",
    )(src)


def exchange(v):
    return lax.all_to_all(v, "bins", split_axis=0, concat_axis=0, tiled=True)


def shards(tokens_in, filters, gate, skip, out_grad, out_weight, owner, slot):
    s = Plan(lax.axis_size("bins"), *tokens_in.shape)
    me = lax.axis_index("bins")
    chan = lax.axis_index("chan")
    nchan = lax.axis_size("chan")
    dft, tw, pre = tables(s)
    spec_shape = jax.ShapeDtypeStruct((s.K, 2, s.R, LANES), F32)
    spec_bytes = s.K * 2 * s.R * LANES * 4
    transform = 2 * 2 * s.R * s.R * 2 * LANES * s.K
    held = pltpu.VMEM((s.K, s.R, 2 * LANES), BF16)
    back = pltpu.VMEM((s.K, 2, s.R, LANES), F32)

    packed_x, packed_h = pack(s, tokens_in, filters)
    came = exchange(jnp.stack([packed_x, packed_h], axis=1))
    x, h = came[:, 0], came[:, 1]
    (packed_gate,) = pack(s, gate)
    came_gate = exchange(packed_gate)

    half = nchan // 2
    core_pairs = [(c, c ^ 1) for c in range(nchan)]
    far_pairs = [(c, (c + half) % nchan) for c in range(nchan)]
    far = lax.ppermute(out_grad, "chan", far_pairs)
    near = lax.ppermute(out_grad, "chan", core_pairs)
    far_near = lax.ppermute(far, "chan", core_pairs)
    order = jnp.stack([chan, chan ^ 1, (chan + half) % nchan, ((chan ^ 1) + half) % nchan])
    packed_g = project(s, [out_grad, near, far, far_near], order.astype(jnp.int32), out_weight)
    g = exchange(packed_g)

    code = owner * s.send + slot - me * s.send
    codes = lax.all_gather(code.reshape(1, s.B * s.cols), "bins", axis=0, tiled=True)
    codes = codes.reshape(s.G, s.Q, s.B * s.cols).transpose(1, 0, 2)
    codes = codes.reshape(s.Q, 1, s.G * s.B * s.cols)
    hot_shape = (s.Q, s.B * s.send, s.G * s.B * s.cols)
    hot = pl.pallas_call(
        functools.partial(hot_kernel, s),
        out_shape=jax.ShapeDtypeStruct(hot_shape, BF16),
        grid=(s.Q,),
        in_specs=[pl.BlockSpec((1, 1, hot_shape[2]), lambda q: (q, 0, 0))],
        out_specs=pl.BlockSpec((1,) + hot_shape[1:], lambda q: (q, 0, 0)),
        compiler_params=params(32),
        cost_estimate=cost(math.prod(hot_shape), 2 * math.prod(hot_shape)),
        name="row_choice",
    )(codes)

    my_skip = lax.dynamic_slice_in_dim(skip, me * s.cb, s.cb)
    my_skip = jnp.tile(my_skip, s.G).reshape(1, LANES)

    x_spec, h_spec, u = pl.pallas_call(
        functools.partial(conv_kernel, s),
        out_shape=[spec_shape, spec_shape, jax.ShapeDtypeStruct((s.B, s.R, LANES), F32)],
        in_specs=[vmem()] * 6,
        out_specs=[vmem()] * 3,
        scratch_shapes=[held, back],
        compiler_params=params(40),
        cost_estimate=cost(3 * transform, 4 * spec_bytes),
        name="conv_products",
    )(x, h, my_skip, dft, tw, pre)

    gate_out = pl.pallas_call(
        functools.partial(gate_kernel, s),
        out_shape=jax.ShapeDtypeStruct((s.B, s.Q, s.cols, LANES), BF16),
        in_specs=[vmem()] * 2,
        out_specs=vmem(),
        compiler_params=params(16),
        cost_estimate=cost(s.T * s.C * 4, s.T * s.C * 8),
        name="gate_products",
    )(g, u)
    gate_cols = exchange(gate_out)

    const2 = lambda q: (0, 0)
    const3 = lambda q: (0, 0, 0)
    const4 = lambda q: (0, 0, 0, 0)
    whole = pl.BlockSpec((s.B, s.R, LANES), const3)
    spec_block = pl.BlockSpec((s.K, 2, s.R, LANES), const4)
    y_spec, outbox = pl.pallas_call(
        functools.partial(token_kernel, s),
        out_shape=[spec_shape, jax.ShapeDtypeStruct((s.B, s.Q * s.send, LANES), BF16)],
        grid=(s.Q,),
        in_specs=[
            whole,
            whole,
            spec_block,
            pl.BlockSpec((1, LANES), const2),
            pl.BlockSpec((1,) + hot_shape[1:], lambda q: (q, 0, 0)),
            pl.BlockSpec((2 * s.R, s.R), const2),
            spec_block,
            pl.BlockSpec((s.K, 2, LANES), const3),
        ],
        out_specs=[spec_block, pl.BlockSpec((s.B, s.send, LANES), lambda q: (0, q, 0))],
        scratch_shapes=[
            pltpu.VMEM((s.B, s.R, LANES), BF16),
            held,
            back,
            pltpu.VMEM((s.B, s.R, LANES), BF16),
        ],
        compiler_params=params(48),
        cost_estimate=cost(2 * transform, 3 * spec_bytes + 2 * math.prod(hot_shape)),
        name="token_products",
    )(g, came_gate, h_spec, my_skip, hot, dft, tw, pre)
    inbox = exchange(outbox)

    lag_out = pl.pallas_call(
        functools.partial(filter_kernel, s),
        out_shape=jax.ShapeDtypeStruct((s.B, s.Q, s.cols, LANES), BF16),
        in_specs=[vmem()] * 5,
        out_specs=vmem(),
        scratch_shapes=[back],
        compiler_params=params(32),
        cost_estimate=cost(transform, 3 * spec_bytes),
        name="filter_products",
    )(x_spec, y_spec, dft, tw, pre)
    lag_cols = exchange(lag_out)

    gate_grad = columns(s, gate_cols, BF16)
    grad_rows = owner_rows(s, inbox)
    filter_grad = columns(s, lag_cols, F32)
    return (gate_grad, filter_grad, grad_rows)


def solution(mesh):
    return jax.shard_map(
        shards,
        mesh=mesh,
        in_specs=(
            P("bins", "chan"),
            P("bins", "chan"),
            P("bins", "chan"),
            P("chan"),
            P("bins", "chan"),
            P("chan", None),
            P(None, "bins"),
            P(None, "bins"),
        ),
        out_specs=(P(None, "bins", "chan"), P(None, "bins", "chan"), P("bins", "chan")),
        check_vma=False,
    )
```

time: 1030 us -> 185 us (0.18)
  waiting for transfers between devices: 593 us -> 48 us
  matrix products: 222 us -> 0 us
  local copies, waits for them, and re-layouts: 110 us -> 17.5 us
  Pallas kernels: 0 us -> 45.5 us
  other arithmetic: 31.9 us -> 0.22 us
  blocking collectives: 21.8 us -> 45.3 us
  between operations: 14.5 us -> 0.84 us
    all_to_all x6 -> x5, waiting for transfers between devices: 579 us -> 31.5 us  [exchange(): return lax.all_to_all(v, 'bins', split_axis=0, concat_axis=0, tiled=True)]
    dot_general x13 -> x0, matrix products: 222 us -> none  [the longest x12 215 us: contract(): return jnp.einsum(form, table, values, precision=exact_mode)]
    all_to_all x4 -> x0, local copies, waits for them, and re-layouts: 63 us -> none  [the longest x3 51 us: shards(): lax.all_to_all(turned, 'bins', split_axis=3, concat_axis=2, tiled=True)]
    pallas_call x0 -> x11, Pallas kernels: none -> 45.5 us  [the longest x1 15.6 us: shards(): pl.pallas_call(functools.partial(token_kernel, s), out_shape=[spec_shape,...]
    another operation x3, local copies, waits for them, and re-layouts: 35.8 us -> 1.13 us  [the longest x1 1.04 us: shards(): came = exchange(jnp.stack([packed_x, packed_h], axis=1))]
    all_gather x0 -> x1, blocking collectives: none -> 32.5 us  [shards(): lax.all_gather(code.reshape(1, s.B * s.cols), 'bins', axis=0, tiled=True)]
    another operation x6 -> x2, other arithmetic: 19.3 us -> 0.18 us  [the longest x1 0.1 us: shards(): came = exchange(jnp.stack([packed_x, packed_h], axis=1))]
    ppermute x0 -> x3, waiting for transfers between devices: none -> 16.5 us  [the longest x1 13.8 us: shards(): far = lax.ppermute(out_grad, 'chan', far_pairs)]
  transfers between devices with their start and end apart: 7 -> 8, of which waited for: 5 -> 5; matrix products, arithmetic and copies ran while one was open for 6% -> 2% of each run, Pallas kernels for 0% -> 24%
where the time goes in v1:
time: 185 us
  waiting for transfers between devices  48 us (26%)
  Pallas kernels  45.5 us (25%)
  blocking collectives  45.3 us (24%)
  starting transfers between devices  27.2 us (15%)
  local copies, waits for them, and re-layouts  17.5 us (9%)
    all_gather x1, blocking collectives, shards(): lax.all_gather(code.reshape(1, s.B * s.cols), 'bins', axis=0, tiled=True)  32.5 us
    all_to_all x5, waiting for transfers between devices, exchange(): return lax.all_to_all(v, 'bins', split_axis=0, concat_axis=0, tiled=True)  31.5 us
    all_to_all x5, starting transfers between devices, exchange(): return lax.all_to_all(v, 'bins', split_axis=0, concat_axis=0, tiled=True)  24.1 us
    pallas_call x1, Pallas kernels, shards(): pl.pallas_call(functools.partial(token_kernel, s), out_shape=[spec_shape,...  15.6 us
    unnamed x37, local copies, waits for them, and re-layouts  14.3 us
    ppermute x1, waiting for transfers between devices, shards(): far = lax.ppermute(out_grad, 'chan', far_pairs)  13.8 us
    all_to_all x1, blocking collectives, exchange(): return lax.all_to_all(v, 'bins', split_axis=0, concat_axis=0, tiled=True)  12.7 us
    pallas_call x1, Pallas kernels, shards(): pl.pallas_call(functools.partial(conv_kernel, s), out_shape=[spec_shape,...  12.5 us
  transfers between devices with their start and end apart: 8, of which 5 were waited for; matrix products, arithmetic and copies ran while one was open for 2% of the time, Pallas kernels for 24%

profile of v1, /device:TPU:0, one launch (start us, length us, event | category | flops | bytes accessed | tf_op | source)
XLA Modules:
  0.0 184.6 jit_solution(9306193532394377555)
XLA Ops:
  0.6 3.0 %collective-permute-start.1 = (bf16[512,1024]{1,0:T(8,128)(2,1)}, bf16[512,1024]{1,0:T(8,128)(2,1)S(1)}, u32[]{:S(2)}, u32[]{:S(2)}) collective-permute-start(bf16[512,1024]{1,0:T(8,128)(2,1)} %refs_0_.3), channel_id=1, source_target_pairs={{0,2},{1,3},{2,0},{3,1},{4,6},{5,7},{6,4},{7,5},{8,10},{9,11},{10,... | collective-permute-start | bytes 3145736 | tf_op jit(solution)/shard_map/ppermute | solution.py:489
  7.3 5.8 %all-to-all-start.1 = ((bf16[8,2,256,128]{3,2,1,0:T(8,128)(2,1)}), bf16[8,2,256,128]{3,2,1,0:T(8,128)(2,1)}, u32[]{:S(2)}, u32[]{:S(2)}) async-start(bf16[8,2,256,128]{3,2,1,0:T(8,128)(2,1)} %copy.16), calls=%async_computation.1 | async-start | bytes 2097152 | tf_op jit(solution)/shard_map/all_to_all | solution.py:465
  13.2 13.8 %collective-permute-done.1.refs_2_ = bf16[512,1024]{1,0:T(8,128)(2,1)S(1)} collective-permute-done((bf16[512,1024]{1,0:T(8,128)(2,1)}, bf16[512,1024]{1,0:T(8,128)(2,1)S(1)}, u32[]{:S(2)}, u32[]{:S(2)}) %collective-permute-start.1) | collective-permute-done | bytes 1048608 | tf_op jit(solution)/shard_map/ppermute | solution.py:489
  27.1 2.7 %collective-permute-done.2.refs_3_ = bf16[512,1024]{1,0:T(8,128)(2,1)} collective-permute-done((bf16[512,1024]{1,0:T(8,128)(2,1)S(1)}, bf16[512,1024]{1,0:T(8,128)(2,1)}, u32[]{:S(2)}, u32[]{:S(2)}) %collective-permute-start.2) | collective-permute-done | bytes 1048608 | tf_op jit(solution)/shard_map/ppermute | solution.py:491
  29.8 2.2 %copy-done.3 = bf16[512,4096]{1,0:T(8,128)(2,1)S(1)} copy-done((bf16[512,4096]{1,0:T(8,128)(2,1)S(1)}, bf16[512,4096]{1,0:T(8,128)(2,1)}, u32[]{:S(2)}) %copy-start.3) | copy-done | bytes 4194328
  32.0 5.9 %project_cotangent.1 = bf16[8,256,128]{2,1,0:T(8,128)(2,1)} custom-call(s32[4]{0:T(128)S(1)} %pad_add_fusion.index, bf16[512,1024]{1,0:T(8,128)(2,1)S(1)} %copy-done.10, bf16[512,1024]{1,0:T(8,128)(2,1)S(1)} %collective-permute-done.refs_1_, bf16[512,1024]{1,0:T(8,128)(2,1)S(1)} %collective-permute-done.1.refs_2_, ...), custom_call_target="tpu_custom_call" | custom-call | flops 2147483648 | bytes 8388608 | tf_op jit(solution)/shard_map/project_cotangent/pallas_call | solution.py:285
  38.9 5.2 %all-to-all-start = ((bf16[8,256,128]{2,1,0:T(8,128)(2,1)}), bf16[8,256,128]{2,1,0:T(8,128)(2,1)S(1)}, u32[]{:S(2)}, u32[]{:S(2)}) async-start(bf16[8,256,128]{2,1,0:T(8,128)(2,1)} %project_cotangent.1), calls=%async_computation | async-start | bytes 1048576 | tf_op jit(solution)/shard_map/all_to_all | solution.py:465
  46.1 12.7 %all-to-all-done.g = bf16[8,256,128]{2,1,0:T(8,128)(2,1)S(1)} async-done(((bf16[8,256,128]{2,1,0:T(8,128)(2,1)}), bf16[8,256,128]{2,1,0:T(8,128)(2,1)S(1)}, u32[]{:S(2)}, u32[]{:S(2)}) %all-to-all-start) | async-done | bytes 524320 | tf_op jit(solution)/shard_map/all_to_all | solution.py:465
  58.8 3.6 %all-to-all-start.3 = ((bf16[8,256,128]{2,1,0:T(8,128)(2,1)}), bf16[8,256,128]{2,1,0:T(8,128)(2,1)S(1)}, u32[]{:S(2)}, u32[]{:S(2)}) async-start(bf16[8,256,128]{2,1,0:T(8,128)(2,1)} %copy-done.7), calls=%async_computation.3 | async-start | bytes 1048576 | tf_op jit(solution)/shard_map/all_to_all | solution.py:465
  63.3 1.3 slice_bitcast_fusion
  65.6 12.5 %conv_products.1 = (f32[9,2,256,128]{3,2,1,0:T(8,128)S(1)}, f32[9,2,256,128]{3,2,1,0:T(8,128)S(1)}, f32[8,256,128]{2,1,0:T(8,128)S(1)}) custom-call(bf16[8,256,128]{2,1,0:T(8,128)(2,1)S(1)} %get-tuple-element.18.x, bf16[8,256,128]{2,1,0:T(8,128)(2,1)S(1)} %get-tuple-element.17.h, f32[1,128]{1,0:T(1,128)S(1)} %reshape_tile.3.skip, ...), custom_call_target="tpu_custom_call" | custom-call | flops 1811939328 | bytes 9437184 | tf_op jit(solution)/shard_map/conv_products/pallas_call | solution.py:515
  78.1 1.4 copy-done.4
  79.5 1.5 copy-done.6
  82.0 5.9 %all-to-all-start.2 = ((bf16[8,4,64,128]{3,2,1,0:T(8,128)(2,1)}), bf16[8,4,64,128]{3,2,1,0:T(8,128)(2,1)S(1)}, u32[]{:S(2)}, u32[]{:S(2)}) async-start(bf16[8,4,64,128]{3,2,1,0:T(8,128)(2,1)} %gate_products.1), calls=%async_computation.2 | async-start | bytes 1048576 | tf_op jit(solution)/shard_map/all_to_all | solution.py:465
  88.0 32.5 %all-gather = s32[8,1,512]{2,1,0:T(1,128)S(1)} all-gather(s32[1,1,512]{2,1,0:T(1,128)S(1)} %reshape.19), channel_id=1, replica_groups=mesh['bins'=8,'chan'=4] {'bins'}, dimensions={0}, use_global_device_ids=true | all-gather | bytes 18432 | tf_op jit(solution)/shard_map/all_gather | solution.py:497
  120.7 1.7 row_choice.1.hot
  122.4 3.3 %copy-done = bf16[4,1024,1024]{2,1,0:T(8,128)(2,1)} copy-done((bf16[4,1024,1024]{2,1,0:T(8,128)(2,1)}, bf16[4,1024,1024]{2,1,0:T(8,128)(2,1)S(1)}, u32[]{:S(2)}) %copy-start) | copy-done | bytes 8388632
  125.7 15.6 %token_products.1 = (f32[9,2,256,128]{3,2,1,0:T(8,128)S(1)}, bf16[8,512,128]{2,1,0:T(8,128)(2,1)S(1)}) custom-call(bf16[8,256,128]{2,1,0:T(8,128)(2,1)S(1)} %all-to-all-done.g, bf16[8,256,128]{2,1,0:T(8,128)(2,1)S(1)} %all-to-all-done.3.gate, f32[9,2,256,128]{3,2,1,0:T(8,128)} %copy-done.6, f32[1,128]{1,0:T(1,128)S(1)} %reshape_tile.3.skip, ...), custom_call_target="tpu_custom_call" | custom-call | flops 1207959552 | bytes 15466496 | tf_op jit(solution)/shard_map/token_products/pallas_call | solution.py:542
  142.2 4.5 %filter_products.1 = bf16[8,4,64,128]{3,2,1,0:T(8,128)(2,1)S(1)} custom-call(f32[9,2,256,128]{3,2,1,0:T(8,128)S(1)} %copy-done.5, f32[9,2,256,128]{3,2,1,0:T(8,128)S(1)} %get-tuple-element.15.y_spec, bf16[512,256]{1,0:T(8,128)(2,1)S(1)} %copy-done.9, f32[9,2,256,128]{3,2,1,0:T(8,128)S(1)} %copy-done.2, f32[9,2,128]{2,1,0:T(2,128)S(1)} %copy-done.15), custom_call_target="tpu_custom_call" | custom-call | flops 603979776 | bytes 7077888 | tf_op jit(solution)/shard_map/filter_products/pallas_call | solution.py:569
  146.8 12.7 %all_to_all.30.src = bf16[8,4,64,128]{3,2,1,0:T(8,128)(2,1)S(1)} all-to-all(bf16[8,4,64,128]{3,2,1,0:T(8,128)(2,1)S(1)} %filter_products.1), channel_id=1, replica_groups=mesh['bins'=8,'chan'=4] {'bins'}, dimensions={0} | all-to-all | bytes 1048576 | tf_op jit(solution)/shard_map/all_to_all | solution.py:465
  159.5 3.6 %all-to-all-start.5 = ((bf16[8,512,128]{2,1,0:T(8,128)(2,1)}), bf16[8,512,128]{2,1,0:T(8,128)(2,1)S(1)}, u32[]{:S(2)}, u32[]{:S(2)}) async-start(bf16[8,512,128]{2,1,0:T(8,128)(2,1)} %copy-done.11), calls=%async_computation.5 | async-start | bytes 2097152 | tf_op jit(solution)/shard_map/all_to_all | solution.py:465
  164.1 1.2 unpack_columns.3
  165.3 17.9 %all-to-all-done.5.src = bf16[8,512,128]{2,1,0:T(8,128)(2,1)S(1)} async-done(((bf16[8,512,128]{2,1,0:T(8,128)(2,1)}), bf16[8,512,128]{2,1,0:T(8,128)(2,1)S(1)}, u32[]{:S(2)}, u32[]{:S(2)}) %all-to-all-start.5) | async-done | bytes 1048608 | tf_op jit(solution)/shard_map/all_to_all | solution.py:465
  183.2 1.4 unpack_rows.1
  (54 shorter events, 11.8 us)
Async XLA Ops:
  0.6 26.4 %collective-permute-start.1 = (bf16[512,1024]{1,0:T(8,128)(2,1)}, bf16[512,1024]{1,0:T(8,128)(2,1)S(1)}, u32[]{:S(2)}, u32[]{:S(2)}) collective-permute-start(bf16[512,1024]{1,0:T(8,128)(2,1)} %refs_0_.3), channel_id=1, source_target_pairs={{0,2},{1,3},{2,0},{3,1},{4,6},{5,7},{6,4},{7,5},{8,10},{9,11},{10,... | collective-permute-start | bytes 3145736 | tf_op jit(solution)/shard_map/ppermute | solution.py:489
  3.6 1.0 copy-start.12
  4.7 1.0 copy-start.13
  6.2 6.9 %copy-start.10 = (bf16[512,1024]{1,0:T(8,128)(2,1)S(1)}, bf16[512,1024]{1,0:T(8,128)(2,1)}, u32[]{:S(2)}) copy-start(bf16[512,1024]{1,0:T(8,128)(2,1)} %refs_0_.3) | copy-start | bytes 3145732
  7.3 31.6 %all-to-all-start.1 = ((bf16[8,2,256,128]{3,2,1,0:T(8,128)(2,1)}), bf16[8,2,256,128]{3,2,1,0:T(8,128)(2,1)}, u32[]{:S(2)}, u32[]{:S(2)}) async-start(bf16[8,2,256,128]{3,2,1,0:T(8,128)(2,1)} %copy.16), calls=%async_computation.1 | async-start | bytes 2097152 | tf_op jit(solution)/shard_map/all_to_all | solution.py:465
  13.1 14.0 %collective-permute-start = (bf16[512,1024]{1,0:T(8,128)(2,1)S(1)}, bf16[512,1024]{1,0:T(8,128)(2,1)S(1)}, u32[]{:S(2)}, u32[]{:S(2)}) collective-permute-start(bf16[512,1024]{1,0:T(8,128)(2,1)S(1)} %copy-done.10), channel_id=1, source_target_pairs={{0,1},{1,0},{2,3},{3,2},{4,5},{5,4},{6,7},{7,6},{8,9},{9,8},{10,11... | collective-permute-start | bytes 3145736 | tf_op jit(solution)/shard_map/ppermute | solution.py:490
  27.0 2.8 %collective-permute-start.2 = (bf16[512,1024]{1,0:T(8,128)(2,1)S(1)}, bf16[512,1024]{1,0:T(8,128)(2,1)}, u32[]{:S(2)}, u32[]{:S(2)}) collective-permute-start(bf16[512,1024]{1,0:T(8,128)(2,1)S(1)} %collective-permute-done.1.refs_2_), channel_id=1, source_target_pairs={{0,1},{1,0},{2,3},{3,2},{4,5},{5,4},{6,7},{7,6},{8,9},{9,8},{10,11... | collective-permute-start | bytes 3145736 | tf_op jit(solution)/shard_map/ppermute | solution.py:491
  29.8 2.2 %copy-start.3 = (bf16[512,4096]{1,0:T(8,128)(2,1)S(1)}, bf16[512,4096]{1,0:T(8,128)(2,1)}, u32[]{:S(2)}) copy-start(bf16[512,4096]{1,0:T(8,128)(2,1)} %refs_4_.1) | copy-start | bytes 12582916
  38.9 20.0 %all-to-all-start = ((bf16[8,256,128]{2,1,0:T(8,128)(2,1)}), bf16[8,256,128]{2,1,0:T(8,128)(2,1)S(1)}, u32[]{:S(2)}, u32[]{:S(2)}) async-start(bf16[8,256,128]{2,1,0:T(8,128)(2,1)} %project_cotangent.1), calls=%async_computation | async-start | bytes 1048576 | tf_op jit(solution)/shard_map/all_to_all | solution.py:465
  44.0 1.0 copy-start.14
  45.1 19.5 %copy-start.1 = (f32[9,2,256,128]{3,2,1,0:T(8,128)S(1)}, f32[9,2,256,128]{3,2,1,0:T(8,128)}, u32[]{:S(2)}) copy-start(f32[9,2,256,128]{3,2,1,0:T(8,128)} %constant.45.clone.tw) | copy-start | bytes 7077892
  45.1 19.5 %copy-start.15 = (f32[9,2,128]{2,1,0:T(2,128)S(1)}, f32[9,2,128]{2,1,0:T(2,128)}, u32[]{:S(2)}) copy-start(f32[9,2,128]{2,1,0:T(2,128)} %constant.46.clone.pre) | copy-start | bytes 27652
  58.8 23.2 %all-to-all-start.3 = ((bf16[8,256,128]{2,1,0:T(8,128)(2,1)}), bf16[8,256,128]{2,1,0:T(8,128)(2,1)S(1)}, u32[]{:S(2)}, u32[]{:S(2)}) async-start(bf16[8,256,128]{2,1,0:T(8,128)(2,1)} %copy-done.7), calls=%async_computation.3 | async-start | bytes 1048576 | tf_op jit(solution)/shard_map/all_to_all | solution.py:465
  78.1 1.4 copy-start.4
  79.5 1.5 copy-start.6
  81.0 6.9 %copy-start.16 = (s32[8,64]{1,0:T(8,128)S(1)}, s32[8,64]{1,0:T(8,128)}, u32[]{:S(2)}) copy-start(s32[8,64]{1,0:T(8,128)} %param.18) | copy-start | bytes 6148
  81.0 6.9 %copy-start.17 = (s32[8,64]{1,0:T(8,128)S(1)}, s32[8,64]{1,0:T(8,128)}, u32[]{:S(2)}) copy-start(s32[8,64]{1,0:T(8,128)} %param.17) | copy-start | bytes 6148
  82.0 64.7 %all-to-all-start.2 = ((bf16[8,4,64,128]{3,2,1,0:T(8,128)(2,1)}), bf16[8,4,64,128]{3,2,1,0:T(8,128)(2,1)S(1)}, u32[]{:S(2)}, u32[]{:S(2)}) async-start(bf16[8,4,64,128]{3,2,1,0:T(8,128)(2,1)} %gate_products.1), calls=%async_computation.2 | async-start | bytes 1048576 | tf_op jit(solution)/shard_map/all_to_all | solution.py:465
  120.7 5.0 %copy-start.9 = (bf16[512,256]{1,0:T(8,128)(2,1)S(1)}, bf16[512,256]{1,0:T(8,128)(2,1)}, u32[]{:S(2)}) copy-start(bf16[512,256]{1,0:T(8,128)(2,1)} %constant.44.clone.dft) | copy-start | bytes 786436
  122.4 3.3 %copy-start = (bf16[4,1024,1024]{2,1,0:T(8,128)(2,1)}, bf16[4,1024,1024]{2,1,0:T(8,128)(2,1)S(1)}, u32[]{:S(2)}) copy-start(bf16[4,1024,1024]{2,1,0:T(8,128)(2,1)S(1)} %row_choice.1.hot) | copy-start | bytes 25165828
  125.6 16.6 %copy-start.2 = (f32[9,2,256,128]{3,2,1,0:T(8,128)S(1)}, f32[9,2,256,128]{3,2,1,0:T(8,128)}, u32[]{:S(2)}) copy-start(f32[9,2,256,128]{3,2,1,0:T(8,128)} %constant.45.clone.tw) | copy-start | bytes 7077892
  125.6 16.6 %copy-start.5 = (f32[9,2,256,128]{3,2,1,0:T(8,128)S(1)}, f32[9,2,256,128]{3,2,1,0:T(8,128)}, u32[]{:S(2)}) copy-start(f32[9,2,256,128]{3,2,1,0:T(8,128)} %copy-done.4) | copy-start | bytes 7077892
  141.2 1.0 copy-start.11
  159.5 23.7 %all-to-all-start.5 = ((bf16[8,512,128]{2,1,0:T(8,128)(2,1)}), bf16[8,512,128]{2,1,0:T(8,128)(2,1)S(1)}, u32[]{:S(2)}, u32[]{:S(2)}) async-start(bf16[8,512,128]{2,1,0:T(8,128)(2,1)} %copy-done.11), calls=%async_computation.5 | async-start | bytes 2097152 | tf_op jit(solution)/shard_map/all_to_all | solution.py:465
  (2 other events, 1.7 us)

commit v2 on v1

v2 whole, which is shorter than its diff:
```python
import functools
import math

import jax
import jax.numpy as jnp
import numpy as np
from jax import lax
from jax.experimental import pallas as pl
from jax.experimental.pallas import tpu as pltpu
from jax.sharding import PartitionSpec as P

LANES = 128
F32 = jnp.float32
BF16 = jnp.bfloat16
MIB = 1 << 20


class Plan:
    def __init__(self, blocks, tok, chans):
        self.B = blocks
        self.T = tok
        self.C = chans
        self.cb = chans // blocks
        self.G = LANES // self.cb
        self.R = tok // self.G
        self.tiles = chans // LANES
        self.cols = tok // blocks
        self.send = 2 * self.cols
        self.Q = blocks // self.G
        self.N = 2 * blocks * tok
        self.K = blocks + 1


def wave(num, den):
    ang = 2.0 * np.pi * (np.asarray(num) % den) / den
    return np.cos(ang), -np.sin(ang)


def tables(s):
    rows = np.arange(s.R)
    lane_e = np.arange(LANES) // s.cb
    dft_c, dft_s = wave(rows[:, None] * rows[None, :], s.R)
    stacked = np.concatenate([dft_c, -dft_s], axis=0)
    k1 = np.arange(s.K)
    tw = wave(rows[None, :, None] * (k1[:, None, None] + 2 * s.B * lane_e[None, None, :]), s.N)
    tw = np.stack(tw, axis=1)
    pre = np.stack(wave(k1[:, None] * lane_e[None, :], 2 * s.B * s.G), axis=1)
    return (
        jnp.asarray(stacked, BF16),
        jnp.asarray(tw, F32),
        jnp.asarray(pre, F32),
    )


def lane_group(s, rows):
    return lax.broadcasted_iota(jnp.int32, (rows, LANES), 1) // s.cb


def turn(v, shift):
    shift = shift % LANES
    return v if shift == 0 else pltpu.roll(v, shift, 1)


def lane_transpose(s, parts, group):
    out = []
    for a in range(s.G):
        acc = None
        for g in range(s.G):
            moved = turn(parts[g], (g - a) * s.cb)
            acc = moved if acc is None else jnp.where(group == g, moved, acc)
        out.append(acc)
    return out


def lane_dft(s, re, im, group, sign):
    if s.G == 1:
        return re, im
    if s.G == 2:
        flip = jnp.where(group == 0, 1.0, -1.0).astype(F32)
        return turn(re, s.cb) + flip * re, turn(im, s.cb) + flip * im
    out_re = out_im = None
    for d in range(s.G):
        mre, mim = turn(re, d * s.cb), turn(im, d * s.cb)
        source = (group - d + s.G) % s.G
        angle_index = (group * source) % s.G
        cos_t = jnp.zeros_like(re)
        sin_t = jnp.zeros_like(re)
        for a in range(s.G):
            c, w = wave(a, s.G)
            cos_t = jnp.where(angle_index == a, float(c), cos_t)
            sin_t = jnp.where(angle_index == a, float(w) * sign, sin_t)
        add_re = mre * cos_t - mim * sin_t
        add_im = mre * sin_t + mim * cos_t
        out_re = add_re if out_re is None else out_re + add_re
        out_im = add_im if out_im is None else out_im + add_im
    return out_re, out_im


def weighted(values, weights):
    acc = None
    for v, w in zip(values, weights):
        w = float(w)
        if abs(w) < 1e-12:
            continue
        term = v if abs(w - 1) < 1e-12 else (-v if abs(w + 1) < 1e-12 else v * w)
        acc = term if acc is None else acc + term
    return acc


def add(a, b):
    return b if a is None else (a if b is None else a + b)


def sub(a, b):
    return a if b is None else (-b if a is None else a - b)


def block_dft(s, xs):
    even, odd = range(0, s.B, 2), range(1, s.B, 2)
    out = [None] * s.K
    for k in range(s.B // 2 + 1):
        ce, se = wave(np.array(even) * k, 2 * s.B)
        co, so = wave(np.array(odd) * k, 2 * s.B)
        xe, xo = [xs[i] for i in even], [xs[i] for i in odd]
        ere, eim = weighted(xe, ce), weighted(xe, se)
        ore, oim = weighted(xo, co), weighted(xo, so)
        out[k] = (add(ere, ore), add(eim, oim))
        if k != s.B - k:
            out[s.B - k] = (sub(ere, ore), sub(oim, eim))
    return out


def block_back(s, ts):
    half = s.B // 2
    sums = {}
    for k in range(half + 1):
        tre, tim = ts[k]
        if k == half:
            sums[k] = (tre, tre, tim, tim)
        else:
            ure, uim = ts[s.B - k]
            sums[k] = (tre + ure, tre - ure, tim - uim, tim + uim)
    out = []
    for i in range(s.B):
        acc = None
        for k in range(half + 1):
            c, w = wave(i * k, 2 * s.B)
            gain = 1.0 if k == 0 else 2.0
            re = sums[k][i % 2]
            im = sums[k][2 + i % 2]
            acc = add(acc, weighted([re, im], [gain * float(c), gain * float(w)]))
        out.append(acc)
    return out


CHUNK = 32
TAIL = 16
TW_PIECES = 2


def forward_rows(s, load, held, tw, pre, ready=()):
    def body(c, _):
        rows = pl.ds(pl.multiple_of(c * CHUNK, CHUNK), CHUNK)
        group = lane_group(s, CHUNK)
        spec = block_dft(s, [load(i, rows) for i in range(s.B)])
        for k in range(s.K):
            re, im = spec[k]
            pr, pi = pre[k, 0:1, :], pre[k, 1:2, :]
            if k == 0:
                im = jnp.zeros_like(re)
            elif im is None:
                re, im = re * pr, re * pi
            else:
                re, im = re * pr - im * pi, re * pi + im * pr
            re, im = lane_dft(s, re, im, group, 1.0)
            tr, ti = tw[k, 0, rows, :], tw[k, 1, rows, :]
            held[k, rows, 0:LANES] = (re * tr - im * ti).astype(BF16)
            held[k, rows, LANES : 2 * LANES] = (re * ti + im * tr).astype(BF16)
        return 0

    pieces = max(len(ready), 1)
    per = s.R // CHUNK // pieces
    for n in range(pieces):
        if ready:
            ready[n].wait()
        lax.fori_loop(n * per, (n + 1) * per, body, 0, unroll=min(2, per))


def forward_bins(s, held_k, dft):
    o = jnp.dot(dft[...], held_k, preferred_element_type=F32)
    re = o[: s.R, :LANES] + o[s.R :, LANES:]
    im = o[: s.R, LANES:] - o[s.R :, :LANES]
    return re, im


def inverse_bins(s, re, im, k, dft, tw, pre, back):
    z = jnp.concatenate([re.astype(BF16), im.astype(BF16)], axis=1)
    o = jnp.dot(dft[...], z, preferred_element_type=F32)
    re = o[: s.R, :LANES] - o[s.R :, LANES:]
    im = o[: s.R, LANES:] + o[s.R :, :LANES]
    tr, ti = tw[k, 0], tw[k, 1]
    re, im = re * tr + im * ti, im * tr - re * ti
    re, im = lane_dft(s, re, im, lane_group(s, s.R), -1.0)
    pr, pi = pre[k, 0:1, :], pre[k, 1:2, :]
    back[k, 0] = re * pr + im * pi
    back[k, 1] = im * pr - re * pi


def inverse_rows(s, back, rows):
    return block_back(s, [(back[k, 0, rows, :], back[k, 1, rows, :]) for k in range(s.K)])


def each_bin(s, body):
    for k in range(s.K):
        body(k)


def each_chunk(s, body):
    def step(c, _):
        body(pl.ds(pl.multiple_of(c * CHUNK, CHUNK), CHUNK), c)
        return 0

    lax.fori_loop(0, s.R // CHUNK, step, 0, unroll=2)


def params():
    return pltpu.CompilerParams(vmem_limit_bytes=60 * MIB)


def hbm():
    return pl.BlockSpec(memory_space=pl.ANY)


def vmem():
    return pl.BlockSpec(memory_space=pltpu.VMEM)


def cost(flops, nbytes):
    return pl.CostEstimate(flops=int(flops), bytes_accessed=int(nbytes), transcendentals=0)


def pack_kernel(s, n, *refs):
    arrays, owner, slot, out = refs[:n], refs[n], refs[n + 1], refs[n + 2]
    held, held_owner, held_slot, tail, sems = refs[n + 3 :]
    me = lax.axis_index("bins")
    group = lane_group(s, s.R)
    copies = [pltpu.make_async_copy(arrays[a], held.at[a], sems.at[a]) for a in range(n)]
    copies.append(pltpu.make_async_copy(owner, held_owner, sems.at[n]))
    copies.append(pltpu.make_async_copy(slot, held_slot, sems.at[n + 1]))
    for c in copies:
        c.start()
    for a in range(n):
        copies[a].wait()
        for m in range(s.tiles):
            parts = [
                held[a, p * s.R : (p + 1) * s.R, m * LANES : (m + 1) * LANES].astype(F32)
                for p in range(s.G)
            ]
            for q, v in enumerate(lane_transpose(s, parts, group)):
                out[s.G * m + q, a * s.R : (a + 1) * s.R, :] = v.astype(BF16)
    copies[n].wait()
    copies[n + 1].wait()
    tail[...] = jnp.zeros_like(tail)
    tail[: s.B, : s.cols] = held_owner[...].astype(F32)
    tail[: s.B, s.cols : 2 * s.cols] = (held_slot[...] - me * s.send).astype(F32)
    for b in range(s.B):
        out[b, n * s.R :, :] = tail[...].astype(BF16)


def pack(s, owner, slot, *arrays):
    n = len(arrays)
    return pl.pallas_call(
        functools.partial(pack_kernel, s, n),
        out_shape=jax.ShapeDtypeStruct((s.B, n * s.R + TAIL, LANES), BF16),
        in_specs=[hbm()] * (n + 2),
        out_specs=vmem(),
        scratch_shapes=[
            pltpu.VMEM((n, s.T, s.C), BF16),
            pltpu.VMEM((s.B, s.cols), jnp.int32),
            pltpu.VMEM((s.B, s.cols), jnp.int32),
            pltpu.VMEM((TAIL, LANES), F32),
            pltpu.SemaphoreType.DMA((n + 2,)),
        ],
        compiler_params=params(),
        cost_estimate=cost(n * s.T * s.C * 4, n * s.T * s.C * 4),
        name="pack_channels",
    )(*arrays, owner, slot)


def swap_partners(s, parts):
    return [parts[0]] + [
        lax.ppermute(parts[x], "bins", [(b, b ^ x) for b in range(s.B)]) for x in range(1, s.B)
    ]


def project_part_kernel(s, n, index, *refs):
    pieces, weight, start, out = refs[:n], refs[n], refs[n + 1 : -1], refs[-1]
    k = pl.program_id(0)
    for a in range(n):

        @pl.when(k == a)
        def _():
            v = lax.dot_general(
                pieces[a][...],
                weight[...],
                (((1,), (1,)), ((), ())),
                preferred_element_type=F32,
            )
            if a > 0:
                v = out[...] + v
            elif start:
                v = start[0][...] + v
            out[...] = v


def project_part(s, pieces, order, weight, start=()):
    n = len(pieces)
    feats = pieces[0].shape[1]
    return pl.pallas_call(
        functools.partial(project_part_kernel, s, n),
        out_shape=jax.ShapeDtypeStruct((s.T, s.C), F32),
        grid_spec=pltpu.PrefetchScalarGridSpec(
            num_scalar_prefetch=1,
            grid=(n,),
            in_specs=[pl.BlockSpec((s.T, feats), lambda k, o: (0, 0))] * n
            + [pl.BlockSpec((s.C, feats), lambda k, o: (0, o[k]))]
            + [pl.BlockSpec((s.T, s.C), lambda k, o: (0, 0))] * len(start),
            out_specs=pl.BlockSpec((s.T, s.C), lambda k, o: (0, 0)),
        ),
        compiler_params=params(),
        cost_estimate=cost(2 * s.T * s.C * feats * n, 2 * n * feats * (s.T + s.C)),
        name="project_part",
    )(order, *pieces, weight, *start)


def project_finish_kernel(s, n, index, *refs):
    pieces, weight, start, gate = refs[:n], refs[n], refs[n + 1], refs[n + 2]
    dy_out, away, kept, acc = refs[n + 3 :]
    k = pl.program_id(0)
    me = lax.axis_index("bins")
    for a in range(n):

        @pl.when(k == a)
        def _():
            v = lax.dot_general(
                pieces[a][...],
                weight[...],
                (((1,), (1,)), ((), ())),
                preferred_element_type=F32,
            )
            acc[...] = v + (start if a == 0 else acc)[...]

    @pl.when(k == n - 1)
    def _():
        g = acc[...].astype(BF16).astype(F32)
        acc[...] = g
        half = s.T // 2
        mine = me // (s.B // 2)
        kept[...] = acc[pl.ds(pl.multiple_of(mine * half, half), half), :].astype(BF16)
        away[...] = acc[pl.ds(pl.multiple_of((1 - mine) * half, half), half), :].astype(BF16)
        group = lane_group(s, s.R)
        for m in range(s.tiles):
            parts = []
            for p in range(s.G):
                at = (slice(p * s.R, (p + 1) * s.R), slice(m * LANES, (m + 1) * LANES))
                parts.append((acc[at] * gate[at].astype(F32)).astype(BF16).astype(F32))
            for q, v in enumerate(lane_transpose(s, parts, group)):
                dy_out[s.G * m + q] = v.astype(BF16)


def project_finish(s, pieces, order, weight, start, gate):
    n = len(pieces)
    feats = pieces[0].shape[1]
    half = jax.ShapeDtypeStruct((s.T // 2, s.C), BF16)
    return pl.pallas_call(
        functools.partial(project_finish_kernel, s, n),
        out_shape=[jax.ShapeDtypeStruct((s.B, s.R, LANES), BF16), half, half],
        grid_spec=pltpu.PrefetchScalarGridSpec(
            num_scalar_prefetch=1,
            grid=(n,),
            in_specs=[pl.BlockSpec((s.T, feats), lambda k, o: (0, 0))] * n
            + [
                pl.BlockSpec((s.C, feats), lambda k, o: (0, o[k])),
                pl.BlockSpec((s.T, s.C), lambda k, o: (0, 0)),
                pl.BlockSpec((s.T, s.C), lambda k, o: (0, 0)),
            ],
            out_specs=[
                pl.BlockSpec((s.B, s.R, LANES), lambda k, o: (0, 0, 0)),
                pl.BlockSpec(half.shape, lambda k, o: (0, 0)),
                pl.BlockSpec(half.shape, lambda k, o: (0, 0)),
            ],
            scratch_shapes=[pltpu.VMEM((s.T, s.C), F32)],
        ),
        compiler_params=params(),
        cost_estimate=cost(2 * s.T * s.C * feats * n, 2 * n * feats * (s.T + s.C)),
        name="project_far",
    )(order, *pieces, weight, start, gate)


def relay_kernel(s, kept, came, *outs):
    me = lax.axis_index("bins")
    for x in range(s.B // 2):
        at = (me ^ x) % (s.B // 2) * s.cols
        rows = pl.ds(pl.multiple_of(at, s.cols), s.cols)
        outs[x][0] = kept[rows, :]
        outs[x][1] = came[rows, :]


def swap_halves(s, away):
    return lax.ppermute(away, "bins", [(b, b ^ (s.B // 2)) for b in range(s.B)])


def to_columns(s, kept, came):
    half = s.B // 2
    parts = pl.pallas_call(
        functools.partial(relay_kernel, s),
        out_shape=[jax.ShapeDtypeStruct((2, s.cols, s.C), BF16)] * half,
        in_specs=[vmem()] * 2,
        out_specs=[vmem()] * half,
        compiler_params=params(),
        cost_estimate=cost(s.T * s.C, s.T * s.C * 4),
        name="relay_rows",
    )(kept, came)
    return [parts[0]] + [
        lax.ppermute(parts[x], "bins", [(b, b ^ x) for b in range(s.B)]) for x in range(1, half)
    ]


def column_blocks(s, out, rows, c, values):
    group = lane_group(s, CHUNK)
    per = s.cols // CHUNK
    q = c // per
    inner = pl.ds(pl.multiple_of(c % per * CHUNK, CHUNK), CHUNK)
    for i2 in range(s.Q):
        parts = [values[s.G * i2 + a] for a in range(s.G)]
        for p, v in enumerate(lane_transpose(s, parts, group)):
            out[p * s.Q + q, i2, inner, :] = v.astype(BF16)


def conv_kernel(s, xh, skip, dft, tw, pre, x_spec, h_spec, u, held, back):
    x, h = xh.at[:, : s.R, :], xh.at[:, s.R : 2 * s.R, :]
    forward_rows(s, lambda i, rows: x[i, rows, :].astype(F32), held, tw, pre)

    def x_bins(k):
        re, im = forward_bins(s, held[k], dft)
        x_spec[k, 0] = re
        x_spec[k, 1] = im

    each_bin(s, x_bins)
    forward_rows(s, lambda i, rows: h[i, rows, :].astype(F32), held, tw, pre)

    def h_bins(k):
        hre, him = forward_bins(s, held[k], dft)
        h_spec[k, 0] = hre
        h_spec[k, 1] = him
        xre, xim = x_spec[k, 0], x_spec[k, 1]
        inverse_bins(s, xre * hre - xim * him, xre * him + xim * hre, k, dft, tw, pre, back)

    each_bin(s, h_bins)

    def last(rows, c):
        conv = inverse_rows(s, back, rows)
        values = [
            conv[i] * (1.0 / s.N) + skip[...] * x[i, rows, :].astype(F32) for i in range(s.B)
        ]
        column_blocks(s, u, rows, c, values)

    each_chunk(s, last)


def row_choice(s, codes, q):
    per = LANES // s.cols
    target = lax.broadcasted_iota(jnp.int32, (s.B * s.send, LANES), 0).astype(F32)
    lane = lax.broadcasted_iota(jnp.int32, (1, LANES), 1) // s.cols
    hits = []
    for p in range(s.G):
        v = codes[p * s.Q + q].astype(F32)
        v = v * float(s.send) + turn(v, -s.cols)
        for t in range(s.B // per):
            row = v[t * per : t * per + 1, :]
            for a in range(1, per):
                other = turn(v[t * per + a : t * per + a + 1, :], a * s.cols)
                row = jnp.where(lane == a, other, row)
            hits.append(jnp.where(target == row, 1.0, 0.0).astype(BF16))
    return jnp.concatenate(hits, axis=1)


def token_kernel(s, *refs):
    dy_at, came, h_at, skip_at, dft_at, tw_at, pre_at, y_at, out_at = refs[:9]
    dy, codes, h_spec, skip, dft, tw, pre, y_spec, out, held, back, tok, sems, y_sems = refs[9:]
    pieces = TW_PIECES
    part = s.R // pieces
    pairs = [(pre_at, pre), (skip_at, skip), (dy_at, dy)]
    for n in range(pieces):
        rows = slice(n * part, (n + 1) * part)
        pairs.append((tw_at.at[:, :, rows, :], tw.at[:, :, rows, :]))
    pairs += [(dft_at, dft), (h_at, h_spec), (came.at[:, 2 * s.R :, :], codes)]
    copies = [pltpu.make_async_copy(a, b, sems.at[n]) for n, (a, b) in enumerate(pairs)]
    for c in copies:
        c.start()
    for c in copies[:3]:
        c.wait()
    forward_rows(s, lambda i, rows: dy[i, rows, :].astype(F32), held, tw, pre, copies[3:-3])
    copies[-3].wait()
    copies[-2].wait()
    stores = []

    def bins(k):
        yre, yim = forward_bins(s, held[k], dft)
        y_spec[k, 0] = yre
        y_spec[k, 1] = yim
        stores.append(pltpu.make_async_copy(y_spec.at[k], y_at.at[k], y_sems.at[k]))
        stores[-1].start()
        hre, him = h_spec[k, 0], h_spec[k, 1]
        inverse_bins(s, hre * yre + him * yim, hre * yim - him * yre, k, dft, tw, pre, back)

    each_bin(s, bins)

    def last(rows, c):
        back_rows = inverse_rows(s, back, rows)
        for i in range(s.B):
            v = back_rows[i] * (1.0 / s.N) + skip[...] * dy[i, rows, :].astype(F32)
            tok[i, rows, :] = v.astype(BF16)

    each_chunk(s, last)

    copies[-1].wait()
    group = lane_group(s, s.B * s.cols)
    for q in range(s.Q):
        rows = slice(q * s.cols, (q + 1) * s.cols)
        v = jnp.concatenate([tok[i, rows, :] for i in range(s.B)], axis=0)
        zero = jnp.zeros_like(v)
        v = jnp.concatenate([jnp.where(group == p, v, zero) for p in range(s.G)], axis=0)
        o = jnp.dot(row_choice(s, codes, q), v, preferred_element_type=F32)
        at = slice(q * s.send, (q + 1) * s.send)
        for b in range(s.B):
            out[b, at, :] = o[b * s.send : (b + 1) * s.send].astype(BF16)
        sem = y_sems.at[s.K + q]
        stores.append(pltpu.make_async_copy(out.at[:, at, :], out_at.at[:, at, :], sem))
        stores[-1].start()
    for c in stores:
        c.wait()


def filter_kernel(s, x_spec, y_spec, u, dft, tw, pre, *refs):
    outs, (back, lags) = refs[: s.B], refs[s.B :]

    def bins(k):
        xre, xim = x_spec[k, 0], x_spec[k, 1]
        yre, yim = y_spec[k, 0], y_spec[k, 1]
        inverse_bins(s, yre * xre + yim * xim, yim * xre - yre * xim, k, dft, tw, pre, back)

    each_bin(s, bins)
    scale = 1.0 / (s.N * math.sqrt(s.B * s.T))

    def last(rows, c):
        column_blocks(s, lags, rows, c, [v * scale for v in inverse_rows(s, back, rows)])

    each_chunk(s, last)
    me = lax.axis_index("bins")
    for x in range(s.B):
        outs[x][0] = u[me ^ x]
        outs[x][1] = lags[me ^ x]


def columns_kernel(s, *refs):
    parts, refs = refs[: s.B], refs[s.B :]
    rows, (gate_grad, filter_grad, src, g) = refs[: s.B // 2], refs[s.B // 2 :]
    me = lax.axis_index("bins")
    for x in range(s.B):
        src[me ^ x] = parts[x][...]
    for x in range(s.B // 2):
        g[me ^ x] = rows[x][0]
        g[me ^ x ^ (s.B // 2)] = rows[x][1]
    group = lane_group(s, s.cols)
    for i2 in range(s.Q):
        for m in range(s.tiles):
            lanes = slice(m * LANES, (m + 1) * LANES)
            for kind in range(2):
                vs = [src[s.G * m + a, kind, i2].astype(F32) for a in range(s.G)]
                for a, v in enumerate(lane_transpose(s, vs, group)):
                    i = s.G * i2 + a
                    if kind == 0:
                        gate_grad[i, :, lanes] = (v * g[i, :, lanes].astype(F32)).astype(BF16)
                    else:
                        filter_grad[i, :, lanes] = v


def columns(s, parts, rows):
    shape = (s.B, s.cols, s.C)
    return pl.pallas_call(
        functools.partial(columns_kernel, s),
        out_shape=[jax.ShapeDtypeStruct(shape, BF16), jax.ShapeDtypeStruct(shape, F32)],
        in_specs=[vmem()] * (s.B + s.B // 2),
        out_specs=[vmem()] * 2,
        scratch_shapes=[
            pltpu.VMEM((s.B, 2, s.Q, s.cols, LANES), BF16),
            pltpu.VMEM(shape, BF16),
        ],
        compiler_params=params(),
        cost_estimate=cost(s.T * s.C * 8, s.T * s.C * 12),
        name="unpack_columns",
    )(*parts, *rows)


def rows_kernel(s, src, out):
    group = lane_group(s, s.send)
    for m in range(s.tiles):
        for q in range(s.Q):
            rows = slice(q * s.send, (q + 1) * s.send)
            parts = [src[s.G * m + g, rows, :].astype(F32) for g in range(s.G)]
            for p, v in enumerate(lane_transpose(s, parts, group)):
                at = (p * s.Q + q) * s.send
                out[at : at + s.send, m * LANES : (m + 1) * LANES] = v.astype(BF16)


def owner_rows(s, src):
    return pl.pallas_call(
        functools.partial(rows_kernel, s),
        out_shape=jax.ShapeDtypeStruct((s.B * s.send, s.C), BF16),
        in_specs=[vmem()],
        out_specs=vmem(),
        compiler_params=params(),
        cost_estimate=cost(s.T * s.C * 4, s.T * s.C * 8),
        name="unpack_rows",
    )(src)


def exchange(v):
    return lax.all_to_all(v, "bins", split_axis=0, concat_axis=0, tiled=True)


def shards(tokens_in, filters, gate, skip, out_grad, out_weight, owner, slot):
    s = Plan(lax.axis_size("bins"), *tokens_in.shape)
    me = lax.axis_index("bins")
    chan = lax.axis_index("chan")
    nchan = lax.axis_size("chan")
    dft, tw, pre = tables(s)
    spec_shape = jax.ShapeDtypeStruct((s.K, 2, s.R, LANES), F32)
    spec_bytes = s.K * 2 * s.R * LANES * 4
    transform = 2 * 2 * s.R * s.R * 2 * LANES * s.K
    held = pltpu.VMEM((s.K, s.R, 2 * LANES), BF16)
    back = pltpu.VMEM((s.K, 2, s.R, LANES), F32)

    came = exchange(pack(s, owner, slot, tokens_in, filters))

    half = nchan // 2
    core_pairs = [(c, c ^ 1) for c in range(nchan)]
    far_pairs = [(c, (c + half) % nchan) for c in range(nchan)]
    far = lax.ppermute(out_grad, "chan", far_pairs)
    near = lax.ppermute(out_grad, "chan", core_pairs)
    order = jnp.stack([chan, chan ^ 1]).astype(jnp.int32)
    start = project_part(s, [out_grad, near], order, out_weight)
    far, start = lax.optimization_barrier((far, start))
    far_near = lax.ppermute(far, "chan", core_pairs)
    far_order = (order + half) % nchan
    start = project_part(s, [far], far_order[:1], out_weight, (start,))
    packed_dy, away, kept = project_finish(s, [far_near], far_order[1:], out_weight, start, gate)
    dy = exchange(packed_dy)
    g_came = swap_halves(s, away)

    my_skip = lax.dynamic_slice_in_dim(skip, me * s.cb, s.cb)
    my_skip = jnp.tile(my_skip, s.G).reshape(1, LANES)

    cols_shape = (s.Q, s.cols, LANES)
    by_dest = (s.B,) + cols_shape
    x_spec, h_spec, u = pl.pallas_call(
        functools.partial(conv_kernel, s),
        out_shape=[spec_shape, spec_shape, jax.ShapeDtypeStruct(by_dest, BF16)],
        in_specs=[vmem()] * 5,
        out_specs=[vmem()] * 3,
        scratch_shapes=[held, back],
        compiler_params=params(),
        cost_estimate=cost(3 * transform, 4 * spec_bytes),
        name="conv_products",
    )(came, my_skip, dft, tw, pre)

    outbox_shape = (s.B, s.Q * s.send, LANES)
    y_spec, outbox = pl.pallas_call(
        functools.partial(token_kernel, s),
        out_shape=[spec_shape, jax.ShapeDtypeStruct(outbox_shape, BF16)],
        in_specs=[hbm()] * 7,
        out_specs=[hbm()] * 2,
        scratch_shapes=[
            pltpu.VMEM((s.B, s.R, LANES), BF16),
            pltpu.VMEM((s.B, TAIL, LANES), BF16),
            back,
            pltpu.VMEM((1, LANES), F32),
            pltpu.VMEM((2 * s.R, s.R), BF16),
            back,
            pltpu.VMEM((s.K, 2, LANES), F32),
            back,
            pltpu.VMEM(outbox_shape, BF16),
            held,
            back,
            pltpu.VMEM((s.B, s.R, LANES), BF16),
            pltpu.SemaphoreType.DMA((6 + TW_PIECES,)),
            pltpu.SemaphoreType.DMA((s.K + s.Q,)),
        ],
        compiler_params=params(),
        cost_estimate=cost(2 * transform, 3 * spec_bytes),
        name="token_products",
    )(dy, came, h_spec, my_skip, dft, tw, pre)
    outbox, g_came = lax.optimization_barrier((outbox, g_came))
    inbox = exchange(outbox)

    parts = pl.pallas_call(
        functools.partial(filter_kernel, s),
        out_shape=[jax.ShapeDtypeStruct((2,) + cols_shape, BF16)] * s.B,
        in_specs=[vmem()] * 6,
        out_specs=[vmem()] * s.B,
        scratch_shapes=[back, pltpu.VMEM(by_dest, BF16)],
        compiler_params=params(),
        cost_estimate=cost(transform, 3 * spec_bytes),
        name="filter_products",
    )(x_spec, y_spec, u, dft, tw, pre)
    parts = swap_partners(s, parts)
    g_rows = to_columns(s, kept, g_came)

    grad_rows = owner_rows(s, inbox)
    parts, grad_rows = lax.optimization_barrier((parts, grad_rows))
    gate_grad, filter_grad = columns(s, parts, g_rows)
    return (gate_grad, filter_grad, grad_rows)


def solution(mesh):
    return jax.shard_map(
        shards,
        mesh=mesh,
        in_specs=(
            P("bins", "chan"),
            P("bins", "chan"),
            P("bins", "chan"),
            P("chan"),
            P("bins", "chan"),
            P("chan", None),
            P(None, "bins"),
            P(None, "bins"),
        ),
        out_specs=(P(None, "bins", "chan"), P(None, "bins", "chan"), P("bins", "chan")),
        check_vma=False,
    )
```

time: 185 us -> 133 us (0.72)
  blocking collectives: 45.3 us -> 0 us
  starting transfers between devices: 27.2 us -> 38.1 us
  waiting for transfers between devices: 48 us -> 37.2 us
  local copies, waits for them, and re-layouts: 17.5 us -> 6.74 us
  Pallas kernels: 45.5 us -> 49.2 us
    all_gather x1 -> x0, blocking collectives: 32.5 us -> none  [shards(): lax.all_gather(code.reshape(1, s.B * s.cols), 'bins', axis=0, tiled=True)]
    all_to_all x5 -> x3, waiting for transfers between devices: 31.5 us -> 7.8 us  [exchange(): return lax.all_to_all(v, 'bins', split_axis=0, concat_axis=0, tiled=True)]
    ppermute x0 -> x11, waiting for transfers between devices: none -> 20.5 us  [the longest x7 18.1 us: swap_partners(): lax.ppermute(parts[x], 'bins', [(b, b ^ x) for b in range(s.B)])]
    ppermute x0 -> x11, starting transfers between devices: none -> 19.9 us  [the longest x7 16.5 us: swap_partners(): lax.ppermute(parts[x], 'bins', [(b, b ^ x) for b in range(s.B)])]
    all_to_all x1 -> x0, blocking collectives: 12.7 us -> none  [exchange(): return lax.all_to_all(v, 'bins', split_axis=0, concat_axis=0, tiled=True)]
    pallas_call x8 -> x7, Pallas kernels: 16 us -> 27.9 us  [the longest x2 9.26 us: project_part(): pl.pallas_call(functools.partial(project_part_kernel, s, n), out_shape=ja...]
    unnamed x37 -> x34, local copies, waits for them, and re-layouts: 14.3 us -> 4.69 us
    all_to_all x5 -> x3, starting transfers between devices: 24.1 us -> 15.1 us  [exchange(): return lax.all_to_all(v, 'bins', split_axis=0, concat_axis=0, tiled=True)]
  transfers between devices with their start and end apart: 8 -> 17, of which waited for: 5 -> 7; matrix products, arithmetic and copies ran while one was open for 2% -> 2% of each run, Pallas kernels for 24% -> 35%
where the time goes in v2:
time: 133 us
  Pallas kernels  49.2 us (37%)
  starting transfers between devices  38.1 us (29%)
  waiting for transfers between devices  37.2 us (28%)
  local copies, waits for them, and re-layouts  6.74 us (5%)
    ppermute x7, waiting for transfers between devices, swap_partners(): lax.ppermute(parts[x], 'bins', [(b, b ^ x) for b in range(s.B)])  18.1 us
    ppermute x7, starting transfers between devices, swap_partners(): lax.ppermute(parts[x], 'bins', [(b, b ^ x) for b in range(s.B)])  16.5 us
    all_to_all x3, starting transfers between devices, exchange(): return lax.all_to_all(v, 'bins', split_axis=0, concat_axis=0, tiled=True)  15.1 us
    pallas_call x1, Pallas kernels, shards(): pl.pallas_call(functools.partial(conv_kernel, s), out_shape=[spec_shape,...  10 us
    pallas_call x2, Pallas kernels, project_part(): pl.pallas_call(functools.partial(project_part_kernel, s, n), out_shape=ja...  9.26 us
    ppermute x1, waiting for transfers between devices, shards(): far = lax.ppermute(out_grad, 'chan', far_pairs)  8.92 us
    pallas_call x1, Pallas kernels, shards(): pl.pallas_call(functools.partial(token_kernel, s), out_shape=[spec_shape,...  8.68 us
    all_to_all x3, waiting for transfers between devices, exchange(): return lax.all_to_all(v, 'bins', split_axis=0, concat_axis=0, tiled=True)  7.8 us
  transfers between devices with their start and end apart: 17, of which 7 were waited for; matrix products, arithmetic and copies ran while one was open for 2% of the time, Pallas kernels for 35%

profile of v2, /device:TPU:0, one launch (start us, length us, event | category | flops | bytes accessed | tf_op | source)
XLA Modules:
  0.0 132.6 jit_solution(3142685225971713996)
XLA Ops:
  1.1 2.6 %collective-permute-start = (bf16[512,1024]{1,0:T(8,128)(2,1)}, bf16[512,1024]{1,0:T(8,128)(2,1)S(1)}, u32[]{:S(2)}, u32[]{:S(2)}) collective-permute-start(bf16[512,1024]{1,0:T(8,128)(2,1)} %refs_0_.3), channel_id=1, source_target_pairs={{0,2},{1,3},{2,0},{3,1},{4,6},{5,7},{6,4},{7,5},{8,10},{9,11},{10,... | collective-permute-start | bytes 3145736 | tf_op jit(solution)/shard_map/ppermute | solution.py:650
  3.7 2.6 %pack_channels.1 = bf16[8,528,128]{2,1,0:T(8,128)(2,1)} custom-call(bf16[512,512]{1,0:T(8,128)(2,1)} %refs_0_.2, bf16[512,512]{1,0:T(8,128)(2,1)} %refs_1_.3, s32[8,64]{1,0:T(8,128)} %refs_2_.2, s32[8,64]{1,0:T(8,128)} %refs_3_.2), custom_call_target="tpu_custom_call" | custom-call | flops 2097152 | bytes 2097152 | tf_op jit(solution)/shard_map/pack_channels/pallas_call | solution.py:272
  6.3 5.8 %all-to-all-start = ((bf16[8,528,128]{2,1,0:T(8,128)(2,1)}), bf16[8,528,128]{2,1,0:T(8,128)(2,1)S(1)}, u32[]{:S(2)}, u32[]{:S(2)}) async-start(bf16[8,528,128]{2,1,0:T(8,128)(2,1)} %pack_channels.1), calls=%async_computation | async-start | bytes 2162688 | tf_op jit(solution)/shard_map/all_to_all | solution.py:630
  13.7 5.0 %project_part.2.refs_2_ = f32[512,512]{1,0:T(8,128)} custom-call(s32[2]{0:T(128)} %get-tuple-element.74.index, bf16[512,1024]{1,0:T(8,128)(2,1)} %refs_0_.3, bf16[512,1024]{1,0:T(8,128)(2,1)} %copy-done.5, bf16[512,4096]{1,0:T(8,128)(2,1)} %refs_1_.5), custom_call_target="tpu_custom_call" | custom-call | flops 1073741824 | bytes 4194304 | tf_op jit(solution)/shard_map/project_part/pallas_call | solution.py:319
  18.8 8.9 %collective-permute-done.refs_0_ = bf16[512,1024]{1,0:T(8,128)(2,1)S(1)} collective-permute-done((bf16[512,1024]{1,0:T(8,128)(2,1)}, bf16[512,1024]{1,0:T(8,128)(2,1)S(1)}, u32[]{:S(2)}, u32[]{:S(2)}) %collective-permute-start) | collective-permute-done | bytes 1048608 | tf_op jit(solution)/shard_map/ppermute | solution.py:650
  28.7 4.2 %project_part.3.refs_2_ = f32[512,512]{1,0:T(8,128)} custom-call(s32[1]{0:T(128)} %get-tuple-element.75.index, bf16[512,1024]{1,0:T(8,128)(2,1)} %copy-done.4, bf16[512,4096]{1,0:T(8,128)(2,1)} %refs_1_.5, f32[512,512]{1,0:T(8,128)} %project_part.2.refs_2_), custom_call_target="tpu_custom_call" | custom-call | flops 536870912 | bytes 2097152 | tf_op jit(solution)/shard_map/project_part/pallas_call | solution.py:319
  33.9 4.5 %project_far.1 = (bf16[8,256,128]{2,1,0:T(8,128)(2,1)}, bf16[256,512]{1,0:T(8,128)(2,1)}, bf16[256,512]{1,0:T(8,128)(2,1)}) custom-call(s32[1]{0:T(128)} %get-tuple-element.76.index, bf16[512,1024]{1,0:T(8,128)(2,1)} %copy-done.3, bf16[512,4096]{1,0:T(8,128)(2,1)} %refs_1_.5, f32[512,512]{1,0:T(8,128)} %project_part.3.refs_2_, bf16[512,512]{1,0:T(8,128)(2,1)} %refs_3_.3), custom_call_target="tpu_custom_call" | custom-call | flops 536870912 | bytes 2097152 | tf_op jit(solution)/shard_map/project_far/pallas_call | solution.py:375
  39.0 5.5 %all-to-all-start.1 = ((bf16[8,256,128]{2,1,0:T(8,128)(2,1)}), bf16[8,256,128]{2,1,0:T(8,128)(2,1)S(1)}, u32[]{:S(2)}, u32[]{:S(2)}) async-start(bf16[8,256,128]{2,1,0:T(8,128)(2,1)} %get-tuple-element.41), calls=%async_computation.1 | async-start | bytes 1048576 | tf_op jit(solution)/shard_map/all_to_all | solution.py:630
  45.9 2.9 %collective-permute-start.10 = (bf16[256,512]{1,0:T(8,128)(2,1)}, bf16[256,512]{1,0:T(8,128)(2,1)S(1)}, u32[]{:S(2)}, u32[]{:S(2)}) collective-permute-start(bf16[256,512]{1,0:T(8,128)(2,1)} %get-tuple-element.54), channel_id=1, source_target_pairs={{0,16},{4,20},{8,24},{12,28},{16,0},{20,4},{24,8},{28,12},{1,17},{... | collective-permute-start | bytes 786440 | tf_op jit(solution)/shard_map/ppermute | solution.py:410
  48.8 10.0 %conv_products.1 = (f32[9,2,256,128]{3,2,1,0:T(8,128)}, f32[9,2,256,128]{3,2,1,0:T(8,128)}, bf16[8,4,64,128]{3,2,1,0:T(8,128)(2,1)}) custom-call(bf16[8,528,128]{2,1,0:T(8,128)(2,1)} %copy-done, f32[1,128]{1,0:T(1,128)} %reshape_tile.3.skip.refs_3_, bf16[512,256]{1,0:T(8,128)(2,1)} %constant.39.clone.dft.refs_4_, ...), custom_call_target="tpu_custom_call" | custom-call | flops 1811939328 | bytes 9437184 | tf_op jit(solution)/shard_map/conv_products/pallas_call | solution.py:667
  58.8 7.2 %all-to-all-done.1.refs_0_ = bf16[8,256,128]{2,1,0:T(8,128)(2,1)S(1)} async-done(((bf16[8,256,128]{2,1,0:T(8,128)(2,1)}), bf16[8,256,128]{2,1,0:T(8,128)(2,1)S(1)}, u32[]{:S(2)}, u32[]{:S(2)}) %all-to-all-start.1) | async-done | bytes 524320 | tf_op jit(solution)/shard_map/all_to_all | solution.py:630
  66.8 8.7 %token_products.1 = (f32[9,2,256,128]{3,2,1,0:T(8,128)}, bf16[8,512,128]{2,1,0:T(8,128)(2,1)}) custom-call(bf16[8,256,128]{2,1,0:T(8,128)(2,1)} %copy-done.2, bf16[8,528,128]{2,1,0:T(8,128)(2,1)} %copy-done, f32[9,2,256,128]{3,2,1,0:T(8,128)} %get-tuple-element.42.refs_2_, f32[1,128]{1,0:T(1,128)} %reshape_tile.3.skip.refs_3_, ...), custom_call_target="tpu_custom_call" | custom-call | flops 1207959552 | bytes 7077888 | tf_op jit(solution)/shard_map/token_products/pallas_call | solution.py:679
  75.5 3.8 %all-to-all-start.2 = ((bf16[8,512,128]{2,1,0:T(8,128)(2,1)}), bf16[8,512,128]{2,1,0:T(8,128)(2,1)S(1)}, u32[]{:S(2)}, u32[]{:S(2)}) async-start(bf16[8,512,128]{2,1,0:T(8,128)(2,1)} %get-tuple-element.55), calls=%async_computation.2 | async-start | bytes 2097152 | tf_op jit(solution)/shard_map/all_to_all | solution.py:630
  79.2 6.5 %filter_products.1 = (bf16[2,4,64,128]{3,2,1,0:T(8,128)(2,1)}, bf16[2,4,64,128]{3,2,1,0:T(8,128)(2,1)}, bf16[2,4,64,128]{3,2,1,0:T(8,128)(2,1)}, bf16[2,4,64,128...) custom-call(f32[9,2,256,128]{3,2,1,0:T(8,128)} %get-tuple-element.38, ...), custom_call_target="tpu_custom_call" | custom-call | flops 603979776 | bytes 7077888 | tf_op jit(solution)/shard_map/filter_products/pallas_call | solution.py:707
  85.8 2.0 %collective-permute-start.3 = (bf16[2,4,64,128]{3,2,1,0:T(8,128)(2,1)}, bf16[2,4,64,128]{3,2,1,0:T(8,128)(2,1)S(1)}, u32[]{:S(2)}, u32[]{:S(2)}) collective-permute-start(bf16[2,4,64,128]{3,2,1,0:T(8,128)(2,1)} %get-tuple-element.46), channel_id=1, source_target_pairs={{0,4},{4,0},{8,12},{12,8},{16,20},{20,16},{24,28},{28,24},{1,5},{5... | collective-permute-start | bytes 393224 | tf_op jit(solution)/shard_map/ppermute | solution.py:292
  89.3 2.8 %collective-permute-start.6 = (bf16[2,4,64,128]{3,2,1,0:T(8,128)(2,1)}, bf16[2,4,64,128]{3,2,1,0:T(8,128)(2,1)S(1)}, u32[]{:S(2)}, u32[]{:S(2)}) collective-permute-start(bf16[2,4,64,128]{3,2,1,0:T(8,128)(2,1)} %get-tuple-element.49), channel_id=1, source_target_pairs={{0,16},{4,20},{8,24},{12,28},{16,0},{20,4},{24,8},{28,12},{1,17},{... | collective-permute-start | bytes 393224 | tf_op jit(solution)/shard_map/ppermute | solution.py:292
  93.6 1.9 %relay_rows.1 = (bf16[2,64,512]{2,1,0:T(8,128)(2,1)}, bf16[2,64,512]{2,1,0:T(8,128)(2,1)}, bf16[2,64,512]{2,1,0:T(8,128)(2,1)}, bf16[2,64,512]{2,1,0:T(8,128)(2,1)}) custom-call(bf16[256,512]{1,0:T(8,128)(2,1)} %get-tuple-element.64.kept, bf16[256,512]{1,0:T(8,128)(2,1)} %copy-done.6), custom_call_target="tpu_custom_call" | custom-call | flops 262144 | bytes 1048576 | tf_op jit(solution)/shard_map/relay_rows/pallas_call | solution.py:415
  95.5 3.9 %collective-permute-start.8 = (bf16[2,4,64,128]{3,2,1,0:T(8,128)(2,1)}, bf16[2,4,64,128]{3,2,1,0:T(8,128)(2,1)S(1)}, u32[]{:S(2)}, u32[]{:S(2)}) collective-permute-start(bf16[2,4,64,128]{3,2,1,0:T(8,128)(2,1)} %get-tuple-element.51), channel_id=1, source_target_pairs={{0,24},{4,28},{8,16},{12,20},{16,8},{20,12},{24,0},{28,4},{1,25},{... | collective-permute-start | bytes 393224 | tf_op jit(solution)/shard_map/ppermute | solution.py:292
  100.4 4.7 %collective-permute-start.9 = (bf16[2,4,64,128]{3,2,1,0:T(8,128)(2,1)}, bf16[2,4,64,128]{3,2,1,0:T(8,128)(2,1)S(1)}, u32[]{:S(2)}, u32[]{:S(2)}) collective-permute-start(bf16[2,4,64,128]{3,2,1,0:T(8,128)(2,1)} %get-tuple-element.52), channel_id=1, source_target_pairs={{0,28},{4,24},{8,20},{12,16},{16,12},{20,8},{24,4},{28,0},{1,29},{... | collective-permute-start | bytes 393224 | tf_op jit(solution)/shard_map/ppermute | solution.py:292
  105.6 14.8 %collective-permute-done.6.refs_4_ = bf16[2,4,64,128]{3,2,1,0:T(8,128)(2,1)S(1)} collective-permute-done((bf16[2,4,64,128]{3,2,1,0:T(8,128)(2,1)}, bf16[2,4,64,128]{3,2,1,0:T(8,128)(2,1)S(1)}, u32[]{:S(2)}, u32[]{:S(2)}) %collective-permute-start.6) | collective-permute-done | bytes 131104 | tf_op jit(solution)/shard_map/ppermute | solution.py:292
  120.5 2.3 %collective-permute-done.7.refs_5_ = bf16[2,4,64,128]{3,2,1,0:T(8,128)(2,1)S(1)} collective-permute-done((bf16[2,4,64,128]{3,2,1,0:T(8,128)(2,1)}, bf16[2,4,64,128]{3,2,1,0:T(8,128)(2,1)S(1)}, u32[]{:S(2)}, u32[]{:S(2)}) %collective-permute-start.7) | collective-permute-done | bytes 131104 | tf_op jit(solution)/shard_map/ppermute | solution.py:292
  123.7 2.6 %unpack_rows.1 = bf16[1024,512]{1,0:T(8,128)(2,1)} custom-call(bf16[8,512,128]{2,1,0:T(8,128)(2,1)} %copy-done.1), custom_call_target="tpu_custom_call" | custom-call | flops 1048576 | bytes 2097152 | tf_op jit(solution)/shard_map/unpack_rows/pallas_call | solution.py:618
  126.4 2.4 %collective-permute-done.13.refs_11_ = bf16[2,64,512]{2,1,0:T(8,128)(2,1)S(1)} collective-permute-done((bf16[2,64,512]{2,1,0:T(8,128)(2,1)}, bf16[2,64,512]{2,1,0:T(8,128)(2,1)S(1)}, u32[]{:S(2)}, u32[]{:S(2)}) %collective-permute-start.13) | collective-permute-done | bytes 131104 | tf_op jit(solution)/shard_map/ppermute | solution.py:425
  129.5 3.1 %unpack_columns.1 = (bf16[8,64,512]{2,1,0:T(8,128)(2,1)}, f32[8,64,512]{2,1,0:T(8,128)}) custom-call(bf16[2,4,64,128]{3,2,1,0:T(8,128)(2,1)} %get-tuple-element.56.refs_0_, bf16[2,4,64,128]{3,2,1,0:T(8,128)(2,1)} %copy-done.7, bf16[2,4,64,128]{3,2,1,0:T(8,128)(2,1)} %copy-done.8, bf16[2,4,64,128]{3,2,1,0:T(8,128)(2,1)} %copy-done.9, ...), custom_call_target="tpu_custom_call" | custom-call | flops 2097152 | bytes 3145728 | tf_op jit(solution)/shard_map/unpack_columns/pallas_call | solution.py:591
  (59 shorter events, 13.1 us)
Async XLA Ops:
  0.6 12.1 %collective-permute-start.1 = (bf16[512,1024]{1,0:T(8,128)(2,1)}, bf16[512,1024]{1,0:T(8,128)(2,1)S(1)}, u32[]{:S(2)}, u32[]{:S(2)}) collective-permute-start(bf16[512,1024]{1,0:T(8,128)(2,1)} %refs_0_.3), channel_id=1, source_target_pairs={{0,1},{1,0},{2,3},{3,2},{4,5},{5,4},{6,7},{7,6},{8,9},{9,8},{10,11... | collective-permute-start | bytes 3145736 | tf_op jit(solution)/shard_map/ppermute | solution.py:651
  1.1 26.5 %collective-permute-start = (bf16[512,1024]{1,0:T(8,128)(2,1)}, bf16[512,1024]{1,0:T(8,128)(2,1)S(1)}, u32[]{:S(2)}, u32[]{:S(2)}) collective-permute-start(bf16[512,1024]{1,0:T(8,128)(2,1)} %refs_0_.3), channel_id=1, source_target_pairs={{0,2},{1,3},{2,0},{3,1},{4,6},{5,7},{6,4},{7,5},{8,10},{9,11},{10,... | collective-permute-start | bytes 3145736 | tf_op jit(solution)/shard_map/ppermute | solution.py:650
  6.3 32.6 %all-to-all-start = ((bf16[8,528,128]{2,1,0:T(8,128)(2,1)}), bf16[8,528,128]{2,1,0:T(8,128)(2,1)S(1)}, u32[]{:S(2)}, u32[]{:S(2)}) async-start(bf16[8,528,128]{2,1,0:T(8,128)(2,1)} %pack_channels.1), calls=%async_computation | async-start | bytes 2162688 | tf_op jit(solution)/shard_map/all_to_all | solution.py:630
  27.7 5.2 %collective-permute-start.2 = (bf16[512,1024]{1,0:T(8,128)(2,1)S(1)}, bf16[512,1024]{1,0:T(8,128)(2,1)S(1)}, u32[]{:S(2)}, u32[]{:S(2)}) collective-permute-start(bf16[512,1024]{1,0:T(8,128)(2,1)S(1)} %collective-permute-done.refs_0_), channel_id=1, source_target_pairs={{0,1},{1,0},{2,3},{3,2},{4,5},{5,4},{6,7},{7,6},{8,9},{9,8},{10,11... | collective-permute-start | bytes 3145736 | tf_op jit(solution)/shard_map/ppermute | solution.py:655
  39.0 9.8 %copy-start = (bf16[8,528,128]{2,1,0:T(8,128)(2,1)}, bf16[8,528,128]{2,1,0:T(8,128)(2,1)S(1)}, u32[]{:S(2)}) copy-start(bf16[8,528,128]{2,1,0:T(8,128)(2,1)S(1)} %all-to-all-done.xh.refs_1_) | copy-start | bytes 3244036
  39.0 27.0 %all-to-all-start.1 = ((bf16[8,256,128]{2,1,0:T(8,128)(2,1)}), bf16[8,256,128]{2,1,0:T(8,128)(2,1)S(1)}, u32[]{:S(2)}, u32[]{:S(2)}) async-start(bf16[8,256,128]{2,1,0:T(8,128)(2,1)} %get-tuple-element.41), calls=%async_computation.1 | async-start | bytes 1048576 | tf_op jit(solution)/shard_map/all_to_all | solution.py:630
  45.9 29.6 %collective-permute-start.10 = (bf16[256,512]{1,0:T(8,128)(2,1)}, bf16[256,512]{1,0:T(8,128)(2,1)S(1)}, u32[]{:S(2)}, u32[]{:S(2)}) collective-permute-start(bf16[256,512]{1,0:T(8,128)(2,1)} %get-tuple-element.54), channel_id=1, source_target_pairs={{0,16},{4,20},{8,24},{12,28},{16,0},{20,4},{24,8},{28,12},{1,17},{... | collective-permute-start | bytes 786440 | tf_op jit(solution)/shard_map/ppermute | solution.py:410
  75.5 10.3 %copy-start.6 = (bf16[256,512]{1,0:T(8,128)(2,1)}, bf16[256,512]{1,0:T(8,128)(2,1)S(1)}, u32[]{:S(2)}) copy-start(bf16[256,512]{1,0:T(8,128)(2,1)S(1)} %collective-permute-done.10.came) | copy-start | bytes 786436
  75.5 47.2 %all-to-all-start.2 = ((bf16[8,512,128]{2,1,0:T(8,128)(2,1)}), bf16[8,512,128]{2,1,0:T(8,128)(2,1)S(1)}, u32[]{:S(2)}, u32[]{:S(2)}) async-start(bf16[8,512,128]{2,1,0:T(8,128)(2,1)} %get-tuple-element.55), calls=%async_computation.2 | async-start | bytes 2097152 | tf_op jit(solution)/shard_map/all_to_all | solution.py:630
  85.8 9.7 %collective-permute-start.3 = (bf16[2,4,64,128]{3,2,1,0:T(8,128)(2,1)}, bf16[2,4,64,128]{3,2,1,0:T(8,128)(2,1)S(1)}, u32[]{:S(2)}, u32[]{:S(2)}) collective-permute-start(bf16[2,4,64,128]{3,2,1,0:T(8,128)(2,1)} %get-tuple-element.46), channel_id=1, source_target_pairs={{0,4},{4,0},{8,12},{12,8},{16,20},{20,16},{24,28},{28,24},{1,5},{5... | collective-permute-start | bytes 393224 | tf_op jit(solution)/shard_map/ppermute | solution.py:292
  87.7 12.7 %collective-permute-start.4 = (bf16[2,4,64,128]{3,2,1,0:T(8,128)(2,1)}, bf16[2,4,64,128]{3,2,1,0:T(8,128)(2,1)S(1)}, u32[]{:S(2)}, u32[]{:S(2)}) collective-permute-start(bf16[2,4,64,128]{3,2,1,0:T(8,128)(2,1)} %get-tuple-element.47), channel_id=1, source_target_pairs={{0,8},{4,12},{8,0},{12,4},{16,24},{20,28},{24,16},{28,20},{1,9},{5... | collective-permute-start | bytes 393224 | tf_op jit(solution)/shard_map/ppermute | solution.py:292
  89.2 15.9 %collective-permute-start.5 = (bf16[2,4,64,128]{3,2,1,0:T(8,128)(2,1)}, bf16[2,4,64,128]{3,2,1,0:T(8,128)(2,1)S(1)}, u32[]{:S(2)}, u32[]{:S(2)}) collective-permute-start(bf16[2,4,64,128]{3,2,1,0:T(8,128)(2,1)} %get-tuple-element.48), channel_id=1, source_target_pairs={{0,12},{4,8},{8,4},{12,0},{16,28},{20,24},{24,20},{28,16},{1,13},{... | collective-permute-start | bytes 393224 | tf_op jit(solution)/shard_map/ppermute | solution.py:292
  89.3 31.1 %collective-permute-start.6 = (bf16[2,4,64,128]{3,2,1,0:T(8,128)(2,1)}, bf16[2,4,64,128]{3,2,1,0:T(8,128)(2,1)S(1)}, u32[]{:S(2)}, u32[]{:S(2)}) collective-permute-start(bf16[2,4,64,128]{3,2,1,0:T(8,128)(2,1)} %get-tuple-element.49), channel_id=1, source_target_pairs={{0,16},{4,20},{8,24},{12,28},{16,0},{20,4},{24,8},{28,12},{1,17},{... | collective-permute-start | bytes 393224 | tf_op jit(solution)/shard_map/ppermute | solution.py:292
  92.1 30.6 %collective-permute-start.7 = (bf16[2,4,64,128]{3,2,1,0:T(8,128)(2,1)}, bf16[2,4,64,128]{3,2,1,0:T(8,128)(2,1)S(1)}, u32[]{:S(2)}, u32[]{:S(2)}) collective-permute-start(bf16[2,4,64,128]{3,2,1,0:T(8,128)(2,1)} %get-tuple-element.50), channel_id=1, source_target_pairs={{0,20},{4,16},{8,28},{12,24},{16,4},{20,0},{24,12},{28,8},{1,21},{... | collective-permute-start | bytes 393224 | tf_op jit(solution)/shard_map/ppermute | solution.py:292
  95.5 33.3 %copy-start.7 = (bf16[2,4,64,128]{3,2,1,0:T(8,128)(2,1)}, bf16[2,4,64,128]{3,2,1,0:T(8,128)(2,1)S(1)}, u32[]{:S(2)}) copy-start(bf16[2,4,64,128]{3,2,1,0:T(8,128)(2,1)S(1)} %collective-permute-done.3.refs_1_) | copy-start | bytes 393220
  95.5 30.9 %collective-permute-start.8 = (bf16[2,4,64,128]{3,2,1,0:T(8,128)(2,1)}, bf16[2,4,64,128]{3,2,1,0:T(8,128)(2,1)S(1)}, u32[]{:S(2)}, u32[]{:S(2)}) collective-permute-start(bf16[2,4,64,128]{3,2,1,0:T(8,128)(2,1)} %get-tuple-element.51), channel_id=1, source_target_pairs={{0,24},{4,28},{8,16},{12,20},{16,8},{20,12},{24,0},{28,4},{1,25},{... | collective-permute-start | bytes 393224 | tf_op jit(solution)/shard_map/ppermute | solution.py:292
  100.4 28.4 %copy-start.8 = (bf16[2,4,64,128]{3,2,1,0:T(8,128)(2,1)}, bf16[2,4,64,128]{3,2,1,0:T(8,128)(2,1)S(1)}, u32[]{:S(2)}) copy-start(bf16[2,4,64,128]{3,2,1,0:T(8,128)(2,1)S(1)} %collective-permute-done.4.refs_2_) | copy-start | bytes 393220
  100.4 25.9 %collective-permute-start.9 = (bf16[2,4,64,128]{3,2,1,0:T(8,128)(2,1)}, bf16[2,4,64,128]{3,2,1,0:T(8,128)(2,1)S(1)}, u32[]{:S(2)}, u32[]{:S(2)}) collective-permute-start(bf16[2,4,64,128]{3,2,1,0:T(8,128)(2,1)} %get-tuple-element.52), channel_id=1, source_target_pairs={{0,28},{4,24},{8,20},{12,16},{16,12},{20,8},{24,4},{28,0},{1,29},{... | collective-permute-start | bytes 393224 | tf_op jit(solution)/shard_map/ppermute | solution.py:292
  105.1 23.7 %copy-start.9 = (bf16[2,4,64,128]{3,2,1,0:T(8,128)(2,1)}, bf16[2,4,64,128]{3,2,1,0:T(8,128)(2,1)S(1)}, u32[]{:S(2)}) copy-start(bf16[2,4,64,128]{3,2,1,0:T(8,128)(2,1)S(1)} %collective-permute-done.5.refs_3_) | copy-start | bytes 393220
  105.1 21.2 %collective-permute-start.11 = (bf16[2,64,512]{2,1,0:T(8,128)(2,1)}, bf16[2,64,512]{2,1,0:T(8,128)(2,1)S(1)}, u32[]{:S(2)}, u32[]{:S(2)}) collective-permute-start(bf16[2,64,512]{2,1,0:T(8,128)(2,1)} %get-tuple-element.67), channel_id=1, source_target_pairs={{0,4},{4,0},{8,12},{12,8},{16,20},{20,16},{24,28},{28,24},{1,5},{5... | collective-permute-start | bytes 393224 | tf_op jit(solution)/shard_map/ppermute | solution.py:425
  120.5 8.4 %copy-start.10 = (bf16[2,4,64,128]{3,2,1,0:T(8,128)(2,1)}, bf16[2,4,64,128]{3,2,1,0:T(8,128)(2,1)S(1)}, u32[]{:S(2)}) copy-start(bf16[2,4,64,128]{3,2,1,0:T(8,128)(2,1)S(1)} %collective-permute-done.6.refs_4_) | copy-start | bytes 393220
  120.5 5.9 %collective-permute-start.12 = (bf16[2,64,512]{2,1,0:T(8,128)(2,1)}, bf16[2,64,512]{2,1,0:T(8,128)(2,1)S(1)}, u32[]{:S(2)}, u32[]{:S(2)}) collective-permute-start(bf16[2,64,512]{2,1,0:T(8,128)(2,1)} %get-tuple-element.68), channel_id=1, source_target_pairs={{0,8},{4,12},{8,0},{12,4},{16,24},{20,28},{24,16},{28,20},{1,9},{5... | collective-permute-start | bytes 393224 | tf_op jit(solution)/shard_map/ppermute | solution.py:425
  122.7 6.1 %copy-start.11 = (bf16[2,4,64,128]{3,2,1,0:T(8,128)(2,1)}, bf16[2,4,64,128]{3,2,1,0:T(8,128)(2,1)S(1)}, u32[]{:S(2)}) copy-start(bf16[2,4,64,128]{3,2,1,0:T(8,128)(2,1)S(1)} %collective-permute-done.7.refs_5_) | copy-start | bytes 393220
  122.7 6.1 %collective-permute-start.13 = (bf16[2,64,512]{2,1,0:T(8,128)(2,1)}, bf16[2,64,512]{2,1,0:T(8,128)(2,1)S(1)}, u32[]{:S(2)}, u32[]{:S(2)}) collective-permute-start(bf16[2,64,512]{2,1,0:T(8,128)(2,1)} %get-tuple-element.69), channel_id=1, source_target_pairs={{0,12},{4,8},{8,4},{12,0},{16,28},{20,24},{24,20},{28,16},{1,13},{... | collective-permute-start | bytes 393224 | tf_op jit(solution)/shard_map/ppermute | solution.py:425
  (10 other events, 15.3 us)

commit v3 on v2

v3 whole, which is shorter than its diff:
```python
import functools
import math

import jax
import jax.numpy as jnp
import numpy as np
from jax import lax
from jax.experimental import pallas as pl
from jax.experimental.pallas import tpu as pltpu
from jax.sharding import PartitionSpec as P

LANES = 128
F32 = jnp.float32
BF16 = jnp.bfloat16
MIB = 1 << 20


class Plan:
    def __init__(self, blocks, tok, chans):
        self.B = blocks
        self.T = tok
        self.C = chans
        self.cb = chans // blocks
        self.G = LANES // self.cb
        self.R = tok // self.G
        self.tiles = chans // LANES
        self.cols = tok // blocks
        self.send = 2 * self.cols
        self.Q = blocks // self.G
        self.N = 2 * blocks * tok
        self.K = blocks + 1


def wave(num, den):
    ang = 2.0 * np.pi * (np.asarray(num) % den) / den
    return np.cos(ang), -np.sin(ang)


def tables(s):
    rows = np.arange(s.R)
    lane_e = np.arange(LANES) // s.cb
    dft_c, dft_s = wave(rows[:, None] * rows[None, :], s.R)
    stacked = np.concatenate([dft_c, -dft_s], axis=0)
    k1 = np.arange(s.K)
    tw = wave(rows[None, :, None] * (k1[:, None, None] + 2 * s.B * lane_e[None, None, :]), s.N)
    tw = np.stack(tw, axis=1)
    pre = np.stack(wave(k1[:, None] * lane_e[None, :], 2 * s.B * s.G), axis=1)
    return (
        jnp.asarray(stacked, BF16),
        jnp.asarray(tw, F32),
        jnp.asarray(pre, F32),
    )


def lane_group(s, rows):
    return lax.broadcasted_iota(jnp.int32, (rows, LANES), 1) // s.cb


def turn(v, shift):
    shift = shift % LANES
    return v if shift == 0 else pltpu.roll(v, shift, 1)


def lane_transpose(s, parts, group):
    out = []
    for a in range(s.G):
        acc = None
        for g in range(s.G):
            moved = turn(parts[g], (g - a) * s.cb)
            acc = moved if acc is None else jnp.where(group == g, moved, acc)
        out.append(acc)
    return out


def lane_dft(s, re, im, group, sign):
    if s.G == 1:
        return re, im
    if s.G == 2:
        flip = jnp.where(group == 0, 1.0, -1.0).astype(F32)
        return turn(re, s.cb) + flip * re, turn(im, s.cb) + flip * im
    out_re = out_im = None
    for d in range(s.G):
        mre, mim = turn(re, d * s.cb), turn(im, d * s.cb)
        source = (group - d + s.G) % s.G
        angle_index = (group * source) % s.G
        cos_t = jnp.zeros_like(re)
        sin_t = jnp.zeros_like(re)
        for a in range(s.G):
            c, w = wave(a, s.G)
            cos_t = jnp.where(angle_index == a, float(c), cos_t)
            sin_t = jnp.where(angle_index == a, float(w) * sign, sin_t)
        add_re = mre * cos_t - mim * sin_t
        add_im = mre * sin_t + mim * cos_t
        out_re = add_re if out_re is None else out_re + add_re
        out_im = add_im if out_im is None else out_im + add_im
    return out_re, out_im


def weighted(values, weights):
    acc = None
    for v, w in zip(values, weights):
        w = float(w)
        if abs(w) < 1e-12:
            continue
        term = v if abs(w - 1) < 1e-12 else (-v if abs(w + 1) < 1e-12 else v * w)
        acc = term if acc is None else acc + term
    return acc


def add(a, b):
    return b if a is None else (a if b is None else a + b)


def sub(a, b):
    return a if b is None else (-b if a is None else a - b)


def block_dft(s, xs):
    even, odd = range(0, s.B, 2), range(1, s.B, 2)
    out = [None] * s.K
    for k in range(s.B // 2 + 1):
        ce, se = wave(np.array(even) * k, 2 * s.B)
        co, so = wave(np.array(odd) * k, 2 * s.B)
        xe, xo = [xs[i] for i in even], [xs[i] for i in odd]
        ere, eim = weighted(xe, ce), weighted(xe, se)
        ore, oim = weighted(xo, co), weighted(xo, so)
        out[k] = (add(ere, ore), add(eim, oim))
        if k != s.B - k:
            out[s.B - k] = (sub(ere, ore), sub(oim, eim))
    return out


def block_back(s, ts):
    half = s.B // 2
    sums = {}
    for k in range(half + 1):
        tre, tim = ts[k]
        if k == half:
            sums[k] = (tre, tre, tim, tim)
        else:
            ure, uim = ts[s.B - k]
            sums[k] = (tre + ure, tre - ure, tim - uim, tim + uim)
    out = []
    for i in range(s.B):
        acc = None
        for k in range(half + 1):
            c, w = wave(i * k, 2 * s.B)
            gain = 1.0 if k == 0 else 2.0
            re = sums[k][i % 2]
            im = sums[k][2 + i % 2]
            acc = add(acc, weighted([re, im], [gain * float(c), gain * float(w)]))
        out.append(acc)
    return out


CHUNK = 32
TAIL = 16
TW_PIECES = 2


def forward_rows(s, load, held, tw, pre, ready=()):
    def body(c, _):
        rows = pl.ds(pl.multiple_of(c * CHUNK, CHUNK), CHUNK)
        group = lane_group(s, CHUNK)
        spec = block_dft(s, [load(i, rows) for i in range(s.B)])
        for k in range(s.K):
            re, im = spec[k]
            pr, pi = pre[k, 0:1, :], pre[k, 1:2, :]
            if k == 0:
                im = jnp.zeros_like(re)
            elif im is None:
                re, im = re * pr, re * pi
            else:
                re, im = re * pr - im * pi, re * pi + im * pr
            re, im = lane_dft(s, re, im, group, 1.0)
            tr, ti = tw[k, 0, rows, :], tw[k, 1, rows, :]
            held[k, rows, 0:LANES] = (re * tr - im * ti).astype(BF16)
            held[k, rows, LANES : 2 * LANES] = (re * ti + im * tr).astype(BF16)
        return 0

    pieces = max(len(ready), 1)
    per = s.R // CHUNK // pieces
    for n in range(pieces):
        if ready:
            ready[n].wait()
        lax.fori_loop(n * per, (n + 1) * per, body, 0, unroll=min(2, per))


def forward_bins(s, held_k, dft):
    o = jnp.dot(dft[...], held_k, preferred_element_type=F32)
    re = o[: s.R, :LANES] + o[s.R :, LANES:]
    im = o[: s.R, LANES:] - o[s.R :, :LANES]
    return re, im


def inverse_bins(s, re, im, k, dft, tw, pre, back):
    z = jnp.concatenate([re.astype(BF16), im.astype(BF16)], axis=1)
    o = jnp.dot(dft[...], z, preferred_element_type=F32)
    re = o[: s.R, :LANES] - o[s.R :, LANES:]
    im = o[: s.R, LANES:] + o[s.R :, :LANES]
    tr, ti = tw[k, 0], tw[k, 1]
    re, im = re * tr + im * ti, im * tr - re * ti
    re, im = lane_dft(s, re, im, lane_group(s, s.R), -1.0)
    pr, pi = pre[k, 0:1, :], pre[k, 1:2, :]
    back[k, 0] = re * pr + im * pi
    back[k, 1] = im * pr - re * pi


def inverse_rows(s, back, rows):
    return block_back(s, [(back[k, 0, rows, :], back[k, 1, rows, :]) for k in range(s.K)])


def each_bin(s, body):
    for k in range(s.K):
        body(k)


def each_chunk(s, body):
    def step(c, _):
        body(pl.ds(pl.multiple_of(c * CHUNK, CHUNK), CHUNK), c)
        return 0

    lax.fori_loop(0, s.R // CHUNK, step, 0, unroll=2)


def params(limit=60):
    return pltpu.CompilerParams(vmem_limit_bytes=limit * MIB)


def hbm():
    return pl.BlockSpec(memory_space=pl.ANY)


def vmem():
    return pl.BlockSpec(memory_space=pltpu.VMEM)


def cost(flops, nbytes):
    return pl.CostEstimate(flops=int(flops), bytes_accessed=int(nbytes), transcendentals=0)


def pack_kernel(s, n, *refs):
    arrays, owner, slot, out_at = refs[:n], *refs[n : n + 3]
    out, held, held_owner, held_slot, tail, sems, out_sems = refs[n + 3 :]
    me = lax.axis_index("bins")
    group = lane_group(s, s.R)
    copies = [pltpu.make_async_copy(owner, held_owner, sems.at[n])]
    copies.append(pltpu.make_async_copy(slot, held_slot, sems.at[n + 1]))
    copies += [pltpu.make_async_copy(arrays[a], held.at[a], sems.at[a]) for a in range(n)]
    for c in copies:
        c.start()
    stores = []

    def store(at):
        sem = out_sems.at[len(stores)]
        stores.append(pltpu.make_async_copy(out.at[:, at, :], out_at.at[:, at, :], sem))
        stores[-1].start()

    copies[0].wait()
    copies[1].wait()
    tail[...] = jnp.zeros_like(tail)
    tail[: s.B, : s.cols] = held_owner[...].astype(F32)
    tail[: s.B, s.cols : 2 * s.cols] = (held_slot[...] - me * s.send).astype(F32)
    for b in range(s.B):
        out[b, n * s.R :, :] = tail[...].astype(BF16)
    store(slice(n * s.R, n * s.R + TAIL))
    for a in range(n):
        copies[2 + a].wait()
        for m in range(s.tiles):
            parts = [
                held[a, p * s.R : (p + 1) * s.R, m * LANES : (m + 1) * LANES].astype(F32)
                for p in range(s.G)
            ]
            for q, v in enumerate(lane_transpose(s, parts, group)):
                out[s.G * m + q, a * s.R : (a + 1) * s.R, :] = v.astype(BF16)
        store(slice(a * s.R, (a + 1) * s.R))
    for c in stores:
        c.wait()


def pack(s, owner, slot, *arrays):
    n = len(arrays)
    rows = n * s.R + TAIL
    return pl.pallas_call(
        functools.partial(pack_kernel, s, n),
        out_shape=jax.ShapeDtypeStruct((s.B, rows, LANES), BF16),
        in_specs=[hbm()] * (n + 2),
        out_specs=hbm(),
        scratch_shapes=[
            pltpu.VMEM((s.B, rows, LANES), BF16),
            pltpu.VMEM((n, s.T, s.C), BF16),
            pltpu.VMEM((s.B, s.cols), jnp.int32),
            pltpu.VMEM((s.B, s.cols), jnp.int32),
            pltpu.VMEM((TAIL, LANES), F32),
            pltpu.SemaphoreType.DMA((n + 2,)),
            pltpu.SemaphoreType.DMA((n + 1,)),
        ],
        compiler_params=params(),
        cost_estimate=cost(n * s.T * s.C * 4, n * s.T * s.C * 4),
        name="pack_channels",
    )(*arrays, owner, slot)


def skip_kernel(s, skip, out):
    me = lax.axis_index("bins")
    row = skip[pl.ds(me // s.G, 1), :]
    lane = lane_group(s, 1)
    for q in range(s.G):
        v = lane_transpose(s, [jnp.where(lane == q, row, 0.0)] * s.G, lane)[q]

        @pl.when(me % s.G == q)
        def _():
            out[...] = v


def own_skip(s, skip):
    return pl.pallas_call(
        functools.partial(skip_kernel, s),
        out_shape=jax.ShapeDtypeStruct((1, LANES), F32),
        in_specs=[vmem()],
        out_specs=vmem(),
        compiler_params=params(),
        cost_estimate=cost(LANES, s.C * 4),
        name="own_skip",
    )(skip.reshape(s.tiles, LANES))


def swap_partners(s, parts, after):
    out = [None] * s.B
    out[0] = parts[0]
    for x in [*range(s.B // 2, s.B), *range(s.B // 2 - 1, 0, -1)]:
        part = parts[x]
        if x in after:
            part, out[after[x]] = lax.optimization_barrier((part, out[after[x]]))
        out[x] = lax.ppermute(part, "bins", [(b, b ^ x) for b in range(s.B)])
    return out


def load_parts(s, hops, pieces, weight, piece_held, weight_held, sems):
    chan = lax.axis_index("chan")
    feats = pieces[0].shape[1]
    copies = []
    for a, hop in enumerate(hops):
        at = pl.ds(pl.multiple_of((chan ^ hop) * feats, feats), feats)
        copies.append(
            (
                pltpu.make_async_copy(pieces[a], piece_held.at[a], sems.at[2 * a]),
                pltpu.make_async_copy(weight.at[:, at], weight_held.at[a], sems.at[2 * a + 1]),
            )
        )
    return copies


def multiply(piece, weight):
    return lax.dot_general(
        piece[...], weight[...], (((1,), (1,)), ((), ())), preferred_element_type=F32
    )


def project_part_kernel(s, hops, *refs):
    n = len(hops)
    pieces, weight, refs = refs[:n], refs[n], refs[n + 1 :]
    out_at, out, piece_held, weight_held, sems = refs[-5:]
    start = refs[:-5]
    copies = load_parts(s, hops, pieces, weight, piece_held, weight_held, sems)
    for pair in copies:
        for c in pair:
            c.start()
    if start:
        first = pltpu.make_async_copy(start[0], out, sems.at[2 * n])
        first.start()
    for a, pair in enumerate(copies):
        for c in pair:
            c.wait()
        v = multiply(piece_held.at[a], weight_held.at[a])
        if start and a == 0:
            first.wait()
        out[...] = out[...] + v if start or a else v
    store = pltpu.make_async_copy(out, out_at, sems.at[2 * n + 1])
    store.start()
    store.wait()


def project_scratch(s, n, feats):
    return [
        pltpu.VMEM((s.T, s.C), F32),
        pltpu.VMEM((n, s.T, feats), BF16),
        pltpu.VMEM((n, s.C, feats), BF16),
        pltpu.SemaphoreType.DMA((2 * n + 2,)),
    ]


def project_cost(s, n, feats):
    return cost(s.T * s.C * n, s.T * s.C)


def project_part(s, pieces, hops, weight, start=()):
    n, feats = len(pieces), pieces[0].shape[1]
    return pl.pallas_call(
        functools.partial(project_part_kernel, s, hops),
        out_shape=jax.ShapeDtypeStruct((s.T, s.C), F32),
        in_specs=[hbm()] * (n + 1 + len(start)),
        out_specs=hbm(),
        scratch_shapes=project_scratch(s, n, feats),
        compiler_params=params(40),
        cost_estimate=project_cost(s, n, feats),
        name="project_part",
    )(*pieces, weight, *start)


def project_finish_kernel(s, hops, *refs):
    pieces, weight, start, gate_at, refs = refs[:1], refs[1], refs[2], refs[3], refs[4:]
    dy_at, (away_at, kept_at, acc, piece_held, weight_held, sems) = refs[: s.B], refs[s.B : s.B + 6]
    gate, dy, g, out_sems = refs[s.B + 6 :]
    me = lax.axis_index("bins")
    ((piece_copy, weight_copy),) = load_parts(
        s, hops, pieces, weight, piece_held, weight_held, sems
    )
    first = pltpu.make_async_copy(start, acc, sems.at[2])
    gate_copy = pltpu.make_async_copy(gate_at, gate, sems.at[3])
    loads = (weight_copy, piece_copy, first, gate_copy)
    for c in loads:
        c.start()
    for c in loads:
        c.wait()
    stores = []

    def store(src, dst):
        stores.append(pltpu.make_async_copy(src, dst, out_sems.at[len(stores)]))
        stores[-1].start()

    v = acc[...] + multiply(piece_held.at[0], weight_held.at[0])
    g[...] = v.astype(BF16)
    group = lane_group(s, s.R)
    for m in range(s.tiles):
        lanes = slice(m * LANES, (m + 1) * LANES)
        parts = []
        for p in range(s.G):
            at = (slice(p * s.R, (p + 1) * s.R), lanes)
            parts.append((g[at].astype(F32) * gate[at].astype(F32)).astype(BF16).astype(F32))
        for q, v in enumerate(lane_transpose(s, parts, group)):
            dy[s.G * m + q] = v.astype(BF16)
    for x in range(s.B):
        store(dy.at[me ^ x], dy_at[x])
    half = s.T // 2
    mine = me // (s.B // 2)
    store(g.at[pl.ds(pl.multiple_of(mine * half, half), half), :], kept_at)
    store(g.at[pl.ds(pl.multiple_of((1 - mine) * half, half), half), :], away_at)
    for c in stores:
        c.wait()


def project_finish(s, piece, hop, weight, start, gate):
    feats = piece.shape[1]
    half = jax.ShapeDtypeStruct((s.T // 2, s.C), BF16)
    return pl.pallas_call(
        functools.partial(project_finish_kernel, s, (hop,)),
        out_shape=[jax.ShapeDtypeStruct((s.R, LANES), BF16)] * s.B + [half, half],
        in_specs=[hbm()] * 4,
        out_specs=[hbm()] * (s.B + 2),
        scratch_shapes=project_scratch(s, 1, feats)
        + [
            pltpu.VMEM((s.T, s.C), BF16),
            pltpu.VMEM((s.B, s.R, LANES), BF16),
            pltpu.VMEM((s.T, s.C), BF16),
            pltpu.SemaphoreType.DMA((s.B + 2,)),
        ],
        compiler_params=params(40),
        cost_estimate=project_cost(s, 1, feats),
        name="project_finish",
    )(piece, weight, start, gate)


def swap_halves(s, away):
    return lax.ppermute(away, "bins", [(b, b ^ (s.B // 2)) for b in range(s.B)])


def column_blocks(s, out, rows, c, values):
    group = lane_group(s, CHUNK)
    per = s.cols // CHUNK
    q = c // per
    inner = pl.ds(pl.multiple_of(c % per * CHUNK, CHUNK), CHUNK)
    for i2 in range(s.Q):
        parts = [values[s.G * i2 + a] for a in range(s.G)]
        for p, v in enumerate(lane_transpose(s, parts, group)):
            out[p * s.Q + q, i2, inner, :] = v.astype(BF16)


def tw_copies(s, tw_at, tw, sems, first):
    part = s.R // TW_PIECES
    out = []
    for n in range(TW_PIECES):
        rows = slice(n * part, (n + 1) * part)
        src, dst = tw_at.at[:, :, rows, :], tw.at[:, :, rows, :]
        out.append(pltpu.make_async_copy(src, dst, sems.at[first + n]))
    return out


def spectrum_kernel(s, xh_at, dft_at, tw_at, pre, h_at, h, dft, tw, h_spec, held, sems, out_sems):
    h_copy = pltpu.make_async_copy(xh_at.at[:, s.R : 2 * s.R, :], h, sems.at[0])
    dft_copy = pltpu.make_async_copy(dft_at, dft, sems.at[1])
    tables_in = tw_copies(s, tw_at, tw, sems, 2)
    for c in [h_copy] + tables_in + [dft_copy]:
        c.start()
    h_copy.wait()
    forward_rows(s, lambda i, rows: h[i, rows, :].astype(F32), held, tw, pre, tables_in)
    dft_copy.wait()
    stores = []

    def bins(k):
        re, im = forward_bins(s, held[k], dft)
        h_spec[k, 0] = re
        h_spec[k, 1] = im
        stores.append(pltpu.make_async_copy(h_spec.at[k], h_at.at[k], out_sems.at[k]))
        stores[-1].start()

    each_bin(s, bins)
    for c in stores:
        c.wait()


def row_choice(s, codes, q):
    per = LANES // s.cols
    target = lax.broadcasted_iota(jnp.int32, (s.B * s.send, LANES), 0).astype(F32)
    lane = lax.broadcasted_iota(jnp.int32, (1, LANES), 1) // s.cols
    hits = []
    for p in range(s.G):
        v = codes[p * s.Q + q].astype(F32)
        v = v * float(s.send) + turn(v, -s.cols)
        for t in range(s.B // per):
            row = v[t * per : t * per + 1, :]
            for a in range(1, per):
                other = turn(v[t * per + a : t * per + a + 1, :], a * s.cols)
                row = jnp.where(lane == a, other, row)
            hits.append(jnp.where(target == row, 1.0, 0.0).astype(BF16))
    return jnp.concatenate(hits, axis=1)


def token_kernel(s, *refs):
    parts, refs = refs[: s.B], refs[s.B :]
    came, h_at, skip_at, dft_at, tw_at, pre_at, y_at, out_at = refs[:8]
    dy, codes, h_spec, skip, dft, tw, pre, y_spec, out, held, back, tok, sems, y_sems = refs[8:]
    me = lax.axis_index("bins")
    pairs = [(came.at[:, 2 * s.R :, :], codes), (pre_at, pre), (skip_at, skip)]
    pairs += [(parts[x], dy.at[me ^ x]) for x in range(s.B)]
    pairs += [(dft_at, dft), (h_at, h_spec)]
    copies = [pltpu.make_async_copy(a, b, sems.at[n]) for n, (a, b) in enumerate(pairs)]
    copies[-2:-2] = tw_copies(s, tw_at, tw, sems, len(pairs))
    for c in copies:
        c.start()
    copies[0].wait()
    first = s.B + 3
    for c in copies[1:first]:
        c.wait()
    forward_rows(s, lambda i, rows: dy[i, rows, :].astype(F32), held, tw, pre, copies[first:-2])
    copies[-2].wait()
    copies[-1].wait()
    stores = []

    def bins(k):
        yre, yim = forward_bins(s, held[k], dft)
        y_spec[k, 0] = yre
        y_spec[k, 1] = yim
        stores.append(pltpu.make_async_copy(y_spec.at[k], y_at.at[k], y_sems.at[k]))
        stores[-1].start()
        hre, him = h_spec[k, 0], h_spec[k, 1]
        inverse_bins(s, hre * yre + him * yim, hre * yim - him * yre, k, dft, tw, pre, back)

    each_bin(s, bins)

    def last(rows, c):
        back_rows = inverse_rows(s, back, rows)
        for i in range(s.B):
            v = back_rows[i] * (1.0 / s.N) + skip[...] * dy[i, rows, :].astype(F32)
            tok[i, rows, :] = v.astype(BF16)

    each_chunk(s, last)

    group = lane_group(s, s.B * s.cols)
    for q in range(s.Q):
        rows = slice(q * s.cols, (q + 1) * s.cols)
        v = jnp.concatenate([tok[i, rows, :] for i in range(s.B)], axis=0)
        zero = jnp.zeros_like(v)
        v = jnp.concatenate([jnp.where(group == p, v, zero) for p in range(s.G)], axis=0)
        o = jnp.dot(row_choice(s, codes, q), v, preferred_element_type=F32)
        at = slice(q * s.send, (q + 1) * s.send)
        for b in range(s.B):
            out[b, at, :] = o[b * s.send : (b + 1) * s.send].astype(BF16)
        sem = y_sems.at[s.K + q]
        stores.append(pltpu.make_async_copy(out.at[:, at, :], out_at.at[:, at, :], sem))
        stores[-1].start()
    for c in stores:
        c.wait()


def products_kernel(s, xh_at, h_at, y_at, kept, g_came, skip, dft_at, tw_at, pre, *refs):
    outs, refs = refs[: s.B], refs[s.B :]
    x, h_spec, y_spec, dft, tw, x_spec, held, back, u, lags, sems = refs
    x_copy = pltpu.make_async_copy(xh_at.at[:, : s.R, :], x, sems.at[0])
    dft_copy = pltpu.make_async_copy(dft_at, dft, sems.at[1])
    h_copy = pltpu.make_async_copy(h_at, h_spec, sems.at[2])
    y_copy = pltpu.make_async_copy(y_at, y_spec, sems.at[3])
    tables_in = tw_copies(s, tw_at, tw, sems, 4)
    for c in [x_copy] + tables_in + [dft_copy, h_copy, y_copy]:
        c.start()
    x_copy.wait()
    forward_rows(s, lambda i, rows: x[i, rows, :].astype(F32), held, tw, pre, tables_in)
    dft_copy.wait()
    h_copy.wait()

    def x_bins(k):
        xre, xim = forward_bins(s, held[k], dft)
        x_spec[k, 0] = xre
        x_spec[k, 1] = xim
        hre, him = h_spec[k, 0], h_spec[k, 1]
        inverse_bins(s, xre * hre - xim * him, xre * him + xim * hre, k, dft, tw, pre, back)

    each_bin(s, x_bins)

    def conv_rows(rows, c):
        conv = inverse_rows(s, back, rows)
        values = [
            conv[i] * (1.0 / s.N) + skip[...] * x[i, rows, :].astype(F32) for i in range(s.B)
        ]
        column_blocks(s, u, rows, c, values)

    each_chunk(s, conv_rows)
    y_copy.wait()

    def lag_bins(k):
        xre, xim = x_spec[k, 0], x_spec[k, 1]
        yre, yim = y_spec[k, 0], y_spec[k, 1]
        inverse_bins(s, yre * xre + yim * xim, yim * xre - yre * xim, k, dft, tw, pre, back)

    each_bin(s, lag_bins)
    scale = 1.0 / (s.N * math.sqrt(s.B * s.T))

    def lag_rows(rows, c):
        column_blocks(s, lags, rows, c, [v * scale for v in inverse_rows(s, back, rows)])

    each_chunk(s, lag_rows)
    me = lax.axis_index("bins")
    for d in range(s.B):
        outs[d][0] = u[me ^ d]
        outs[d][1] = lags[me ^ d]
        if d < s.B // 2:
            at = (me ^ d) % (s.B // 2) * s.cols
            rows = pl.ds(pl.multiple_of(at, s.cols), s.cols)
            for m in range(s.tiles):
                lanes = slice(m * LANES, (m + 1) * LANES)
                outs[d][2, m] = kept[rows, lanes]
                outs[d][3, m] = g_came[rows, lanes]


def rows_kernel(s, inbox_at, rows_at, inbox, rows, in_sems, sems):
    copies = []
    for m in range(s.tiles):
        at = slice(m * s.G, (m + 1) * s.G)
        copies.append(pltpu.make_async_copy(inbox_at.at[at], inbox.at[at], in_sems.at[m]))
        copies[-1].start()
    stores = []
    group = lane_group(s, s.send)
    for m in range(s.tiles):
        copies[m].wait()
        lanes = slice(m * LANES, (m + 1) * LANES)
        for q in range(s.Q):
            vs = [
                inbox[s.G * m + a, q * s.send : (q + 1) * s.send, :].astype(F32)
                for a in range(s.G)
            ]
            for p, v in enumerate(lane_transpose(s, vs, group)):
                at = (p * s.Q + q) * s.send
                rows[at : at + s.send, lanes] = v.astype(BF16)
        src, dst = rows.at[:, lanes], rows_at.at[:, lanes]
        stores.append(pltpu.make_async_copy(src, dst, sems.at[m]))
        stores[-1].start()
    for c in stores:
        c.wait()


def owner_rows(s, inbox):
    rows_shape = (s.B * s.send, s.C)
    return pl.pallas_call(
        functools.partial(rows_kernel, s),
        out_shape=jax.ShapeDtypeStruct(rows_shape, BF16),
        in_specs=[hbm()],
        out_specs=hbm(),
        scratch_shapes=[
            pltpu.VMEM(inbox.shape, BF16),
            pltpu.VMEM(rows_shape, BF16),
            pltpu.SemaphoreType.DMA((s.tiles,)),
            pltpu.SemaphoreType.DMA((s.tiles,)),
        ],
        compiler_params=params(40),
        cost_estimate=cost(s.T * s.C * 4, s.T * s.C * 8),
        name="owner_rows",
    )(inbox)


def columns_kernel(s, *refs):
    parts, refs = refs[: s.B], refs[s.B :]
    half = s.B // 2
    gate_at, filter_at, src, g, gate_grad, filter_grad, part_sems, g_sems, sems = refs
    me = lax.axis_index("bins")
    copies = []
    for x in range(s.B):
        block = src.at[me ^ x]
        copies.append(pltpu.make_async_copy(parts[x].at[:2], block, part_sems.at[x]))
    for x in range(half):
        for far in range(2):
            block = g.at[me ^ x ^ (far * half)]
            sem = g_sems.at[2 * x + far]
            copies.append(pltpu.make_async_copy(parts[x].at[2 + far], block, sem))
    for c in copies:
        c.start()
    for c in copies[s.B :]:
        c.wait()
    stores = []
    group = lane_group(s, s.cols)
    for n in range(s.tiles):
        for c in copies[s.G * n : s.G * (n + 1)]:
            c.wait()
        m = me // s.G ^ n
        lanes = pl.ds(pl.multiple_of(m * LANES, LANES), LANES)
        for kind, (out, out_at) in enumerate(((gate_grad, gate_at), (filter_grad, filter_at))):
            for i2 in range(s.Q):
                vs = [src[s.G * m + a, kind, i2].astype(F32) for a in range(s.G)]
                for a, v in enumerate(lane_transpose(s, vs, group)):
                    i = s.G * i2 + a
                    if kind == 0:
                        v = (v * g[i, m].astype(F32)).astype(BF16)
                    out[i, :, lanes] = v
            sem = sems.at[len(stores)]
            at = (slice(None), slice(None), lanes)
            stores.append(pltpu.make_async_copy(out.at[at], out_at.at[at], sem))
            stores[-1].start()
    for c in stores:
        c.wait()


def columns(s, parts):
    cols_shape = (s.B, s.cols, s.C)
    return pl.pallas_call(
        functools.partial(columns_kernel, s),
        out_shape=[
            jax.ShapeDtypeStruct(cols_shape, BF16),
            jax.ShapeDtypeStruct(cols_shape, F32),
        ],
        in_specs=[hbm()] * s.B,
        out_specs=[hbm()] * 2,
        scratch_shapes=[
            pltpu.VMEM((s.B,) + parts[-1].shape, BF16),
            pltpu.VMEM((s.B, s.tiles, s.cols, LANES), BF16),
            pltpu.VMEM(cols_shape, BF16),
            pltpu.VMEM(cols_shape, F32),
            pltpu.SemaphoreType.DMA((s.B,)),
            pltpu.SemaphoreType.DMA((s.B,)),
            pltpu.SemaphoreType.DMA((2 * s.tiles,)),
        ],
        compiler_params=params(40),
        cost_estimate=cost(s.T * s.C * 8, s.T * s.C * 12),
        name="columns",
    )(*parts)


def exchange(v):
    return lax.all_to_all(v, "bins", split_axis=0, concat_axis=0, tiled=True)


def shards(tokens_in, filters, gate, skip, out_grad, out_weight, owner, slot):
    s = Plan(lax.axis_size("bins"), *tokens_in.shape)
    me = lax.axis_index("bins")
    nchan = lax.axis_size("chan")
    dft, tw, pre = tables(s)
    spec_shape = jax.ShapeDtypeStruct((s.K, 2, s.R, LANES), F32)
    spec_bytes = s.K * 2 * s.R * LANES * 4
    transform = 2 * 2 * s.R * s.R * 2 * LANES * s.K
    held = pltpu.VMEM((s.K, s.R, 2 * LANES), BF16)
    back = pltpu.VMEM((s.K, 2, s.R, LANES), F32)

    packed = pack(s, owner, slot, tokens_in, filters)
    came = exchange(packed)

    across = nchan // 2
    core_pairs = [(c, c ^ 1) for c in range(nchan)]
    far = lax.ppermute(out_grad, "chan", [(c, c ^ across) for c in range(nchan)])
    near = lax.ppermute(out_grad, "chan", core_pairs)
    start = project_part(s, [out_grad, near], (0, 1), out_weight)
    my_skip = own_skip(s, skip)
    far, start, my_skip = lax.optimization_barrier((far, start, my_skip))
    far_near = lax.ppermute(far, "chan", core_pairs)
    start = project_part(s, [far], (across,), out_weight, (start,))
    *dy, away, kept = project_finish(s, far_near, across ^ 1, out_weight, start, gate)
    dy = swap_partners(s, dy, {1: 2})

    block = pltpu.VMEM((s.B, s.R, LANES), BF16)
    dft_held = pltpu.VMEM((2 * s.R, s.R), BF16)
    h_spec = pl.pallas_call(
        functools.partial(spectrum_kernel, s),
        out_shape=spec_shape,
        in_specs=[hbm(), hbm(), hbm(), vmem()],
        out_specs=hbm(),
        scratch_shapes=[
            block,
            dft_held,
            back,
            back,
            held,
            pltpu.SemaphoreType.DMA((2 + TW_PIECES,)),
            pltpu.SemaphoreType.DMA((s.K,)),
        ],
        compiler_params=params(),
        cost_estimate=cost(10 * transform, 2 * spec_bytes),
        name="filter_spectrum",
    )(came, dft, tw, pre)

    away, dy[4] = lax.optimization_barrier((away, dy[4]))
    g_came = swap_halves(s, away)

    outbox_shape = (s.B, s.Q * s.send, LANES)
    y_spec, outbox = pl.pallas_call(
        functools.partial(token_kernel, s),
        out_shape=[spec_shape, jax.ShapeDtypeStruct(outbox_shape, BF16)],
        in_specs=[hbm()] * (s.B + 6),
        out_specs=[hbm()] * 2,
        scratch_shapes=[
            block,
            pltpu.VMEM((s.B, TAIL, LANES), BF16),
            back,
            pltpu.VMEM((1, LANES), F32),
            dft_held,
            back,
            pltpu.VMEM((s.K, 2, LANES), F32),
            back,
            pltpu.VMEM(outbox_shape, BF16),
            held,
            back,
            block,
            pltpu.SemaphoreType.DMA((s.B + 5 + TW_PIECES,)),
            pltpu.SemaphoreType.DMA((s.K + s.Q,)),
        ],
        compiler_params=params(),
        cost_estimate=cost(20 * transform, 3 * spec_bytes),
        name="token_products",
    )(*dy, came, h_spec, my_skip, dft, tw, pre)
    outbox, g_came = lax.optimization_barrier((outbox, g_came))
    inbox = exchange(outbox)

    cols_shape = (s.Q, s.cols, LANES)
    by_dest = pltpu.VMEM((s.B,) + cols_shape, BF16)
    parts = pl.pallas_call(
        functools.partial(products_kernel, s),
        out_shape=[
            jax.ShapeDtypeStruct((4 if x < s.B // 2 else 2,) + cols_shape, BF16)
            for x in range(s.B)
        ],
        in_specs=[hbm()] * 3 + [vmem()] * 3 + [hbm()] * 2 + [vmem()],
        out_specs=[vmem()] * s.B,
        scratch_shapes=[
            block,
            back,
            back,
            dft_held,
            back,
            back,
            held,
            back,
            by_dest,
            by_dest,
            pltpu.SemaphoreType.DMA((4 + TW_PIECES,)),
        ],
        compiler_params=params(),
        cost_estimate=cost(3 * transform, 4 * spec_bytes),
        name="conv_and_filter",
    )(came, h_spec, y_spec, kept, g_came, my_skip, dft, tw, pre)
    grad_rows = owner_rows(s, inbox)
    *parts, last = parts
    last, grad_rows = lax.optimization_barrier((last, grad_rows))
    parts = swap_partners(s, [*parts, last], {1: 2})
    gate_grad, filter_grad = columns(s, parts)
    return (gate_grad, filter_grad, grad_rows)


def solution(mesh):
    return jax.shard_map(
        shards,
        mesh=mesh,
        in_specs=(
            P("bins", "chan"),
            P("bins", "chan"),
            P("bins", "chan"),
            P("chan"),
            P("bins", "chan"),
            P("chan", None),
            P(None, "bins"),
            P(None, "bins"),
        ),
        out_specs=(P(None, "bins", "chan"), P(None, "bins", "chan"), P("bins", "chan")),
        check_vma=False,
    )
```

time: 133 us -> 119 us (0.89)
  the two profiles are of different devices: /device:TPU:0 before, /device:TPU:10 now
where the time goes in v3:
time: 119 us
  Pallas kernels  38.1 us (32%)
  starting transfers between devices  37.8 us (32%)
  waiting for transfers between devices  36.9 us (31%)
  local copies, waits for them, and re-layouts  5.14 us (4%)
    ppermute x14, waiting for transfers between devices, swap_partners(): out[x] = lax.ppermute(part, 'bins', [(b, b ^ x) for b in range(s.B)])  24.6 us
    ppermute x14, starting transfers between devices, swap_partners(): out[x] = lax.ppermute(part, 'bins', [(b, b ^ x) for b in range(s.B)])  21.3 us
    all_to_all x2, starting transfers between devices, exchange(): return lax.all_to_all(v, 'bins', split_axis=0, concat_axis=0, tiled=True)  11.4 us
    ppermute x1, waiting for transfers between devices, shards(): lax.ppermute(out_grad, 'chan', [(c, c ^ across) for c in range(nchan)])  10.9 us
    pallas_call x1, Pallas kernels, shards(): pl.pallas_call(functools.partial(products_kernel, s), out_shape=[jax.Shap...  9.92 us
    pallas_call x1, Pallas kernels, shards(): pl.pallas_call(functools.partial(token_kernel, s), out_shape=[spec_shape,...  8.85 us
    pallas_call x1, Pallas kernels, shards(): pl.pallas_call(functools.partial(spectrum_kernel, s), out_shape=spec_shap...  5.19 us
    unnamed x30, local copies, waits for them, and re-layouts  5.14 us
  transfers between devices with their start and end apart: 20, of which 6 were waited for; matrix products, arithmetic and copies ran while one was open for 0% of the time, Pallas kernels for 29%

profile of v3, /device:TPU:10, one launch (start us, length us, event | category | flops | bytes accessed | tf_op | source)
XLA Modules:
  0.0 118.9 jit_solution(4828284971209727043)
XLA Ops:
  1.3 2.3 %pack_channels.1 = bf16[8,528,128]{2,1,0:T(8,128)(2,1)} custom-call(bf16[512,512]{1,0:T(8,128)(2,1)} %refs_0_.2, bf16[512,512]{1,0:T(8,128)(2,1)} %refs_1_.3, s32[8,64]{1,0:T(8,128)} %refs_2_.2, s32[8,64]{1,0:T(8,128)} %refs_3_.2), custom_call_target="tpu_custom_call" | custom-call | flops 2097152 | bytes 2097152 | tf_op jit(solution)/shard_map/pack_channels/pallas_call | solution.py:284
  3.7 6.3 %all-to-all-start = ((bf16[8,528,128]{2,1,0:T(8,128)(2,1)}), bf16[8,528,128]{2,1,0:T(8,128)(2,1)}, u32[]{:S(2)}, u32[]{:S(2)}) async-start(bf16[8,528,128]{2,1,0:T(8,128)(2,1)} %pack_channels.1), calls=%async_computation | async-start | bytes 2162688 | tf_op jit(solution)/shard_map/all_to_all | solution.py:767
  11.4 2.2 %copy-done = bf16[512,4096]{1,0:T(8,128)(2,1)S(1)} copy-done((bf16[512,4096]{1,0:T(8,128)(2,1)S(1)}, bf16[512,4096]{1,0:T(8,128)(2,1)}, u32[]{:S(2)}) %copy-start) | copy-done | bytes 4194328
  13.6 2.0 %project_part.2.refs_2_ = f32[512,512]{1,0:T(8,128)S(1)} custom-call(bf16[512,1024]{1,0:T(8,128)(2,1)S(1)} %copy-done.2, bf16[512,1024]{1,0:T(8,128)(2,1)S(1)} %collective-permute-done.1.refs_1_, bf16[512,4096]{1,0:T(8,128)(2,1)S(1)} %copy-done), custom_call_target="tpu_custom_call" | custom-call | flops 524288 | bytes 262144 | tf_op jit(solution)/shard_map/project_part/pallas_call | solution.py:399
  15.6 10.9 %collective-permute-done.refs_0_ = bf16[512,1024]{1,0:T(8,128)(2,1)S(1)} collective-permute-done((bf16[512,1024]{1,0:T(8,128)(2,1)}, bf16[512,1024]{1,0:T(8,128)(2,1)S(1)}, u32[]{:S(2)}, u32[]{:S(2)}) %collective-permute-start) | collective-permute-done | bytes 1048608 | tf_op jit(solution)/shard_map/ppermute | solution.py:786
  29.2 2.2 %project_finish.1 = (bf16[256,128]{1,0:T(8,128)(2,1)S(1)}, bf16[256,128]{1,0:T(8,128)(2,1)S(1)}, bf16[256,128]{1,0:T(8,128)(2,1)S(1)}, bf16[256,128]{1,0:T(8,128...) custom-call(bf16[512,1024]{1,0:T(8,128)(2,1)S(1)} %collective-permut, ...), custom_call_target="tpu_custom_call" | custom-call | flops 262144 | bytes 262144 | tf_op jit(solution)/shard_map/project_finish/pallas_call | solution.py:456
  33.1 2.6 %collective-permute-start.6 = (bf16[256,128]{1,0:T(8,128)(2,1)S(1)}, bf16[256,128]{1,0:T(8,128)(2,1)S(1)}, u32[]{:S(2)}, u32[]{:S(2)}) collective-permute-start(bf16[256,128]{1,0:T(8,128)(2,1)S(1)} %get-tuple-element.47), channel_id=1, source_target_pairs={{0,16},{4,20},{8,24},{12,28},{16,0},{20,4},{24,8},{28,12},{1,17},{... | collective-permute-start | bytes 196616 | tf_op jit(solution)/shard_map/ppermute | solution.py:335
  35.7 2.5 %collective-permute-start.5 = (bf16[256,128]{1,0:T(8,128)(2,1)S(1)}, bf16[256,128]{1,0:T(8,128)(2,1)S(1)}, u32[]{:S(2)}, u32[]{:S(2)}) collective-permute-start(bf16[256,128]{1,0:T(8,128)(2,1)S(1)} %get-tuple-element.45), channel_id=1, source_target_pairs={{0,12},{4,8},{8,4},{12,0},{16,28},{20,24},{24,20},{28,16},{1,13},{... | collective-permute-start | bytes 196616 | tf_op jit(solution)/shard_map/ppermute | solution.py:335
  38.5 1.6 %collective-permute-start.8 = (bf16[256,128]{1,0:T(8,128)(2,1)S(1)}, bf16[256,128]{1,0:T(8,128)(2,1)S(1)}, u32[]{:S(2)}, u32[]{:S(2)}) collective-permute-start(bf16[256,128]{1,0:T(8,128)(2,1)S(1)} %get-tuple-element.50), channel_id=1, source_target_pairs={{0,24},{4,28},{8,16},{12,20},{16,8},{20,12},{24,0},{28,4},{1,25},{... | collective-permute-start | bytes 196616 | tf_op jit(solution)/shard_map/ppermute | solution.py:335
  42.0 5.2 %filter_spectrum.1.refs_9_.h_at = f32[9,2,256,128]{3,2,1,0:T(8,128)} custom-call(bf16[8,528,128]{2,1,0:T(8,128)(2,1)} %all-to-all-done.xh_at.refs_8_, bf16[512,256]{1,0:T(8,128)(2,1)} %constant.6.clone.dft_at.refs_11_, f32[9,2,256,128]{3,2,1,0:T(8,128)} %constant.7.clone.tw_at.refs_12_, f32[9,2,128]{2,1,0:T(2,128)} %constant.8.clone.pre.refs_13_), custom_call_target="tpu_custom_call" | custom-call | flops 6039797760 | bytes 4718592 | tf_op jit(solution)/shard_map/filter_spectrum/pallas_call | solution.py:798
  47.3 4.5 %collective-permute-start.10 = (bf16[256,512]{1,0:T(8,128)(2,1)S(1)}, bf16[256,512]{1,0:T(8,128)(2,1)S(1)}, u32[]{:S(2)}, u32[]{:S(2)}) collective-permute-start(bf16[256,512]{1,0:T(8,128)(2,1)S(1)} %get-tuple-element.56), channel_id=1, source_target_pairs={{0,16},{4,20},{8,24},{12,28},{16,0},{20,4},{24,8},{28,12},{1,17},{... | collective-permute-start | bytes 786440 | tf_op jit(solution)/shard_map/ppermute | solution.py:475
  52.4 8.8 %token_products.1 = (f32[9,2,256,128]{3,2,1,0:T(8,128)}, bf16[8,512,128]{2,1,0:T(8,128)(2,1)}) custom-call(bf16[256,128]{1,0:T(8,128)(2,1)} %copy-done.6, bf16[256,128]{1,0:T(8,128)(2,1)} %copy-done.14, bf16[256,128]{1,0:T(8,128)(2,1)} %copy-done.8, bf16[256,128]{1,0:T(8,128)(2,1)} %copy-done.10, bf16[256,128]{1,0:T(8,128)(2,1)} %copy-done.9, ...), custom_call_target="tpu_custom_call" | custom-call | flops 12079595520 | bytes 7077888 | tf_op jit(solution)/shard_map/token_products/pallas_call | solution.py:821
  61.3 5.1 %all-to-all-start.1 = ((bf16[8,512,128]{2,1,0:T(8,128)(2,1)}), bf16[8,512,128]{2,1,0:T(8,128)(2,1)S(1)}, u32[]{:S(2)}, u32[]{:S(2)}) async-start(bf16[8,512,128]{2,1,0:T(8,128)(2,1)} %get-tuple-element.68), calls=%async_computation.1 | async-start | bytes 2097152 | tf_op jit(solution)/shard_map/all_to_all | solution.py:767
  66.4 9.9 %conv_and_filter.1 = (bf16[4,4,64,128]{3,2,1,0:T(8,128)(2,1)}, bf16[4,4,64,128]{3,2,1,0:T(8,128)(2,1)}, bf16[4,4,64,128]{3,2,1,0:T(8,128)(2,1)}, bf16[4,4,64,128...) custom-call(bf16[8,528,128]{2,1,0:T(8,128)(2,1)} %all-to-all-done.xh, ...), custom_call_target="tpu_custom_call" | custom-call | flops 1811939328 | bytes 9437184 | tf_op jit(solution)/shard_map/conv_and_filter/pallas_call | solution.py:851
  76.4 2.9 %collective-permute-start.14 = (bf16[2,4,64,128]{3,2,1,0:T(8,128)(2,1)}, bf16[2,4,64,128]{3,2,1,0:T(8,128)(2,1)S(1)}, u32[]{:S(2)}, u32[]{:S(2)}) collective-permute-start(bf16[2,4,64,128]{3,2,1,0:T(8,128)(2,1)} %get-tuple-element.64), channel_id=1, source_target_pairs={{0,16},{4,20},{8,24},{12,28},{16,0},{20,4},{24,8},{28,12},{1,17},{... | collective-permute-start | bytes 393224 | tf_op jit(solution)/shard_map/ppermute | solution.py:335
  79.3 2.4 %collective-permute-start.13 = (bf16[4,4,64,128]{3,2,1,0:T(8,128)(2,1)}, bf16[4,4,64,128]{3,2,1,0:T(8,128)(2,1)S(1)}, u32[]{:S(2)}, u32[]{:S(2)}) collective-permute-start(bf16[4,4,64,128]{3,2,1,0:T(8,128)(2,1)} %get-tuple-element.63), channel_id=1, source_target_pairs={{0,12},{4,8},{8,4},{12,0},{16,28},{20,24},{24,20},{28,16},{1,13},{... | collective-permute-start | bytes 786440 | tf_op jit(solution)/shard_map/ppermute | solution.py:335
  81.7 9.4 %collective-permute-done.11.refs_2_ = bf16[4,4,64,128]{3,2,1,0:T(8,128)(2,1)S(1)} collective-permute-done((bf16[4,4,64,128]{3,2,1,0:T(8,128)(2,1)}, bf16[4,4,64,128]{3,2,1,0:T(8,128)(2,1)S(1)}, u32[]{:S(2)}, u32[]{:S(2)}) %collective-permute-start.11) | collective-permute-done | bytes 262176 | tf_op jit(solution)/shard_map/ppermute | solution.py:335
  91.1 1.6 %collective-permute-start.12 = (bf16[4,4,64,128]{3,2,1,0:T(8,128)(2,1)}, bf16[4,4,64,128]{3,2,1,0:T(8,128)(2,1)S(1)}, u32[]{:S(2)}, u32[]{:S(2)}) collective-permute-start(bf16[4,4,64,128]{3,2,1,0:T(8,128)(2,1)} %get-tuple-element.61), channel_id=1, source_target_pairs={{0,4},{4,0},{8,12},{12,8},{16,20},{20,16},{24,28},{28,24},{1,5},{5... | collective-permute-start | bytes 786440 | tf_op jit(solution)/shard_map/ppermute | solution.py:335
  92.7 2.6 %collective-permute-start.15 = (bf16[2,4,64,128]{3,2,1,0:T(8,128)(2,1)}, bf16[2,4,64,128]{3,2,1,0:T(8,128)(2,1)S(1)}, u32[]{:S(2)}, u32[]{:S(2)}) collective-permute-start(bf16[2,4,64,128]{3,2,1,0:T(8,128)(2,1)} %get-tuple-element.65), channel_id=1, source_target_pairs={{0,20},{4,16},{8,28},{12,24},{16,4},{20,0},{24,12},{28,8},{1,21},{... | collective-permute-start | bytes 393224 | tf_op jit(solution)/shard_map/ppermute | solution.py:335
  96.7 2.4 %collective-permute-start.17 = (bf16[2,4,64,128]{3,2,1,0:T(8,128)(2,1)}, bf16[2,4,64,128]{3,2,1,0:T(8,128)(2,1)S(1)}, u32[]{:S(2)}, u32[]{:S(2)}) collective-permute-start(bf16[2,4,64,128]{3,2,1,0:T(8,128)(2,1)} %get-tuple-element.69), channel_id=1, source_target_pairs={{0,28},{4,24},{8,20},{12,16},{16,12},{20,8},{24,4},{28,0},{1,29},{... | collective-permute-start | bytes 393224 | tf_op jit(solution)/shard_map/ppermute | solution.py:335
  99.1 8.9 %collective-permute-done.15.refs_5_ = bf16[2,4,64,128]{3,2,1,0:T(8,128)(2,1)S(1)} collective-permute-done((bf16[2,4,64,128]{3,2,1,0:T(8,128)(2,1)}, bf16[2,4,64,128]{3,2,1,0:T(8,128)(2,1)S(1)}, u32[]{:S(2)}, u32[]{:S(2)}) %collective-permute-start.15) | collective-permute-done | bytes 131104 | tf_op jit(solution)/shard_map/ppermute | solution.py:335
  108.0 3.9 %collective-permute-done.16.refs_6_ = bf16[2,4,64,128]{3,2,1,0:T(8,128)(2,1)S(1)} collective-permute-done((bf16[2,4,64,128]{3,2,1,0:T(8,128)(2,1)}, bf16[2,4,64,128]{3,2,1,0:T(8,128)(2,1)S(1)}, u32[]{:S(2)}, u32[]{:S(2)}) %collective-permute-start.16) | collective-permute-done | bytes 131104 | tf_op jit(solution)/shard_map/ppermute | solution.py:335
  111.9 2.4 %collective-permute-done.17.refs_7_ = bf16[2,4,64,128]{3,2,1,0:T(8,128)(2,1)S(1)} collective-permute-done((bf16[2,4,64,128]{3,2,1,0:T(8,128)(2,1)}, bf16[2,4,64,128]{3,2,1,0:T(8,128)(2,1)S(1)}, u32[]{:S(2)}, u32[]{:S(2)}) %collective-permute-start.17) | collective-permute-done | bytes 131104 | tf_op jit(solution)/shard_map/ppermute | solution.py:335
  115.3 3.5 %columns.1 = (bf16[8,64,512]{2,1,0:T(8,128)(2,1)}, f32[8,64,512]{2,1,0:T(8,128)}) custom-call(bf16[4,4,64,128]{3,2,1,0:T(8,128)(2,1)S(1)} %copy-done.5, bf16[4,4,64,128]{3,2,1,0:T(8,128)(2,1)S(1)} %collective-permute-done.12.refs_1_, bf16[4,4,64,128]{3,2,1,0:T(8,128)(2,1)S(1)} %collective-permute-done.11.refs_2_, ...), custom_call_target="tpu_custom_call" | custom-call | flops 2097152 | bytes 3145728 | tf_op jit(solution)/shard_map/columns/pallas_call | solution.py:743
  (56 shorter events, 11.9 us)
Async XLA Ops:
  0.6 10.7 %copy-start.2 = (bf16[512,1024]{1,0:T(8,128)(2,1)S(1)}, bf16[512,1024]{1,0:T(8,128)(2,1)}, u32[]{:S(2)}) copy-start(bf16[512,1024]{1,0:T(8,128)(2,1)} %refs_0_.3) | copy-start | bytes 3145732
  0.6 10.7 %collective-permute-start.1 = (bf16[512,1024]{1,0:T(8,128)(2,1)}, bf16[512,1024]{1,0:T(8,128)(2,1)S(1)}, u32[]{:S(2)}, u32[]{:S(2)}) collective-permute-start(bf16[512,1024]{1,0:T(8,128)(2,1)} %refs_0_.3), channel_id=1, source_target_pairs={{0,1},{1,0},{2,3},{3,2},{4,5},{5,4},{6,7},{7,6},{8,9},{9,8},{10,11... | collective-permute-start | bytes 3145736 | tf_op jit(solution)/shard_map/ppermute | solution.py:787
  0.7 25.8 %collective-permute-start = (bf16[512,1024]{1,0:T(8,128)(2,1)}, bf16[512,1024]{1,0:T(8,128)(2,1)S(1)}, u32[]{:S(2)}, u32[]{:S(2)}) collective-permute-start(bf16[512,1024]{1,0:T(8,128)(2,1)} %refs_0_.3), channel_id=1, source_target_pairs={{0,2},{1,3},{2,0},{3,1},{4,6},{5,7},{6,4},{7,5},{8,10},{9,11},{10,... | collective-permute-start | bytes 3145736 | tf_op jit(solution)/shard_map/ppermute | solution.py:786
  3.7 38.4 %all-to-all-start = ((bf16[8,528,128]{2,1,0:T(8,128)(2,1)}), bf16[8,528,128]{2,1,0:T(8,128)(2,1)}, u32[]{:S(2)}, u32[]{:S(2)}) async-start(bf16[8,528,128]{2,1,0:T(8,128)(2,1)} %pack_channels.1), calls=%async_computation | async-start | bytes 2162688 | tf_op jit(solution)/shard_map/all_to_all | solution.py:767
  13.6 13.0 %copy-start.1 = (bf16[512,4096]{1,0:T(8,128)(2,1)S(1)}, bf16[512,4096]{1,0:T(8,128)(2,1)}, u32[]{:S(2)}) copy-start(bf16[512,4096]{1,0:T(8,128)(2,1)} %refs_1_.5) | copy-start | bytes 12582916
  15.6 13.6 %copy-start.3 = (bf16[512,512]{1,0:T(8,128)(2,1)S(1)}, bf16[512,512]{1,0:T(8,128)(2,1)}, u32[]{:S(2)}) copy-start(bf16[512,512]{1,0:T(8,128)(2,1)} %refs_3_.3) | copy-start | bytes 1572868
  26.5 2.7 %collective-permute-start.2 = (bf16[512,1024]{1,0:T(8,128)(2,1)S(1)}, bf16[512,1024]{1,0:T(8,128)(2,1)S(1)}, u32[]{:S(2)}, u32[]{:S(2)}) collective-permute-start(bf16[512,1024]{1,0:T(8,128)(2,1)S(1)} %collective-permute-done.refs_0_), channel_id=1, source_target_pairs={{0,1},{1,0},{2,3},{3,2},{4,5},{5,4},{6,7},{7,6},{8,9},{9,8},{10,11... | collective-permute-start | bytes 3145736 | tf_op jit(solution)/shard_map/ppermute | solution.py:791
  32.7 7.4 %collective-permute-start.3 = (bf16[256,128]{1,0:T(8,128)(2,1)S(1)}, bf16[256,128]{1,0:T(8,128)(2,1)S(1)}, u32[]{:S(2)}, u32[]{:S(2)}) collective-permute-start(bf16[256,128]{1,0:T(8,128)(2,1)S(1)} %get-tuple-element.42), channel_id=1, source_target_pairs={{0,8},{4,12},{8,0},{12,4},{16,24},{20,28},{24,16},{28,20},{1,9},{5... | collective-permute-start | bytes 196616 | tf_op jit(solution)/shard_map/ppermute | solution.py:335
  33.1 8.4 %collective-permute-start.6 = (bf16[256,128]{1,0:T(8,128)(2,1)S(1)}, bf16[256,128]{1,0:T(8,128)(2,1)S(1)}, u32[]{:S(2)}, u32[]{:S(2)}) collective-permute-start(bf16[256,128]{1,0:T(8,128)(2,1)S(1)} %get-tuple-element.47), channel_id=1, source_target_pairs={{0,16},{4,20},{8,24},{12,28},{16,0},{20,4},{24,8},{28,12},{1,17},{... | collective-permute-start | bytes 196616 | tf_op jit(solution)/shard_map/ppermute | solution.py:335
  35.7 11.5 %collective-permute-start.5 = (bf16[256,128]{1,0:T(8,128)(2,1)S(1)}, bf16[256,128]{1,0:T(8,128)(2,1)S(1)}, u32[]{:S(2)}, u32[]{:S(2)}) collective-permute-start(bf16[256,128]{1,0:T(8,128)(2,1)S(1)} %get-tuple-element.45), channel_id=1, source_target_pairs={{0,12},{4,8},{8,4},{12,0},{16,28},{20,24},{24,20},{28,16},{1,13},{... | collective-permute-start | bytes 196616 | tf_op jit(solution)/shard_map/ppermute | solution.py:335
  38.2 13.5 %collective-permute-start.7 = (bf16[256,128]{1,0:T(8,128)(2,1)S(1)}, bf16[256,128]{1,0:T(8,128)(2,1)S(1)}, u32[]{:S(2)}, u32[]{:S(2)}) collective-permute-start(bf16[256,128]{1,0:T(8,128)(2,1)S(1)} %get-tuple-element.49), channel_id=1, source_target_pairs={{0,20},{4,16},{8,28},{12,24},{16,4},{20,0},{24,12},{28,8},{1,21},{... | collective-permute-start | bytes 196616 | tf_op jit(solution)/shard_map/ppermute | solution.py:335
  38.5 13.2 %collective-permute-start.8 = (bf16[256,128]{1,0:T(8,128)(2,1)S(1)}, bf16[256,128]{1,0:T(8,128)(2,1)S(1)}, u32[]{:S(2)}, u32[]{:S(2)}) collective-permute-start(bf16[256,128]{1,0:T(8,128)(2,1)S(1)} %get-tuple-element.50), channel_id=1, source_target_pairs={{0,24},{4,28},{8,16},{12,20},{16,8},{20,12},{24,0},{28,4},{1,25},{... | collective-permute-start | bytes 196616 | tf_op jit(solution)/shard_map/ppermute | solution.py:335
  40.1 7.1 %copy-start.8 = (bf16[256,128]{1,0:T(8,128)(2,1)}, bf16[256,128]{1,0:T(8,128)(2,1)S(1)}, u32[]{:S(2)}) copy-start(bf16[256,128]{1,0:T(8,128)(2,1)S(1)} %collective-permute-done.3.refs_2_) | copy-start | bytes 196612
  40.1 11.6 %collective-permute-start.9 = (bf16[256,128]{1,0:T(8,128)(2,1)S(1)}, bf16[256,128]{1,0:T(8,128)(2,1)S(1)}, u32[]{:S(2)}, u32[]{:S(2)}) collective-permute-start(bf16[256,128]{1,0:T(8,128)(2,1)S(1)} %get-tuple-element.51), channel_id=1, source_target_pairs={{0,28},{4,24},{8,20},{12,16},{16,12},{20,8},{24,4},{28,0},{1,29},{... | collective-permute-start | bytes 196616 | tf_op jit(solution)/shard_map/ppermute | solution.py:335
  41.5 10.2 %collective-permute-start.4 = (bf16[256,128]{1,0:T(8,128)(2,1)S(1)}, bf16[256,128]{1,0:T(8,128)(2,1)S(1)}, u32[]{:S(2)}, u32[]{:S(2)}) collective-permute-start(bf16[256,128]{1,0:T(8,128)(2,1)S(1)} %get-tuple-element.43), channel_id=1, source_target_pairs={{0,4},{4,0},{8,12},{12,8},{16,20},{20,16},{24,28},{28,24},{1,5},{5... | collective-permute-start | bytes 196616 | tf_op jit(solution)/shard_map/ppermute | solution.py:335
  47.3 14.0 %collective-permute-start.10 = (bf16[256,512]{1,0:T(8,128)(2,1)S(1)}, bf16[256,512]{1,0:T(8,128)(2,1)S(1)}, u32[]{:S(2)}, u32[]{:S(2)}) collective-permute-start(bf16[256,512]{1,0:T(8,128)(2,1)S(1)} %get-tuple-element.56), channel_id=1, source_target_pairs={{0,16},{4,20},{8,24},{12,28},{16,0},{20,4},{24,8},{28,12},{1,17},{... | collective-permute-start | bytes 786440 | tf_op jit(solution)/shard_map/ppermute | solution.py:475
  61.3 34.0 %all-to-all-start.1 = ((bf16[8,512,128]{2,1,0:T(8,128)(2,1)}), bf16[8,512,128]{2,1,0:T(8,128)(2,1)S(1)}, u32[]{:S(2)}, u32[]{:S(2)}) async-start(bf16[8,512,128]{2,1,0:T(8,128)(2,1)} %get-tuple-element.68), calls=%async_computation.1 | async-start | bytes 2097152 | tf_op jit(solution)/shard_map/all_to_all | solution.py:767
  76.3 14.8 %collective-permute-start.11 = (bf16[4,4,64,128]{3,2,1,0:T(8,128)(2,1)}, bf16[4,4,64,128]{3,2,1,0:T(8,128)(2,1)S(1)}, u32[]{:S(2)}, u32[]{:S(2)}) collective-permute-start(bf16[4,4,64,128]{3,2,1,0:T(8,128)(2,1)} %get-tuple-element.60), channel_id=1, source_target_pairs={{0,8},{4,12},{8,0},{12,4},{16,24},{20,28},{24,16},{28,20},{1,9},{5... | collective-permute-start | bytes 786440 | tf_op jit(solution)/shard_map/ppermute | solution.py:335
  76.4 20.3 %collective-permute-start.14 = (bf16[2,4,64,128]{3,2,1,0:T(8,128)(2,1)}, bf16[2,4,64,128]{3,2,1,0:T(8,128)(2,1)S(1)}, u32[]{:S(2)}, u32[]{:S(2)}) collective-permute-start(bf16[2,4,64,128]{3,2,1,0:T(8,128)(2,1)} %get-tuple-element.64), channel_id=1, source_target_pairs={{0,16},{4,20},{8,24},{12,28},{16,0},{20,4},{24,8},{28,12},{1,17},{... | collective-permute-start | bytes 393224 | tf_op jit(solution)/shard_map/ppermute | solution.py:335
  79.3 32.5 %collective-permute-start.13 = (bf16[4,4,64,128]{3,2,1,0:T(8,128)(2,1)}, bf16[4,4,64,128]{3,2,1,0:T(8,128)(2,1)S(1)}, u32[]{:S(2)}, u32[]{:S(2)}) collective-permute-start(bf16[4,4,64,128]{3,2,1,0:T(8,128)(2,1)} %get-tuple-element.63), channel_id=1, source_target_pairs={{0,12},{4,8},{8,4},{12,0},{16,28},{20,24},{24,20},{28,16},{1,13},{... | collective-permute-start | bytes 786440 | tf_op jit(solution)/shard_map/ppermute | solution.py:335
  91.1 20.8 %collective-permute-start.12 = (bf16[4,4,64,128]{3,2,1,0:T(8,128)(2,1)}, bf16[4,4,64,128]{3,2,1,0:T(8,128)(2,1)S(1)}, u32[]{:S(2)}, u32[]{:S(2)}) collective-permute-start(bf16[4,4,64,128]{3,2,1,0:T(8,128)(2,1)} %get-tuple-element.61), channel_id=1, source_target_pairs={{0,4},{4,0},{8,12},{12,8},{16,20},{20,16},{24,28},{28,24},{1,5},{5... | collective-permute-start | bytes 786440 | tf_op jit(solution)/shard_map/ppermute | solution.py:335
  92.7 15.3 %collective-permute-start.15 = (bf16[2,4,64,128]{3,2,1,0:T(8,128)(2,1)}, bf16[2,4,64,128]{3,2,1,0:T(8,128)(2,1)S(1)}, u32[]{:S(2)}, u32[]{:S(2)}) collective-permute-start(bf16[2,4,64,128]{3,2,1,0:T(8,128)(2,1)} %get-tuple-element.65), channel_id=1, source_target_pairs={{0,20},{4,16},{8,28},{12,24},{16,4},{20,0},{24,12},{28,8},{1,21},{... | collective-permute-start | bytes 393224 | tf_op jit(solution)/shard_map/ppermute | solution.py:335
  95.3 16.6 %collective-permute-start.16 = (bf16[2,4,64,128]{3,2,1,0:T(8,128)(2,1)}, bf16[2,4,64,128]{3,2,1,0:T(8,128)(2,1)S(1)}, u32[]{:S(2)}, u32[]{:S(2)}) collective-permute-start(bf16[2,4,64,128]{3,2,1,0:T(8,128)(2,1)} %get-tuple-element.66), channel_id=1, source_target_pairs={{0,24},{4,28},{8,16},{12,20},{16,8},{20,12},{24,0},{28,4},{1,25},{... | collective-permute-start | bytes 393224 | tf_op jit(solution)/shard_map/ppermute | solution.py:335
  96.7 17.6 %collective-permute-start.17 = (bf16[2,4,64,128]{3,2,1,0:T(8,128)(2,1)}, bf16[2,4,64,128]{3,2,1,0:T(8,128)(2,1)S(1)}, u32[]{:S(2)}, u32[]{:S(2)}) collective-permute-start(bf16[2,4,64,128]{3,2,1,0:T(8,128)(2,1)} %get-tuple-element.69), channel_id=1, source_target_pairs={{0,28},{4,24},{8,20},{12,16},{16,12},{20,8},{24,4},{28,0},{1,29},{... | collective-permute-start | bytes 393224 | tf_op jit(solution)/shard_map/ppermute | solution.py:335
  (11 other events, 22.4 us)

commit v4 on v3

--- a/solution.py
+++ b/solution.py
@@ -455,7 +455,7 @@
     half = jax.ShapeDtypeStruct((s.T // 2, s.C), BF16)
     return pl.pallas_call(
         functools.partial(project_finish_kernel, s, (hop,)),
-        out_shape=[jax.ShapeDtypeStruct((s.R, LANES), BF16)] * s.B + [half, half],
+        out_shape=[pltpu.HBM((s.R, LANES), BF16)] * s.B + [pltpu.HBM(half.shape, BF16)] * 2,
         in_specs=[hbm()] * 4,
         out_specs=[hbm()] * (s.B + 2),
         scratch_shapes=project_scratch(s, 1, feats)
@@ -496,16 +496,28 @@
     return out
 
 
-def spectrum_kernel(s, xh_at, dft_at, tw_at, pre, h_at, h, dft, tw, h_spec, held, sems, out_sems):
+def spectrum_kernel(s, xh_at, dft_at, tw_at, pre, *refs):
+    h_at, x_at, codes_at, h, x, codes, dft, tw, h_spec, held, sems, out_sems = refs
     h_copy = pltpu.make_async_copy(xh_at.at[:, s.R : 2 * s.R, :], h, sems.at[0])
     dft_copy = pltpu.make_async_copy(dft_at, dft, sems.at[1])
     tables_in = tw_copies(s, tw_at, tw, sems, 2)
-    for c in [h_copy] + tables_in + [dft_copy]:
+    base = 2 + TW_PIECES
+    through = [
+        pltpu.make_async_copy(xh_at.at[:, : s.R, :], x, sems.at[base]),
+        pltpu.make_async_copy(xh_at.at[:, 2 * s.R :, :], codes, sems.at[base + 1]),
+    ]
+    stores = [
+        pltpu.make_async_copy(x, x_at, out_sems.at[s.K]),
+        pltpu.make_async_copy(codes, codes_at, out_sems.at[s.K + 1]),
+    ]
+    for c in [h_copy] + tables_in + [dft_copy] + through:
         c.start()
     h_copy.wait()
     forward_rows(s, lambda i, rows: h[i, rows, :].astype(F32), held, tw, pre, tables_in)
     dft_copy.wait()
-    stores = []
+    for came, kept in zip(through, stores):
+        came.wait()
+        kept.start()
 
     def bins(k):
         re, im = forward_bins(s, held[k], dft)
@@ -536,13 +548,17 @@
     return jnp.concatenate(hits, axis=1)
 
 
+def arrival_order(s):
+    return [*range(s.B // 2, s.B), 0, *range(2, s.B // 2), 1]
+
+
 def token_kernel(s, *refs):
     parts, refs = refs[: s.B], refs[s.B :]
-    came, h_at, skip_at, dft_at, tw_at, pre_at, y_at, out_at = refs[:8]
+    codes_at, h_at, skip_at, dft_at, tw_at, pre_at, y_at, out_at = refs[:8]
     dy, codes, h_spec, skip, dft, tw, pre, y_spec, out, held, back, tok, sems, y_sems = refs[8:]
     me = lax.axis_index("bins")
-    pairs = [(came.at[:, 2 * s.R :, :], codes), (pre_at, pre), (skip_at, skip)]
-    pairs += [(parts[x], dy.at[me ^ x]) for x in range(s.B)]
+    pairs = [(codes_at, codes), (pre_at, pre), (skip_at, skip)]
+    pairs += [(parts[n], dy.at[me ^ x]) for n, x in enumerate(arrival_order(s))]
     pairs += [(dft_at, dft), (h_at, h_spec)]
     copies = [pltpu.make_async_copy(a, b, sems.at[n]) for n, (a, b) in enumerate(pairs)]
     copies[-2:-2] = tw_copies(s, tw_at, tw, sems, len(pairs))
@@ -593,10 +609,10 @@
         c.wait()
 
 
-def products_kernel(s, xh_at, h_at, y_at, kept, g_came, skip, dft_at, tw_at, pre, *refs):
+def products_kernel(s, x_at, h_at, y_at, kept, g_came, skip, dft_at, tw_at, pre, *refs):
     outs, refs = refs[: s.B], refs[s.B :]
     x, h_spec, y_spec, dft, tw, x_spec, held, back, u, lags, sems = refs
-    x_copy = pltpu.make_async_copy(xh_at.at[:, : s.R, :], x, sems.at[0])
+    x_copy = pltpu.make_async_copy(x_at, x, sems.at[0])
     dft_copy = pltpu.make_async_copy(dft_at, dft, sems.at[1])
     h_copy = pltpu.make_async_copy(h_at, h_spec, sems.at[2])
     y_copy = pltpu.make_async_copy(y_at, y_spec, sems.at[3])
@@ -757,7 +773,7 @@
             pltpu.SemaphoreType.DMA((s.B,)),
             pltpu.SemaphoreType.DMA((2 * s.tiles,)),
         ],
-        compiler_params=params(40),
+        compiler_params=params(56),
         cost_estimate=cost(s.T * s.C * 8, s.T * s.C * 12),
         name="columns",
     )(*parts)
@@ -785,42 +801,48 @@
     core_pairs = [(c, c ^ 1) for c in range(nchan)]
     far = lax.ppermute(out_grad, "chan", [(c, c ^ across) for c in range(nchan)])
     near = lax.ppermute(out_grad, "chan", core_pairs)
-    start = project_part(s, [out_grad, near], (0, 1), out_weight)
+    start = project_part(s, [out_grad], (0,), out_weight)
     my_skip = own_skip(s, skip)
     far, start, my_skip = lax.optimization_barrier((far, start, my_skip))
     far_near = lax.ppermute(far, "chan", core_pairs)
-    start = project_part(s, [far], (across,), out_weight, (start,))
+    start = project_part(s, [near, far], (1, across), out_weight, (start,))
     *dy, away, kept = project_finish(s, far_near, across ^ 1, out_weight, start, gate)
     dy = swap_partners(s, dy, {1: 2})
 
     block = pltpu.VMEM((s.B, s.R, LANES), BF16)
     dft_held = pltpu.VMEM((2 * s.R, s.R), BF16)
-    h_spec = pl.pallas_call(
+    h_spec, x, codes = pl.pallas_call(
         functools.partial(spectrum_kernel, s),
-        out_shape=spec_shape,
+        out_shape=[
+            pltpu.HBM(spec_shape.shape, F32),
+            pltpu.HBM((s.B, s.R, LANES), BF16),
+            pltpu.HBM((s.B, TAIL, LANES), BF16),
+        ],
         in_specs=[hbm(), hbm(), hbm(), vmem()],
-        out_specs=hbm(),
+        out_specs=[hbm()] * 3,
         scratch_shapes=[
             block,
+            block,
+            pltpu.VMEM((s.B, TAIL, LANES), BF16),
             dft_held,
             back,
             back,
             held,
-            pltpu.SemaphoreType.DMA((2 + TW_PIECES,)),
-            pltpu.SemaphoreType.DMA((s.K,)),
+            pltpu.SemaphoreType.DMA((4 + TW_PIECES,)),
+            pltpu.SemaphoreType.DMA((s.K + 2,)),
         ],
-        compiler_params=params(),
+        compiler_params=params(58),
         cost_estimate=cost(10 * transform, 2 * spec_bytes),
         name="filter_spectrum",
     )(came, dft, tw, pre)
 
-    away, dy[4] = lax.optimization_barrier((away, dy[4]))
+    away, dy[s.B - 1] = lax.optimization_barrier((away, dy[s.B - 1]))
     g_came = swap_halves(s, away)
 
     outbox_shape = (s.B, s.Q * s.send, LANES)
     y_spec, outbox = pl.pallas_call(
         functools.partial(token_kernel, s),
-        out_shape=[spec_shape, jax.ShapeDtypeStruct(outbox_shape, BF16)],
+        out_shape=[pltpu.HBM(spec_shape.shape, F32), pltpu.HBM(outbox_shape, BF16)],
         in_specs=[hbm()] * (s.B + 6),
         out_specs=[hbm()] * 2,
         scratch_shapes=[
@@ -839,10 +861,10 @@
             pltpu.SemaphoreType.DMA((s.B + 5 + TW_PIECES,)),
             pltpu.SemaphoreType.DMA((s.K + s.Q,)),
         ],
-        compiler_params=params(),
+        compiler_params=params(60),
         cost_estimate=cost(20 * transform, 3 * spec_bytes),
         name="token_products",
-    )(*dy, came, h_spec, my_skip, dft, tw, pre)
+    )(*[dy[x] for x in arrival_order(s)], codes, h_spec, my_skip, dft, tw, pre)
     outbox, g_came = lax.optimization_barrier((outbox, g_came))
     inbox = exchange(outbox)
 
@@ -872,7 +894,7 @@
         compiler_params=params(),
         cost_estimate=cost(3 * transform, 4 * spec_bytes),
         name="conv_and_filter",
-    )(came, h_spec, y_spec, kept, g_came, my_skip, dft, tw, pre)
+    )(x, h_spec, y_spec, kept, g_came, my_skip, dft, tw, pre)
     grad_rows = owner_rows(s, inbox)
     *parts, last = parts
     last, grad_rows = lax.optimization_barrier((last, grad_rows))

time: 119 us -> 114 us (0.958)
  the two profiles are of different devices: /device:TPU:10 before, /device:TPU:0 now
where the time goes in v4:
time: 114 us
  starting transfers between devices  42.6 us (37%)
  Pallas kernels  37.6 us (33%)
  waiting for transfers between devices  29.1 us (26%)
  local copies, waits for them, and re-layouts  3.52 us (3%)
    ppermute x14, starting transfers between devices, swap_partners(): out[x] = lax.ppermute(part, 'bins', [(b, b ^ x) for b in range(s.B)])  23.4 us
    ppermute x14, waiting for transfers between devices, swap_partners(): out[x] = lax.ppermute(part, 'bins', [(b, b ^ x) for b in range(s.B)])  18.2 us
    ppermute x1, waiting for transfers between devices, shards(): lax.ppermute(out_grad, 'chan', [(c, c ^ across) for c in range(nchan)])  10.4 us
    pallas_call x1, Pallas kernels, shards(): pl.pallas_call(functools.partial(products_kernel, s), out_shape=[jax.Shap...  9.98 us
    all_to_all x2, starting transfers between devices, exchange(): return lax.all_to_all(v, 'bins', split_axis=0, concat_axis=0, tiled=True)  9.6 us
    pallas_call x1, Pallas kernels, shards(): pl.pallas_call(functools.partial(token_kernel, s), out_shape=[pltpu.HBM(s...  8.85 us
    ppermute x1, starting transfers between devices, swap_halves(): return lax.ppermute(away, 'bins', [(b, b ^ s.B // 2) for b in range(s.B)])  6.5 us
    pallas_call x1, Pallas kernels, shards(): pl.pallas_call(functools.partial(spectrum_kernel, s), out_shape=[pltpu.HB...  5.18 us
  transfers between devices with their start and end apart: 20, of which 6 were waited for; matrix products, arithmetic and copies ran while one was open for 0% of the time, Pallas kernels for 30%

profile of v4, /device:TPU:0, one launch (start us, length us, event | category | flops | bytes accessed | tf_op | source)
XLA Modules:
  0.0 113.9 jit_solution(12622114072720536551)
XLA Ops:
  0.6 3.0 %collective-permute-start = (bf16[512,1024]{1,0:T(8,128)(2,1)}, bf16[512,1024]{1,0:T(8,128)(2,1)S(1)}, u32[]{:S(2)}, u32[]{:S(2)}) collective-permute-start(bf16[512,1024]{1,0:T(8,128)(2,1)} %refs_0_.3), channel_id=1, source_target_pairs={{0,2},{1,3},{2,0},{3,1},{4,6},{5,7},{6,4},{7,5},{8,10},{9,11},{10,... | collective-permute-start | bytes 3145736 | tf_op jit(solution)/shard_map/ppermute | solution.py:802
  3.6 2.4 %pack_channels.1 = bf16[8,528,128]{2,1,0:T(8,128)(2,1)} custom-call(bf16[512,512]{1,0:T(8,128)(2,1)} %refs_0_.2, bf16[512,512]{1,0:T(8,128)(2,1)} %refs_1_.3, s32[8,64]{1,0:T(8,128)} %refs_2_.2, s32[8,64]{1,0:T(8,128)} %refs_3_.2), custom_call_target="tpu_custom_call" | custom-call | flops 2097152 | bytes 2097152 | tf_op jit(solution)/shard_map/pack_channels/pallas_call | solution.py:284
  6.0 5.8 %all-to-all-start = ((bf16[8,528,128]{2,1,0:T(8,128)(2,1)}), bf16[8,528,128]{2,1,0:T(8,128)(2,1)}, u32[]{:S(2)}, u32[]{:S(2)}) async-start(bf16[8,528,128]{2,1,0:T(8,128)(2,1)} %pack_channels.1), calls=%async_computation | async-start | bytes 2162688 | tf_op jit(solution)/shard_map/all_to_all | solution.py:783
  13.3 2.2 %copy-done = bf16[512,4096]{1,0:T(8,128)(2,1)S(1)} copy-done((bf16[512,4096]{1,0:T(8,128)(2,1)S(1)}, bf16[512,4096]{1,0:T(8,128)(2,1)}, u32[]{:S(2)}) %copy-start) | copy-done | bytes 4194328
  16.6 10.4 %collective-permute-done.refs_1_ = bf16[512,1024]{1,0:T(8,128)(2,1)S(1)} collective-permute-done((bf16[512,1024]{1,0:T(8,128)(2,1)}, bf16[512,1024]{1,0:T(8,128)(2,1)S(1)}, u32[]{:S(2)}, u32[]{:S(2)}) %collective-permute-start) | collective-permute-done | bytes 1048608 | tf_op jit(solution)/shard_map/ppermute | solution.py:802
  27.0 2.1 %project_part.3.refs_2_ = f32[512,512]{1,0:T(8,128)S(1)} custom-call(bf16[512,1024]{1,0:T(8,128)(2,1)S(1)} %collective-permute-done.2.refs_0_, bf16[512,1024]{1,0:T(8,128)(2,1)S(1)} %collective-permute-done.refs_1_, bf16[512,4096]{1,0:T(8,128)(2,1)S(1)} %copy-done.1, f32[512,512]{1,0:T(8,128)S(1)} %project_part.2.refs_3_), custom_call_target="tpu_custom_call" | custom-call | flops 524288 | bytes 262144 | tf_op jit(solution)/shard_map/project_part/pallas_call | solution.py:399
  29.7 2.4 %project_finish.1 = (bf16[256,128]{1,0:T(8,128)(2,1)}, bf16[256,128]{1,0:T(8,128)(2,1)}, bf16[256,128]{1,0:T(8,128)(2,1)}, bf16[256,128]{1,0:T(8,128)(2,1)}, bf1...) custom-call(bf16[512,1024]{1,0:T(8,128)(2,1)S(1)} %collective-permut, ...), custom_call_target="tpu_custom_call" | custom-call | flops 262144 | bytes 262144 | tf_op jit(solution)/shard_map/project_finish/pallas_call | solution.py:456
  32.1 1.9 %collective-permute-start.7 = (bf16[256,128]{1,0:T(8,128)(2,1)}, bf16[256,128]{1,0:T(8,128)(2,1)S(1)}, u32[]{:S(2)}, u32[]{:S(2)}) collective-permute-start(bf16[256,128]{1,0:T(8,128)(2,1)} %get-tuple-element.53), channel_id=1, source_target_pairs={{0,8},{4,12},{8,0},{12,4},{16,24},{20,28},{24,16},{28,20},{1,9},{5... | collective-permute-start | bytes 196616 | tf_op jit(solution)/shard_map/ppermute | solution.py:335
  34.0 3.4 %collective-permute-start.6 = (bf16[256,128]{1,0:T(8,128)(2,1)}, bf16[256,128]{1,0:T(8,128)(2,1)S(1)}, u32[]{:S(2)}, u32[]{:S(2)}) collective-permute-start(bf16[256,128]{1,0:T(8,128)(2,1)} %get-tuple-element.49), channel_id=1, source_target_pairs={{0,28},{4,24},{8,20},{12,16},{16,12},{20,8},{24,4},{28,0},{1,29},{... | collective-permute-start | bytes 196616 | tf_op jit(solution)/shard_map/ppermute | solution.py:335
  37.4 2.9 %collective-permute-start.4 = (bf16[256,128]{1,0:T(8,128)(2,1)}, bf16[256,128]{1,0:T(8,128)(2,1)S(1)}, u32[]{:S(2)}, u32[]{:S(2)}) collective-permute-start(bf16[256,128]{1,0:T(8,128)(2,1)} %get-tuple-element.46), channel_id=1, source_target_pairs={{0,20},{4,16},{8,28},{12,24},{16,4},{20,0},{24,12},{28,8},{1,21},{... | collective-permute-start | bytes 196616 | tf_op jit(solution)/shard_map/ppermute | solution.py:335
  43.2 5.2 %filter_spectrum.1 = (f32[9,2,256,128]{3,2,1,0:T(8,128)}, bf16[8,256,128]{2,1,0:T(8,128)(2,1)}, bf16[8,16,128]{2,1,0:T(8,128)(2,1)}) custom-call(bf16[8,528,128]{2,1,0:T(8,128)(2,1)} %all-to-all-done.xh_at, bf16[512,256]{1,0:T(8,128)(2,1)} %constant.6.clone.dft_at.refs_11_, f32[9,2,256,128]{3,2,1,0:T(8,128)} %constant.7.clone.tw_at.refs_12_, ...), custom_call_target="tpu_custom_call" | custom-call | flops 6039797760 | bytes 4718592 | tf_op jit(solution)/shard_map/filter_spectrum/pallas_call | solution.py:814
  48.5 6.5 %collective-permute-start.10 = (bf16[256,512]{1,0:T(8,128)(2,1)S(1)}, bf16[256,512]{1,0:T(8,128)(2,1)S(1)}, u32[]{:S(2)}, u32[]{:S(2)}) collective-permute-start(bf16[256,512]{1,0:T(8,128)(2,1)S(1)} %copy-done.12), channel_id=1, source_target_pairs={{0,16},{4,20},{8,24},{12,28},{16,0},{20,4},{24,8},{28,12},{1,17},{... | collective-permute-start | bytes 786440 | tf_op jit(solution)/shard_map/ppermute | solution.py:475
  55.7 8.8 %token_products.1 = (f32[9,2,256,128]{3,2,1,0:T(8,128)}, bf16[8,512,128]{2,1,0:T(8,128)(2,1)}) custom-call(bf16[256,128]{1,0:T(8,128)(2,1)} %copy-done.15, bf16[256,128]{1,0:T(8,128)(2,1)} %copy-done.16, bf16[256,128]{1,0:T(8,128)(2,1)} %copy-done.17, bf16[256,128]{1,0:T(8,128)(2,1)} %copy-done.14, bf16[256,128]{1,0:T(8,128)(2,1)} %get-tuple-element.51.refs_4_, ...), custom_call_target="tpu_custom_call" | custom-call | flops 12079595520 | bytes 7077888 | tf_op jit(solution)/shard_map/token_products/pallas_call | solution.py:843
  64.6 3.8 %all-to-all-start.1 = ((bf16[8,512,128]{2,1,0:T(8,128)(2,1)}), bf16[8,512,128]{2,1,0:T(8,128)(2,1)S(1)}, u32[]{:S(2)}, u32[]{:S(2)}) async-start(bf16[8,512,128]{2,1,0:T(8,128)(2,1)} %get-tuple-element.74), calls=%async_computation.1 | async-start | bytes 2097152 | tf_op jit(solution)/shard_map/all_to_all | solution.py:783
  68.3 10.0 %conv_and_filter.1 = (bf16[4,4,64,128]{3,2,1,0:T(8,128)(2,1)}, bf16[4,4,64,128]{3,2,1,0:T(8,128)(2,1)}, bf16[4,4,64,128]{3,2,1,0:T(8,128)(2,1)}, bf16[4,4,64,128...) custom-call(bf16[8,256,128]{2,1,0:T(8,128)(2,1)} %get-tuple-element., ...), custom_call_target="tpu_custom_call" | custom-call | flops 1811939328 | bytes 9437184 | tf_op jit(solution)/shard_map/conv_and_filter/pallas_call | solution.py:873
  78.3 1.8 %collective-permute-start.11 = (bf16[4,4,64,128]{3,2,1,0:T(8,128)(2,1)}, bf16[4,4,64,128]{3,2,1,0:T(8,128)(2,1)S(1)}, u32[]{:S(2)}, u32[]{:S(2)}) collective-permute-start(bf16[4,4,64,128]{3,2,1,0:T(8,128)(2,1)} %get-tuple-element.66), channel_id=1, source_target_pairs={{0,8},{4,12},{8,0},{12,4},{16,24},{20,28},{24,16},{28,20},{1,9},{5... | collective-permute-start | bytes 786440 | tf_op jit(solution)/shard_map/ppermute | solution.py:335
  80.1 2.4 %collective-permute-start.14 = (bf16[2,4,64,128]{3,2,1,0:T(8,128)(2,1)}, bf16[2,4,64,128]{3,2,1,0:T(8,128)(2,1)S(1)}, u32[]{:S(2)}, u32[]{:S(2)}) collective-permute-start(bf16[2,4,64,128]{3,2,1,0:T(8,128)(2,1)} %get-tuple-element.70), channel_id=1, source_target_pairs={{0,16},{4,20},{8,24},{12,28},{16,0},{20,4},{24,8},{28,12},{1,17},{... | collective-permute-start | bytes 393224 | tf_op jit(solution)/shard_map/ppermute | solution.py:335
  84.0 10.3 %collective-permute-done.11.refs_2_ = bf16[4,4,64,128]{3,2,1,0:T(8,128)(2,1)S(1)} collective-permute-done((bf16[4,4,64,128]{3,2,1,0:T(8,128)(2,1)}, bf16[4,4,64,128]{3,2,1,0:T(8,128)(2,1)S(1)}, u32[]{:S(2)}, u32[]{:S(2)}) %collective-permute-start.11) | collective-permute-done | bytes 262176 | tf_op jit(solution)/shard_map/ppermute | solution.py:335
  95.3 2.9 %collective-permute-start.15 = (bf16[2,4,64,128]{3,2,1,0:T(8,128)(2,1)}, bf16[2,4,64,128]{3,2,1,0:T(8,128)(2,1)S(1)}, u32[]{:S(2)}, u32[]{:S(2)}) collective-permute-start(bf16[2,4,64,128]{3,2,1,0:T(8,128)(2,1)} %get-tuple-element.71), channel_id=1, source_target_pairs={{0,20},{4,16},{8,28},{12,24},{16,4},{20,0},{24,12},{28,8},{1,21},{... | collective-permute-start | bytes 393224 | tf_op jit(solution)/shard_map/ppermute | solution.py:335
  99.9 2.3 %collective-permute-done.14.refs_4_ = bf16[2,4,64,128]{3,2,1,0:T(8,128)(2,1)S(1)} collective-permute-done((bf16[2,4,64,128]{3,2,1,0:T(8,128)(2,1)}, bf16[2,4,64,128]{3,2,1,0:T(8,128)(2,1)S(1)}, u32[]{:S(2)}, u32[]{:S(2)}) %collective-permute-start.14) | collective-permute-done | bytes 131104 | tf_op jit(solution)/shard_map/ppermute | solution.py:335
  102.2 2.4 %collective-permute-start.17 = (bf16[2,4,64,128]{3,2,1,0:T(8,128)(2,1)}, bf16[2,4,64,128]{3,2,1,0:T(8,128)(2,1)S(1)}, u32[]{:S(2)}, u32[]{:S(2)}) collective-permute-start(bf16[2,4,64,128]{3,2,1,0:T(8,128)(2,1)} %get-tuple-element.75), channel_id=1, source_target_pairs={{0,28},{4,24},{8,20},{12,16},{16,12},{20,8},{24,4},{28,0},{1,29},{... | collective-permute-start | bytes 393224 | tf_op jit(solution)/shard_map/ppermute | solution.py:335
  104.5 3.9 %collective-permute-done.15.refs_5_ = bf16[2,4,64,128]{3,2,1,0:T(8,128)(2,1)S(1)} collective-permute-done((bf16[2,4,64,128]{3,2,1,0:T(8,128)(2,1)}, bf16[2,4,64,128]{3,2,1,0:T(8,128)(2,1)S(1)}, u32[]{:S(2)}, u32[]{:S(2)}) %collective-permute-start.15) | collective-permute-done | bytes 131104 | tf_op jit(solution)/shard_map/ppermute | solution.py:335
  108.5 1.7 %collective-permute-done.17.refs_7_ = bf16[2,4,64,128]{3,2,1,0:T(8,128)(2,1)S(1)} collective-permute-done((bf16[2,4,64,128]{3,2,1,0:T(8,128)(2,1)}, bf16[2,4,64,128]{3,2,1,0:T(8,128)(2,1)S(1)}, u32[]{:S(2)}, u32[]{:S(2)}) %collective-permute-start.17) | collective-permute-done | bytes 131104 | tf_op jit(solution)/shard_map/ppermute | solution.py:335
  110.8 2.9 %columns.1 = (bf16[8,64,512]{2,1,0:T(8,128)(2,1)}, f32[8,64,512]{2,1,0:T(8,128)}) custom-call(bf16[4,4,64,128]{3,2,1,0:T(8,128)(2,1)} %get-tuple-element.64.refs_0_, bf16[4,4,64,128]{3,2,1,0:T(8,128)(2,1)} %copy-done.6, bf16[4,4,64,128]{3,2,1,0:T(8,128)(2,1)} %copy-done.4, bf16[4,4,64,128]{3,2,1,0:T(8,128)(2,1)} %copy-done.5, ...), custom_call_target="tpu_custom_call" | custom-call | flops 2097152 | bytes 3145728 | tf_op jit(solution)/shard_map/columns/pallas_call | solution.py:759
  (66 shorter events, 11.5 us)
Async XLA Ops:
  0.6 11.2 %copy-start.2 = (bf16[512,1024]{1,0:T(8,128)(2,1)S(1)}, bf16[512,1024]{1,0:T(8,128)(2,1)}, u32[]{:S(2)}) copy-start(bf16[512,1024]{1,0:T(8,128)(2,1)} %refs_0_.3) | copy-start | bytes 3145732
  0.6 26.4 %collective-permute-start = (bf16[512,1024]{1,0:T(8,128)(2,1)}, bf16[512,1024]{1,0:T(8,128)(2,1)S(1)}, u32[]{:S(2)}, u32[]{:S(2)}) collective-permute-start(bf16[512,1024]{1,0:T(8,128)(2,1)} %refs_0_.3), channel_id=1, source_target_pairs={{0,2},{1,3},{2,0},{3,1},{4,6},{5,7},{6,4},{7,5},{8,10},{9,11},{10,... | collective-permute-start | bytes 3145736 | tf_op jit(solution)/shard_map/ppermute | solution.py:802
  6.0 37.2 %all-to-all-start = ((bf16[8,528,128]{2,1,0:T(8,128)(2,1)}), bf16[8,528,128]{2,1,0:T(8,128)(2,1)}, u32[]{:S(2)}, u32[]{:S(2)}) async-start(bf16[8,528,128]{2,1,0:T(8,128)(2,1)} %pack_channels.1), calls=%async_computation | async-start | bytes 2162688 | tf_op jit(solution)/shard_map/all_to_all | solution.py:783
  11.9 15.1 %collective-permute-start.2 = (bf16[512,1024]{1,0:T(8,128)(2,1)S(1)}, bf16[512,1024]{1,0:T(8,128)(2,1)S(1)}, u32[]{:S(2)}, u32[]{:S(2)}) collective-permute-start(bf16[512,1024]{1,0:T(8,128)(2,1)S(1)} %copy-done.2), channel_id=1, source_target_pairs={{0,1},{1,0},{2,3},{3,2},{4,5},{5,4},{6,7},{7,6},{8,9},{9,8},{10,11... | collective-permute-start | bytes 3145736 | tf_op jit(solution)/shard_map/ppermute | solution.py:803
  15.5 11.6 %copy-start.1 = (bf16[512,4096]{1,0:T(8,128)(2,1)S(1)}, bf16[512,4096]{1,0:T(8,128)(2,1)}, u32[]{:S(2)}) copy-start(bf16[512,4096]{1,0:T(8,128)(2,1)} %refs_1_.5) | copy-start | bytes 12582916
  16.6 13.1 %copy-start.3 = (bf16[512,512]{1,0:T(8,128)(2,1)S(1)}, bf16[512,512]{1,0:T(8,128)(2,1)}, u32[]{:S(2)}) copy-start(bf16[512,512]{1,0:T(8,128)(2,1)} %refs_3_.3) | copy-start | bytes 1572868
  27.0 2.7 %collective-permute-start.1 = (bf16[512,1024]{1,0:T(8,128)(2,1)S(1)}, bf16[512,1024]{1,0:T(8,128)(2,1)S(1)}, u32[]{:S(2)}, u32[]{:S(2)}) collective-permute-start(bf16[512,1024]{1,0:T(8,128)(2,1)S(1)} %collective-permute-done.refs_1_), channel_id=1, source_target_pairs={{0,1},{1,0},{2,3},{3,2},{4,5},{5,4},{6,7},{7,6},{8,9},{9,8},{10,11... | collective-permute-start | bytes 3145736 | tf_op jit(solution)/shard_map/ppermute | solution.py:807
  32.1 9.5 %collective-permute-start.7 = (bf16[256,128]{1,0:T(8,128)(2,1)}, bf16[256,128]{1,0:T(8,128)(2,1)S(1)}, u32[]{:S(2)}, u32[]{:S(2)}) collective-permute-start(bf16[256,128]{1,0:T(8,128)(2,1)} %get-tuple-element.53), channel_id=1, source_target_pairs={{0,8},{4,12},{8,0},{12,4},{16,24},{20,28},{24,16},{28,20},{1,9},{5... | collective-permute-start | bytes 196616 | tf_op jit(solution)/shard_map/ppermute | solution.py:335
  34.0 8.0 %collective-permute-start.6 = (bf16[256,128]{1,0:T(8,128)(2,1)}, bf16[256,128]{1,0:T(8,128)(2,1)S(1)}, u32[]{:S(2)}, u32[]{:S(2)}) collective-permute-start(bf16[256,128]{1,0:T(8,128)(2,1)} %get-tuple-element.49), channel_id=1, source_target_pairs={{0,28},{4,24},{8,20},{12,16},{16,12},{20,8},{24,4},{28,0},{1,29},{... | collective-permute-start | bytes 196616 | tf_op jit(solution)/shard_map/ppermute | solution.py:335
  37.4 11.1 %collective-permute-start.3 = (bf16[256,128]{1,0:T(8,128)(2,1)}, bf16[256,128]{1,0:T(8,128)(2,1)S(1)}, u32[]{:S(2)}, u32[]{:S(2)}) collective-permute-start(bf16[256,128]{1,0:T(8,128)(2,1)} %get-tuple-element.45), channel_id=1, source_target_pairs={{0,16},{4,20},{8,24},{12,28},{16,0},{20,4},{24,8},{28,12},{1,17},{... | collective-permute-start | bytes 196616 | tf_op jit(solution)/shard_map/ppermute | solution.py:335
  37.4 17.6 %collective-permute-start.4 = (bf16[256,128]{1,0:T(8,128)(2,1)}, bf16[256,128]{1,0:T(8,128)(2,1)S(1)}, u32[]{:S(2)}, u32[]{:S(2)}) collective-permute-start(bf16[256,128]{1,0:T(8,128)(2,1)} %get-tuple-element.46), channel_id=1, source_target_pairs={{0,20},{4,16},{8,28},{12,24},{16,4},{20,0},{24,12},{28,8},{1,21},{... | collective-permute-start | bytes 196616 | tf_op jit(solution)/shard_map/ppermute | solution.py:335
  40.3 14.7 %collective-permute-start.5 = (bf16[256,128]{1,0:T(8,128)(2,1)}, bf16[256,128]{1,0:T(8,128)(2,1)S(1)}, u32[]{:S(2)}, u32[]{:S(2)}) collective-permute-start(bf16[256,128]{1,0:T(8,128)(2,1)} %get-tuple-element.47), channel_id=1, source_target_pairs={{0,24},{4,28},{8,16},{12,20},{16,8},{20,12},{24,0},{28,4},{1,25},{... | collective-permute-start | bytes 196616 | tf_op jit(solution)/shard_map/ppermute | solution.py:335
  41.6 13.4 %collective-permute-start.8 = (bf16[256,128]{1,0:T(8,128)(2,1)}, bf16[256,128]{1,0:T(8,128)(2,1)S(1)}, u32[]{:S(2)}, u32[]{:S(2)}) collective-permute-start(bf16[256,128]{1,0:T(8,128)(2,1)} %get-tuple-element.55), channel_id=1, source_target_pairs={{0,12},{4,8},{8,4},{12,0},{16,28},{20,24},{24,20},{28,16},{1,13},{... | collective-permute-start | bytes 196616 | tf_op jit(solution)/shard_map/ppermute | solution.py:335
  42.0 13.0 %collective-permute-start.9 = (bf16[256,128]{1,0:T(8,128)(2,1)}, bf16[256,128]{1,0:T(8,128)(2,1)S(1)}, u32[]{:S(2)}, u32[]{:S(2)}) collective-permute-start(bf16[256,128]{1,0:T(8,128)(2,1)} %get-tuple-element.56), channel_id=1, source_target_pairs={{0,4},{4,0},{8,12},{12,8},{16,20},{20,16},{24,28},{28,24},{1,5},{5... | collective-permute-start | bytes 196616 | tf_op jit(solution)/shard_map/ppermute | solution.py:335
  48.5 16.1 %collective-permute-start.10 = (bf16[256,512]{1,0:T(8,128)(2,1)S(1)}, bf16[256,512]{1,0:T(8,128)(2,1)S(1)}, u32[]{:S(2)}, u32[]{:S(2)}) collective-permute-start(bf16[256,512]{1,0:T(8,128)(2,1)S(1)} %copy-done.12), channel_id=1, source_target_pairs={{0,16},{4,20},{8,24},{12,28},{16,0},{20,4},{24,8},{28,12},{1,17},{... | collective-permute-start | bytes 786440 | tf_op jit(solution)/shard_map/ppermute | solution.py:475
  64.6 33.9 %all-to-all-start.1 = ((bf16[8,512,128]{2,1,0:T(8,128)(2,1)}), bf16[8,512,128]{2,1,0:T(8,128)(2,1)S(1)}, u32[]{:S(2)}, u32[]{:S(2)}) async-start(bf16[8,512,128]{2,1,0:T(8,128)(2,1)} %get-tuple-element.74), calls=%async_computation.1 | async-start | bytes 2097152 | tf_op jit(solution)/shard_map/all_to_all | solution.py:783
  78.3 15.9 %collective-permute-start.11 = (bf16[4,4,64,128]{3,2,1,0:T(8,128)(2,1)}, bf16[4,4,64,128]{3,2,1,0:T(8,128)(2,1)S(1)}, u32[]{:S(2)}, u32[]{:S(2)}) collective-permute-start(bf16[4,4,64,128]{3,2,1,0:T(8,128)(2,1)} %get-tuple-element.66), channel_id=1, source_target_pairs={{0,8},{4,12},{8,0},{12,4},{16,24},{20,28},{24,16},{28,20},{1,9},{5... | collective-permute-start | bytes 786440 | tf_op jit(solution)/shard_map/ppermute | solution.py:335
  80.1 22.1 %collective-permute-start.14 = (bf16[2,4,64,128]{3,2,1,0:T(8,128)(2,1)}, bf16[2,4,64,128]{3,2,1,0:T(8,128)(2,1)S(1)}, u32[]{:S(2)}, u32[]{:S(2)}) collective-permute-start(bf16[2,4,64,128]{3,2,1,0:T(8,128)(2,1)} %get-tuple-element.70), channel_id=1, source_target_pairs={{0,16},{4,20},{8,24},{12,28},{16,0},{20,4},{24,8},{28,12},{1,17},{... | collective-permute-start | bytes 393224 | tf_op jit(solution)/shard_map/ppermute | solution.py:335
  82.5 25.9 %collective-permute-start.13 = (bf16[4,4,64,128]{3,2,1,0:T(8,128)(2,1)}, bf16[4,4,64,128]{3,2,1,0:T(8,128)(2,1)S(1)}, u32[]{:S(2)}, u32[]{:S(2)}) collective-permute-start(bf16[4,4,64,128]{3,2,1,0:T(8,128)(2,1)} %get-tuple-element.69), channel_id=1, source_target_pairs={{0,12},{4,8},{8,4},{12,0},{16,28},{20,24},{24,20},{28,16},{1,13},{... | collective-permute-start | bytes 786440 | tf_op jit(solution)/shard_map/ppermute | solution.py:335
  94.3 15.9 %copy-start.4 = (bf16[4,4,64,128]{3,2,1,0:T(8,128)(2,1)}, bf16[4,4,64,128]{3,2,1,0:T(8,128)(2,1)S(1)}, u32[]{:S(2)}) copy-start(bf16[4,4,64,128]{3,2,1,0:T(8,128)(2,1)S(1)} %collective-permute-done.11.refs_2_) | copy-start | bytes 786436
  94.3 14.2 %collective-permute-start.12 = (bf16[4,4,64,128]{3,2,1,0:T(8,128)(2,1)}, bf16[4,4,64,128]{3,2,1,0:T(8,128)(2,1)S(1)}, u32[]{:S(2)}, u32[]{:S(2)}) collective-permute-start(bf16[4,4,64,128]{3,2,1,0:T(8,128)(2,1)} %get-tuple-element.67), channel_id=1, source_target_pairs={{0,4},{4,0},{8,12},{12,8},{16,20},{20,16},{24,28},{28,24},{1,5},{5... | collective-permute-start | bytes 786440 | tf_op jit(solution)/shard_map/ppermute | solution.py:335
  95.3 13.1 %collective-permute-start.15 = (bf16[2,4,64,128]{3,2,1,0:T(8,128)(2,1)}, bf16[2,4,64,128]{3,2,1,0:T(8,128)(2,1)S(1)}, u32[]{:S(2)}, u32[]{:S(2)}) collective-permute-start(bf16[2,4,64,128]{3,2,1,0:T(8,128)(2,1)} %get-tuple-element.71), channel_id=1, source_target_pairs={{0,20},{4,16},{8,28},{12,24},{16,4},{20,0},{24,12},{28,8},{1,21},{... | collective-permute-start | bytes 393224 | tf_op jit(solution)/shard_map/ppermute | solution.py:335
  98.2 10.2 %collective-permute-start.16 = (bf16[2,4,64,128]{3,2,1,0:T(8,128)(2,1)}, bf16[2,4,64,128]{3,2,1,0:T(8,128)(2,1)S(1)}, u32[]{:S(2)}, u32[]{:S(2)}) collective-permute-start(bf16[2,4,64,128]{3,2,1,0:T(8,128)(2,1)} %get-tuple-element.72), channel_id=1, source_target_pairs={{0,24},{4,28},{8,16},{12,20},{16,8},{20,12},{24,0},{28,4},{1,25},{... | collective-permute-start | bytes 393224 | tf_op jit(solution)/shard_map/ppermute | solution.py:335
  102.2 8.0 %collective-permute-start.17 = (bf16[2,4,64,128]{3,2,1,0:T(8,128)(2,1)}, bf16[2,4,64,128]{3,2,1,0:T(8,128)(2,1)S(1)}, u32[]{:S(2)}, u32[]{:S(2)}) collective-permute-start(bf16[2,4,64,128]{3,2,1,0:T(8,128)(2,1)} %get-tuple-element.75), channel_id=1, source_target_pairs={{0,28},{4,24},{8,20},{12,16},{16,12},{20,8},{24,4},{28,0},{1,29},{... | collective-permute-start | bytes 393224 | tf_op jit(solution)/shard_map/ppermute | solution.py:335
  (16 other events, 50.5 us)

commit v5 on v4

--- a/solution.py
+++ b/solution.py
@@ -797,16 +797,18 @@
     packed = pack(s, owner, slot, tokens_in, filters)
     came = exchange(packed)
 
-    across = nchan // 2
     core_pairs = [(c, c ^ 1) for c in range(nchan)]
-    far = lax.ppermute(out_grad, "chan", [(c, c ^ across) for c in range(nchan)])
+    hops = list(range(2, nchan, 2))
+    far = [lax.ppermute(out_grad, "chan", [(c, c ^ h) for c in range(nchan)]) for h in hops]
     near = lax.ppermute(out_grad, "chan", core_pairs)
     start = project_part(s, [out_grad], (0,), out_weight)
     my_skip = own_skip(s, skip)
-    far, start, my_skip = lax.optimization_barrier((far, start, my_skip))
-    far_near = lax.ppermute(far, "chan", core_pairs)
-    start = project_part(s, [near, far], (1, across), out_weight, (start,))
-    *dy, away, kept = project_finish(s, far_near, across ^ 1, out_weight, start, gate)
+    *far, start, my_skip = lax.optimization_barrier((*far, start, my_skip))
+    far_near = [lax.ppermute(v, "chan", core_pairs) for v in far]
+    start = project_part(s, [near, *far], (1, *hops), out_weight, (start,))
+    for v, h in zip(far_near[:-1], hops[:-1]):
+        start = project_part(s, [v], (h ^ 1,), out_weight, (start,))
+    *dy, away, kept = project_finish(s, far_near[-1], hops[-1] ^ 1, out_weight, start, gate)
     dy = swap_partners(s, dy, {1: 2})
 
     block = pltpu.VMEM((s.B, s.R, LANES), BF16)

time: 114 us -> 114 us (level)
  no operation moved by 1% of the time
where the time goes in v5:
time: 114 us
  starting transfers between devices  42.6 us (37%)
  Pallas kernels  37.6 us (33%)
  waiting for transfers between devices  29.1 us (26%)
  local copies, waits for them, and re-layouts  3.52 us (3%)
    ppermute x14, starting transfers between devices, swap_partners(): out[x] = lax.ppermute(part, 'bins', [(b, b ^ x) for b in range(s.B)])  23.4 us
    ppermute x14, waiting for transfers between devices, swap_partners(): out[x] = lax.ppermute(part, 'bins', [(b, b ^ x) for b in range(s.B)])  18.2 us
    ppermute x1, waiting for transfers between devices, shards(): lax.ppermute(out_grad, 'chan', [(c, c ^ h) for c in range(nchan)])  10.4 us
    pallas_call x1, Pallas kernels, shards(): pl.pallas_call(functools.partial(products_kernel, s), out_shape=[jax.Shap...  9.98 us
    all_to_all x2, starting transfers between devices, exchange(): return lax.all_to_all(v, 'bins', split_axis=0, concat_axis=0, tiled=True)  9.6 us
    pallas_call x1, Pallas kernels, shards(): pl.pallas_call(functools.partial(token_kernel, s), out_shape=[pltpu.HBM(s...  8.85 us
    ppermute x1, starting transfers between devices, swap_halves(): return lax.ppermute(away, 'bins', [(b, b ^ s.B // 2) for b in range(s.B)])  6.5 us
    pallas_call x1, Pallas kernels, shards(): pl.pallas_call(functools.partial(spectrum_kernel, s), out_shape=[pltpu.HB...  5.18 us
  transfers between devices with their start and end apart: 20, of which 6 were waited for; matrix products, arithmetic and copies ran while one was open for 0% of the time, Pallas kernels for 30%

profile of v5, /device:TPU:0, one launch (start us, length us, event | category | flops | bytes accessed | tf_op | source)
XLA Modules:
  0.0 113.9 jit_solution(12622114072720536551)
XLA Ops:
  0.6 3.0 %collective-permute-start = (bf16[512,1024]{1,0:T(8,128)(2,1)}, bf16[512,1024]{1,0:T(8,128)(2,1)S(1)}, u32[]{:S(2)}, u32[]{:S(2)}) collective-permute-start(bf16[512,1024]{1,0:T(8,128)(2,1)} %refs_0_.3), channel_id=1, source_target_pairs={{0,2},{1,3},{2,0},{3,1},{4,6},{5,7},{6,4},{7,5},{8,10},{9,11},{10,... | collective-permute-start | bytes 3145736 | tf_op jit(solution)/shard_map/ppermute | solution.py:802
  3.6 2.4 %pack_channels.1 = bf16[8,528,128]{2,1,0:T(8,128)(2,1)} custom-call(bf16[512,512]{1,0:T(8,128)(2,1)} %refs_0_.2, bf16[512,512]{1,0:T(8,128)(2,1)} %refs_1_.3, s32[8,64]{1,0:T(8,128)} %refs_2_.2, s32[8,64]{1,0:T(8,128)} %refs_3_.2), custom_call_target="tpu_custom_call" | custom-call | flops 2097152 | bytes 2097152 | tf_op jit(solution)/shard_map/pack_channels/pallas_call | solution.py:284
  6.0 5.8 %all-to-all-start = ((bf16[8,528,128]{2,1,0:T(8,128)(2,1)}), bf16[8,528,128]{2,1,0:T(8,128)(2,1)}, u32[]{:S(2)}, u32[]{:S(2)}) async-start(bf16[8,528,128]{2,1,0:T(8,128)(2,1)} %pack_channels.1), calls=%async_computation | async-start | bytes 2162688 | tf_op jit(solution)/shard_map/all_to_all | solution.py:783
  13.3 2.2 %copy-done = bf16[512,4096]{1,0:T(8,128)(2,1)S(1)} copy-done((bf16[512,4096]{1,0:T(8,128)(2,1)S(1)}, bf16[512,4096]{1,0:T(8,128)(2,1)}, u32[]{:S(2)}) %copy-start) | copy-done | bytes 4194328
  16.6 10.4 %collective-permute-done.refs_1_ = bf16[512,1024]{1,0:T(8,128)(2,1)S(1)} collective-permute-done((bf16[512,1024]{1,0:T(8,128)(2,1)}, bf16[512,1024]{1,0:T(8,128)(2,1)S(1)}, u32[]{:S(2)}, u32[]{:S(2)}) %collective-permute-start) | collective-permute-done | bytes 1048608 | tf_op jit(solution)/shard_map/ppermute | solution.py:802
  27.0 2.1 %project_part.3.refs_2_ = f32[512,512]{1,0:T(8,128)S(1)} custom-call(bf16[512,1024]{1,0:T(8,128)(2,1)S(1)} %collective-permute-done.2.refs_0_, bf16[512,1024]{1,0:T(8,128)(2,1)S(1)} %collective-permute-done.refs_1_, bf16[512,4096]{1,0:T(8,128)(2,1)S(1)} %copy-done.1, f32[512,512]{1,0:T(8,128)S(1)} %project_part.2.refs_3_), custom_call_target="tpu_custom_call" | custom-call | flops 524288 | bytes 262144 | tf_op jit(solution)/shard_map/project_part/pallas_call | solution.py:399
  29.7 2.4 %project_finish.1 = (bf16[256,128]{1,0:T(8,128)(2,1)}, bf16[256,128]{1,0:T(8,128)(2,1)}, bf16[256,128]{1,0:T(8,128)(2,1)}, bf16[256,128]{1,0:T(8,128)(2,1)}, bf1...) custom-call(bf16[512,1024]{1,0:T(8,128)(2,1)S(1)} %collective-permut, ...), custom_call_target="tpu_custom_call" | custom-call | flops 262144 | bytes 262144 | tf_op jit(solution)/shard_map/project_finish/pallas_call | solution.py:456
  32.1 1.9 %collective-permute-start.7 = (bf16[256,128]{1,0:T(8,128)(2,1)}, bf16[256,128]{1,0:T(8,128)(2,1)S(1)}, u32[]{:S(2)}, u32[]{:S(2)}) collective-permute-start(bf16[256,128]{1,0:T(8,128)(2,1)} %get-tuple-element.53), channel_id=1, source_target_pairs={{0,8},{4,12},{8,0},{12,4},{16,24},{20,28},{24,16},{28,20},{1,9},{5... | collective-permute-start | bytes 196616 | tf_op jit(solution)/shard_map/ppermute | solution.py:335
  34.0 3.4 %collective-permute-start.6 = (bf16[256,128]{1,0:T(8,128)(2,1)}, bf16[256,128]{1,0:T(8,128)(2,1)S(1)}, u32[]{:S(2)}, u32[]{:S(2)}) collective-permute-start(bf16[256,128]{1,0:T(8,128)(2,1)} %get-tuple-element.49), channel_id=1, source_target_pairs={{0,28},{4,24},{8,20},{12,16},{16,12},{20,8},{24,4},{28,0},{1,29},{... | collective-permute-start | bytes 196616 | tf_op jit(solution)/shard_map/ppermute | solution.py:335
  37.4 2.9 %collective-permute-start.4 = (bf16[256,128]{1,0:T(8,128)(2,1)}, bf16[256,128]{1,0:T(8,128)(2,1)S(1)}, u32[]{:S(2)}, u32[]{:S(2)}) collective-permute-start(bf16[256,128]{1,0:T(8,128)(2,1)} %get-tuple-element.46), channel_id=1, source_target_pairs={{0,20},{4,16},{8,28},{12,24},{16,4},{20,0},{24,12},{28,8},{1,21},{... | collective-permute-start | bytes 196616 | tf_op jit(solution)/shard_map/ppermute | solution.py:335
  43.2 5.2 %filter_spectrum.1 = (f32[9,2,256,128]{3,2,1,0:T(8,128)}, bf16[8,256,128]{2,1,0:T(8,128)(2,1)}, bf16[8,16,128]{2,1,0:T(8,128)(2,1)}) custom-call(bf16[8,528,128]{2,1,0:T(8,128)(2,1)} %all-to-all-done.xh_at, bf16[512,256]{1,0:T(8,128)(2,1)} %constant.6.clone.dft_at.refs_11_, f32[9,2,256,128]{3,2,1,0:T(8,128)} %constant.7.clone.tw_at.refs_12_, ...), custom_call_target="tpu_custom_call" | custom-call | flops 6039797760 | bytes 4718592 | tf_op jit(solution)/shard_map/filter_spectrum/pallas_call | solution.py:816
  48.5 6.5 %collective-permute-start.10 = (bf16[256,512]{1,0:T(8,128)(2,1)S(1)}, bf16[256,512]{1,0:T(8,128)(2,1)S(1)}, u32[]{:S(2)}, u32[]{:S(2)}) collective-permute-start(bf16[256,512]{1,0:T(8,128)(2,1)S(1)} %copy-done.12), channel_id=1, source_target_pairs={{0,16},{4,20},{8,24},{12,28},{16,0},{20,4},{24,8},{28,12},{1,17},{... | collective-permute-start | bytes 786440 | tf_op jit(solution)/shard_map/ppermute | solution.py:475
  55.7 8.8 %token_products.1 = (f32[9,2,256,128]{3,2,1,0:T(8,128)}, bf16[8,512,128]{2,1,0:T(8,128)(2,1)}) custom-call(bf16[256,128]{1,0:T(8,128)(2,1)} %copy-done.15, bf16[256,128]{1,0:T(8,128)(2,1)} %copy-done.16, bf16[256,128]{1,0:T(8,128)(2,1)} %copy-done.17, bf16[256,128]{1,0:T(8,128)(2,1)} %copy-done.14, bf16[256,128]{1,0:T(8,128)(2,1)} %get-tuple-element.51.refs_4_, ...), custom_call_target="tpu_custom_call" | custom-call | flops 12079595520 | bytes 7077888 | tf_op jit(solution)/shard_map/token_products/pallas_call | solution.py:845
  64.6 3.8 %all-to-all-start.1 = ((bf16[8,512,128]{2,1,0:T(8,128)(2,1)}), bf16[8,512,128]{2,1,0:T(8,128)(2,1)S(1)}, u32[]{:S(2)}, u32[]{:S(2)}) async-start(bf16[8,512,128]{2,1,0:T(8,128)(2,1)} %get-tuple-element.74), calls=%async_computation.1 | async-start | bytes 2097152 | tf_op jit(solution)/shard_map/all_to_all | solution.py:783
  68.3 10.0 %conv_and_filter.1 = (bf16[4,4,64,128]{3,2,1,0:T(8,128)(2,1)}, bf16[4,4,64,128]{3,2,1,0:T(8,128)(2,1)}, bf16[4,4,64,128]{3,2,1,0:T(8,128)(2,1)}, bf16[4,4,64,128...) custom-call(bf16[8,256,128]{2,1,0:T(8,128)(2,1)} %get-tuple-element., ...), custom_call_target="tpu_custom_call" | custom-call | flops 1811939328 | bytes 9437184 | tf_op jit(solution)/shard_map/conv_and_filter/pallas_call | solution.py:875
  78.3 1.8 %collective-permute-start.11 = (bf16[4,4,64,128]{3,2,1,0:T(8,128)(2,1)}, bf16[4,4,64,128]{3,2,1,0:T(8,128)(2,1)S(1)}, u32[]{:S(2)}, u32[]{:S(2)}) collective-permute-start(bf16[4,4,64,128]{3,2,1,0:T(8,128)(2,1)} %get-tuple-element.66), channel_id=1, source_target_pairs={{0,8},{4,12},{8,0},{12,4},{16,24},{20,28},{24,16},{28,20},{1,9},{5... | collective-permute-start | bytes 786440 | tf_op jit(solution)/shard_map/ppermute | solution.py:335
  80.1 2.4 %collective-permute-start.14 = (bf16[2,4,64,128]{3,2,1,0:T(8,128)(2,1)}, bf16[2,4,64,128]{3,2,1,0:T(8,128)(2,1)S(1)}, u32[]{:S(2)}, u32[]{:S(2)}) collective-permute-start(bf16[2,4,64,128]{3,2,1,0:T(8,128)(2,1)} %get-tuple-element.70), channel_id=1, source_target_pairs={{0,16},{4,20},{8,24},{12,28},{16,0},{20,4},{24,8},{28,12},{1,17},{... | collective-permute-start | bytes 393224 | tf_op jit(solution)/shard_map/ppermute | solution.py:335
  84.0 10.3 %collective-permute-done.11.refs_2_ = bf16[4,4,64,128]{3,2,1,0:T(8,128)(2,1)S(1)} collective-permute-done((bf16[4,4,64,128]{3,2,1,0:T(8,128)(2,1)}, bf16[4,4,64,128]{3,2,1,0:T(8,128)(2,1)S(1)}, u32[]{:S(2)}, u32[]{:S(2)}) %collective-permute-start.11) | collective-permute-done | bytes 262176 | tf_op jit(solution)/shard_map/ppermute | solution.py:335
  95.3 2.9 %collective-permute-start.15 = (bf16[2,4,64,128]{3,2,1,0:T(8,128)(2,1)}, bf16[2,4,64,128]{3,2,1,0:T(8,128)(2,1)S(1)}, u32[]{:S(2)}, u32[]{:S(2)}) collective-permute-start(bf16[2,4,64,128]{3,2,1,0:T(8,128)(2,1)} %get-tuple-element.71), channel_id=1, source_target_pairs={{0,20},{4,16},{8,28},{12,24},{16,4},{20,0},{24,12},{28,8},{1,21},{... | collective-permute-start | bytes 393224 | tf_op jit(solution)/shard_map/ppermute | solution.py:335
  99.9 2.3 %collective-permute-done.14.refs_4_ = bf16[2,4,64,128]{3,2,1,0:T(8,128)(2,1)S(1)} collective-permute-done((bf16[2,4,64,128]{3,2,1,0:T(8,128)(2,1)}, bf16[2,4,64,128]{3,2,1,0:T(8,128)(2,1)S(1)}, u32[]{:S(2)}, u32[]{:S(2)}) %collective-permute-start.14) | collective-permute-done | bytes 131104 | tf_op jit(solution)/shard_map/ppermute | solution.py:335
  102.2 2.4 %collective-permute-start.17 = (bf16[2,4,64,128]{3,2,1,0:T(8,128)(2,1)}, bf16[2,4,64,128]{3,2,1,0:T(8,128)(2,1)S(1)}, u32[]{:S(2)}, u32[]{:S(2)}) collective-permute-start(bf16[2,4,64,128]{3,2,1,0:T(8,128)(2,1)} %get-tuple-element.75), channel_id=1, source_target_pairs={{0,28},{4,24},{8,20},{12,16},{16,12},{20,8},{24,4},{28,0},{1,29},{... | collective-permute-start | bytes 393224 | tf_op jit(solution)/shard_map/ppermute | solution.py:335
  104.5 3.9 %collective-permute-done.15.refs_5_ = bf16[2,4,64,128]{3,2,1,0:T(8,128)(2,1)S(1)} collective-permute-done((bf16[2,4,64,128]{3,2,1,0:T(8,128)(2,1)}, bf16[2,4,64,128]{3,2,1,0:T(8,128)(2,1)S(1)}, u32[]{:S(2)}, u32[]{:S(2)}) %collective-permute-start.15) | collective-permute-done | bytes 131104 | tf_op jit(solution)/shard_map/ppermute | solution.py:335
  108.5 1.7 %collective-permute-done.17.refs_7_ = bf16[2,4,64,128]{3,2,1,0:T(8,128)(2,1)S(1)} collective-permute-done((bf16[2,4,64,128]{3,2,1,0:T(8,128)(2,1)}, bf16[2,4,64,128]{3,2,1,0:T(8,128)(2,1)S(1)}, u32[]{:S(2)}, u32[]{:S(2)}) %collective-permute-start.17) | collective-permute-done | bytes 131104 | tf_op jit(solution)/shard_map/ppermute | solution.py:335
  110.8 2.9 %columns.1 = (bf16[8,64,512]{2,1,0:T(8,128)(2,1)}, f32[8,64,512]{2,1,0:T(8,128)}) custom-call(bf16[4,4,64,128]{3,2,1,0:T(8,128)(2,1)} %get-tuple-element.64.refs_0_, bf16[4,4,64,128]{3,2,1,0:T(8,128)(2,1)} %copy-done.6, bf16[4,4,64,128]{3,2,1,0:T(8,128)(2,1)} %copy-done.4, bf16[4,4,64,128]{3,2,1,0:T(8,128)(2,1)} %copy-done.5, ...), custom_call_target="tpu_custom_call" | custom-call | flops 2097152 | bytes 3145728 | tf_op jit(solution)/shard_map/columns/pallas_call | solution.py:759
  (66 shorter events, 11.5 us)
Async XLA Ops:
  0.6 11.2 %copy-start.2 = (bf16[512,1024]{1,0:T(8,128)(2,1)S(1)}, bf16[512,1024]{1,0:T(8,128)(2,1)}, u32[]{:S(2)}) copy-start(bf16[512,1024]{1,0:T(8,128)(2,1)} %refs_0_.3) | copy-start | bytes 3145732
  0.6 26.4 %collective-permute-start = (bf16[512,1024]{1,0:T(8,128)(2,1)}, bf16[512,1024]{1,0:T(8,128)(2,1)S(1)}, u32[]{:S(2)}, u32[]{:S(2)}) collective-permute-start(bf16[512,1024]{1,0:T(8,128)(2,1)} %refs_0_.3), channel_id=1, source_target_pairs={{0,2},{1,3},{2,0},{3,1},{4,6},{5,7},{6,4},{7,5},{8,10},{9,11},{10,... | collective-permute-start | bytes 3145736 | tf_op jit(solution)/shard_map/ppermute | solution.py:802
  6.0 37.2 %all-to-all-start = ((bf16[8,528,128]{2,1,0:T(8,128)(2,1)}), bf16[8,528,128]{2,1,0:T(8,128)(2,1)}, u32[]{:S(2)}, u32[]{:S(2)}) async-start(bf16[8,528,128]{2,1,0:T(8,128)(2,1)} %pack_channels.1), calls=%async_computation | async-start | bytes 2162688 | tf_op jit(solution)/shard_map/all_to_all | solution.py:783
  11.9 15.1 %collective-permute-start.2 = (bf16[512,1024]{1,0:T(8,128)(2,1)S(1)}, bf16[512,1024]{1,0:T(8,128)(2,1)S(1)}, u32[]{:S(2)}, u32[]{:S(2)}) collective-permute-start(bf16[512,1024]{1,0:T(8,128)(2,1)S(1)} %copy-done.2), channel_id=1, source_target_pairs={{0,1},{1,0},{2,3},{3,2},{4,5},{5,4},{6,7},{7,6},{8,9},{9,8},{10,11... | collective-permute-start | bytes 3145736 | tf_op jit(solution)/shard_map/ppermute | solution.py:803
  15.5 11.6 %copy-start.1 = (bf16[512,4096]{1,0:T(8,128)(2,1)S(1)}, bf16[512,4096]{1,0:T(8,128)(2,1)}, u32[]{:S(2)}) copy-start(bf16[512,4096]{1,0:T(8,128)(2,1)} %refs_1_.5) | copy-start | bytes 12582916
  16.6 13.1 %copy-start.3 = (bf16[512,512]{1,0:T(8,128)(2,1)S(1)}, bf16[512,512]{1,0:T(8,128)(2,1)}, u32[]{:S(2)}) copy-start(bf16[512,512]{1,0:T(8,128)(2,1)} %refs_3_.3) | copy-start | bytes 1572868
  27.0 2.7 %collective-permute-start.1 = (bf16[512,1024]{1,0:T(8,128)(2,1)S(1)}, bf16[512,1024]{1,0:T(8,128)(2,1)S(1)}, u32[]{:S(2)}, u32[]{:S(2)}) collective-permute-start(bf16[512,1024]{1,0:T(8,128)(2,1)S(1)} %collective-permute-done.refs_1_), channel_id=1, source_target_pairs={{0,1},{1,0},{2,3},{3,2},{4,5},{5,4},{6,7},{7,6},{8,9},{9,8},{10,11... | collective-permute-start | bytes 3145736 | tf_op jit(solution)/shard_map/ppermute | solution.py:807
  32.1 9.5 %collective-permute-start.7 = (bf16[256,128]{1,0:T(8,128)(2,1)}, bf16[256,128]{1,0:T(8,128)(2,1)S(1)}, u32[]{:S(2)}, u32[]{:S(2)}) collective-permute-start(bf16[256,128]{1,0:T(8,128)(2,1)} %get-tuple-element.53), channel_id=1, source_target_pairs={{0,8},{4,12},{8,0},{12,4},{16,24},{20,28},{24,16},{28,20},{1,9},{5... | collective-permute-start | bytes 196616 | tf_op jit(solution)/shard_map/ppermute | solution.py:335
  34.0 8.0 %collective-permute-start.6 = (bf16[256,128]{1,0:T(8,128)(2,1)}, bf16[256,128]{1,0:T(8,128)(2,1)S(1)}, u32[]{:S(2)}, u32[]{:S(2)}) collective-permute-start(bf16[256,128]{1,0:T(8,128)(2,1)} %get-tuple-element.49), channel_id=1, source_target_pairs={{0,28},{4,24},{8,20},{12,16},{16,12},{20,8},{24,4},{28,0},{1,29},{... | collective-permute-start | bytes 196616 | tf_op jit(solution)/shard_map/ppermute | solution.py:335
  37.4 11.1 %collective-permute-start.3 = (bf16[256,128]{1,0:T(8,128)(2,1)}, bf16[256,128]{1,0:T(8,128)(2,1)S(1)}, u32[]{:S(2)}, u32[]{:S(2)}) collective-permute-start(bf16[256,128]{1,0:T(8,128)(2,1)} %get-tuple-element.45), channel_id=1, source_target_pairs={{0,16},{4,20},{8,24},{12,28},{16,0},{20,4},{24,8},{28,12},{1,17},{... | collective-permute-start | bytes 196616 | tf_op jit(solution)/shard_map/ppermute | solution.py:335
  37.4 17.6 %collective-permute-start.4 = (bf16[256,128]{1,0:T(8,128)(2,1)}, bf16[256,128]{1,0:T(8,128)(2,1)S(1)}, u32[]{:S(2)}, u32[]{:S(2)}) collective-permute-start(bf16[256,128]{1,0:T(8,128)(2,1)} %get-tuple-element.46), channel_id=1, source_target_pairs={{0,20},{4,16},{8,28},{12,24},{16,4},{20,0},{24,12},{28,8},{1,21},{... | collective-permute-start | bytes 196616 | tf_op jit(solution)/shard_map/ppermute | solution.py:335
  40.3 14.7 %collective-permute-start.5 = (bf16[256,128]{1,0:T(8,128)(2,1)}, bf16[256,128]{1,0:T(8,128)(2,1)S(1)}, u32[]{:S(2)}, u32[]{:S(2)}) collective-permute-start(bf16[256,128]{1,0:T(8,128)(2,1)} %get-tuple-element.47), channel_id=1, source_target_pairs={{0,24},{4,28},{8,16},{12,20},{16,8},{20,12},{24,0},{28,4},{1,25},{... | collective-permute-start | bytes 196616 | tf_op jit(solution)/shard_map/ppermute | solution.py:335
  41.6 13.4 %collective-permute-start.8 = (bf16[256,128]{1,0:T(8,128)(2,1)}, bf16[256,128]{1,0:T(8,128)(2,1)S(1)}, u32[]{:S(2)}, u32[]{:S(2)}) collective-permute-start(bf16[256,128]{1,0:T(8,128)(2,1)} %get-tuple-element.55), channel_id=1, source_target_pairs={{0,12},{4,8},{8,4},{12,0},{16,28},{20,24},{24,20},{28,16},{1,13},{... | collective-permute-start | bytes 196616 | tf_op jit(solution)/shard_map/ppermute | solution.py:335
  42.0 13.0 %collective-permute-start.9 = (bf16[256,128]{1,0:T(8,128)(2,1)}, bf16[256,128]{1,0:T(8,128)(2,1)S(1)}, u32[]{:S(2)}, u32[]{:S(2)}) collective-permute-start(bf16[256,128]{1,0:T(8,128)(2,1)} %get-tuple-element.56), channel_id=1, source_target_pairs={{0,4},{4,0},{8,12},{12,8},{16,20},{20,16},{24,28},{28,24},{1,5},{5... | collective-permute-start | bytes 196616 | tf_op jit(solution)/shard_map/ppermute | solution.py:335
  48.5 16.1 %collective-permute-start.10 = (bf16[256,512]{1,0:T(8,128)(2,1)S(1)}, bf16[256,512]{1,0:T(8,128)(2,1)S(1)}, u32[]{:S(2)}, u32[]{:S(2)}) collective-permute-start(bf16[256,512]{1,0:T(8,128)(2,1)S(1)} %copy-done.12), channel_id=1, source_target_pairs={{0,16},{4,20},{8,24},{12,28},{16,0},{20,4},{24,8},{28,12},{1,17},{... | collective-permute-start | bytes 786440 | tf_op jit(solution)/shard_map/ppermute | solution.py:475
  64.6 33.9 %all-to-all-start.1 = ((bf16[8,512,128]{2,1,0:T(8,128)(2,1)}), bf16[8,512,128]{2,1,0:T(8,128)(2,1)S(1)}, u32[]{:S(2)}, u32[]{:S(2)}) async-start(bf16[8,512,128]{2,1,0:T(8,128)(2,1)} %get-tuple-element.74), calls=%async_computation.1 | async-start | bytes 2097152 | tf_op jit(solution)/shard_map/all_to_all | solution.py:783
  78.3 15.9 %collective-permute-start.11 = (bf16[4,4,64,128]{3,2,1,0:T(8,128)(2,1)}, bf16[4,4,64,128]{3,2,1,0:T(8,128)(2,1)S(1)}, u32[]{:S(2)}, u32[]{:S(2)}) collective-permute-start(bf16[4,4,64,128]{3,2,1,0:T(8,128)(2,1)} %get-tuple-element.66), channel_id=1, source_target_pairs={{0,8},{4,12},{8,0},{12,4},{16,24},{20,28},{24,16},{28,20},{1,9},{5... | collective-permute-start | bytes 786440 | tf_op jit(solution)/shard_map/ppermute | solution.py:335
  80.1 22.1 %collective-permute-start.14 = (bf16[2,4,64,128]{3,2,1,0:T(8,128)(2,1)}, bf16[2,4,64,128]{3,2,1,0:T(8,128)(2,1)S(1)}, u32[]{:S(2)}, u32[]{:S(2)}) collective-permute-start(bf16[2,4,64,128]{3,2,1,0:T(8,128)(2,1)} %get-tuple-element.70), channel_id=1, source_target_pairs={{0,16},{4,20},{8,24},{12,28},{16,0},{20,4},{24,8},{28,12},{1,17},{... | collective-permute-start | bytes 393224 | tf_op jit(solution)/shard_map/ppermute | solution.py:335
  82.5 25.9 %collective-permute-start.13 = (bf16[4,4,64,128]{3,2,1,0:T(8,128)(2,1)}, bf16[4,4,64,128]{3,2,1,0:T(8,128)(2,1)S(1)}, u32[]{:S(2)}, u32[]{:S(2)}) collective-permute-start(bf16[4,4,64,128]{3,2,1,0:T(8,128)(2,1)} %get-tuple-element.69), channel_id=1, source_target_pairs={{0,12},{4,8},{8,4},{12,0},{16,28},{20,24},{24,20},{28,16},{1,13},{... | collective-permute-start | bytes 786440 | tf_op jit(solution)/shard_map/ppermute | solution.py:335
  94.3 15.9 %copy-start.4 = (bf16[4,4,64,128]{3,2,1,0:T(8,128)(2,1)}, bf16[4,4,64,128]{3,2,1,0:T(8,128)(2,1)S(1)}, u32[]{:S(2)}) copy-start(bf16[4,4,64,128]{3,2,1,0:T(8,128)(2,1)S(1)} %collective-permute-done.11.refs_2_) | copy-start | bytes 786436
  94.3 14.2 %collective-permute-start.12 = (bf16[4,4,64,128]{3,2,1,0:T(8,128)(2,1)}, bf16[4,4,64,128]{3,2,1,0:T(8,128)(2,1)S(1)}, u32[]{:S(2)}, u32[]{:S(2)}) collective-permute-start(bf16[4,4,64,128]{3,2,1,0:T(8,128)(2,1)} %get-tuple-element.67), channel_id=1, source_target_pairs={{0,4},{4,0},{8,12},{12,8},{16,20},{20,16},{24,28},{28,24},{1,5},{5... | collective-permute-start | bytes 786440 | tf_op jit(solution)/shard_map/ppermute | solution.py:335
  95.3 13.1 %collective-permute-start.15 = (bf16[2,4,64,128]{3,2,1,0:T(8,128)(2,1)}, bf16[2,4,64,128]{3,2,1,0:T(8,128)(2,1)S(1)}, u32[]{:S(2)}, u32[]{:S(2)}) collective-permute-start(bf16[2,4,64,128]{3,2,1,0:T(8,128)(2,1)} %get-tuple-element.71), channel_id=1, source_target_pairs={{0,20},{4,16},{8,28},{12,24},{16,4},{20,0},{24,12},{28,8},{1,21},{... | collective-permute-start | bytes 393224 | tf_op jit(solution)/shard_map/ppermute | solution.py:335
  98.2 10.2 %collective-permute-start.16 = (bf16[2,4,64,128]{3,2,1,0:T(8,128)(2,1)}, bf16[2,4,64,128]{3,2,1,0:T(8,128)(2,1)S(1)}, u32[]{:S(2)}, u32[]{:S(2)}) collective-permute-start(bf16[2,4,64,128]{3,2,1,0:T(8,128)(2,1)} %get-tuple-element.72), channel_id=1, source_target_pairs={{0,24},{4,28},{8,16},{12,20},{16,8},{20,12},{24,0},{28,4},{1,25},{... | collective-permute-start | bytes 393224 | tf_op jit(solution)/shard_map/ppermute | solution.py:335
  102.2 8.0 %collective-permute-start.17 = (bf16[2,4,64,128]{3,2,1,0:T(8,128)(2,1)}, bf16[2,4,64,128]{3,2,1,0:T(8,128)(2,1)S(1)}, u32[]{:S(2)}, u32[]{:S(2)}) collective-permute-start(bf16[2,4,64,128]{3,2,1,0:T(8,128)(2,1)} %get-tuple-element.75), channel_id=1, source_target_pairs={{0,28},{4,24},{8,20},{12,16},{16,12},{20,8},{24,4},{28,0},{1,29},{... | collective-permute-start | bytes 393224 | tf_op jit(solution)/shard_map/ppermute | solution.py:335
  (16 other events, 50.5 us)

commit v6 on v5

--- a/solution.py
+++ b/solution.py
@@ -153,7 +153,7 @@
     return out
 
 
-CHUNK = 32
+CHUNK = 16
 TAIL = 16
 TW_PIECES = 2
 
@@ -183,7 +183,7 @@
     for n in range(pieces):
         if ready:
             ready[n].wait()
-        lax.fori_loop(n * per, (n + 1) * per, body, 0, unroll=min(2, per))
+        lax.fori_loop(n * per, (n + 1) * per, body, 0, unroll=min(4, per))
 
 
 def forward_bins(s, held_k, dft):
@@ -220,7 +220,7 @@
         body(pl.ds(pl.multiple_of(c * CHUNK, CHUNK), CHUNK), c)
         return 0
 
-    lax.fori_loop(0, s.R // CHUNK, step, 0, unroll=2)
+    lax.fori_loop(0, s.R // CHUNK, step, 0, unroll=4)
 
 
 def params(limit=60):

time: 114 us -> 114 us (level)
  no operation moved by 1% of the time
where the time goes in v6:
time: 114 us
  starting transfers between devices  42.4 us (37%)
  Pallas kernels  37.5 us (33%)
  waiting for transfers between devices  29.4 us (26%)
  local copies, waits for them, and re-layouts  3.52 us (3%)
    ppermute x14, starting transfers between devices, swap_partners(): out[x] = lax.ppermute(part, 'bins', [(b, b ^ x) for b in range(s.B)])  23.3 us
    ppermute x14, waiting for transfers between devices, swap_partners(): out[x] = lax.ppermute(part, 'bins', [(b, b ^ x) for b in range(s.B)])  18.5 us
    ppermute x1, waiting for transfers between devices, shards(): lax.ppermute(out_grad, 'chan', [(c, c ^ h) for c in range(nchan)])  10.4 us
    pallas_call x1, Pallas kernels, shards(): pl.pallas_call(functools.partial(products_kernel, s), out_shape=[jax.Shap...  9.91 us
    all_to_all x2, starting transfers between devices, exchange(): return lax.all_to_all(v, 'bins', split_axis=0, concat_axis=0, tiled=True)  9.6 us
    pallas_call x1, Pallas kernels, shards(): pl.pallas_call(functools.partial(token_kernel, s), out_shape=[pltpu.HBM(s...  8.77 us
    ppermute x1, starting transfers between devices, swap_halves(): return lax.ppermute(away, 'bins', [(b, b ^ s.B // 2) for b in range(s.B)])  6.5 us
    pallas_call x1, Pallas kernels, shards(): pl.pallas_call(functools.partial(spectrum_kernel, s), out_shape=[pltpu.HB...  5.16 us
  transfers between devices with their start and end apart: 20, of which 6 were waited for; matrix products, arithmetic and copies ran while one was open for 0% of the time, Pallas kernels for 30%

profile of v6, /device:TPU:0, one launch (start us, length us, event | category | flops | bytes accessed | tf_op | source)
XLA Modules:
  0.0 113.9 jit_solution(12125151959046688790)
XLA Ops:
  0.6 3.0 %collective-permute-start = (bf16[512,1024]{1,0:T(8,128)(2,1)}, bf16[512,1024]{1,0:T(8,128)(2,1)S(1)}, u32[]{:S(2)}, u32[]{:S(2)}) collective-permute-start(bf16[512,1024]{1,0:T(8,128)(2,1)} %refs_0_.3), channel_id=1, source_target_pairs={{0,2},{1,3},{2,0},{3,1},{4,6},{5,7},{6,4},{7,5},{8,10},{9,11},{10,... | collective-permute-start | bytes 3145736 | tf_op jit(solution)/shard_map/ppermute | solution.py:802
  3.6 2.4 %pack_channels.1 = bf16[8,528,128]{2,1,0:T(8,128)(2,1)} custom-call(bf16[512,512]{1,0:T(8,128)(2,1)} %refs_0_.2, bf16[512,512]{1,0:T(8,128)(2,1)} %refs_1_.3, s32[8,64]{1,0:T(8,128)} %refs_2_.2, s32[8,64]{1,0:T(8,128)} %refs_3_.2), custom_call_target="tpu_custom_call" | custom-call | flops 2097152 | bytes 2097152 | tf_op jit(solution)/shard_map/pack_channels/pallas_call | solution.py:284
  6.0 5.8 %all-to-all-start = ((bf16[8,528,128]{2,1,0:T(8,128)(2,1)}), bf16[8,528,128]{2,1,0:T(8,128)(2,1)}, u32[]{:S(2)}, u32[]{:S(2)}) async-start(bf16[8,528,128]{2,1,0:T(8,128)(2,1)} %pack_channels.1), calls=%async_computation | async-start | bytes 2162688 | tf_op jit(solution)/shard_map/all_to_all | solution.py:783
  13.3 2.2 %copy-done = bf16[512,4096]{1,0:T(8,128)(2,1)S(1)} copy-done((bf16[512,4096]{1,0:T(8,128)(2,1)S(1)}, bf16[512,4096]{1,0:T(8,128)(2,1)}, u32[]{:S(2)}) %copy-start) | copy-done | bytes 4194328
  16.6 10.4 %collective-permute-done.refs_1_ = bf16[512,1024]{1,0:T(8,128)(2,1)S(1)} collective-permute-done((bf16[512,1024]{1,0:T(8,128)(2,1)}, bf16[512,1024]{1,0:T(8,128)(2,1)S(1)}, u32[]{:S(2)}, u32[]{:S(2)}) %collective-permute-start) | collective-permute-done | bytes 1048608 | tf_op jit(solution)/shard_map/ppermute | solution.py:802
  27.0 2.1 %project_part.3.refs_2_ = f32[512,512]{1,0:T(8,128)S(1)} custom-call(bf16[512,1024]{1,0:T(8,128)(2,1)S(1)} %collective-permute-done.2.refs_0_, bf16[512,1024]{1,0:T(8,128)(2,1)S(1)} %collective-permute-done.refs_1_, bf16[512,4096]{1,0:T(8,128)(2,1)S(1)} %copy-done.1, f32[512,512]{1,0:T(8,128)S(1)} %project_part.2.refs_3_), custom_call_target="tpu_custom_call" | custom-call | flops 524288 | bytes 262144 | tf_op jit(solution)/shard_map/project_part/pallas_call | solution.py:399
  29.7 2.4 %project_finish.1 = (bf16[256,128]{1,0:T(8,128)(2,1)}, bf16[256,128]{1,0:T(8,128)(2,1)}, bf16[256,128]{1,0:T(8,128)(2,1)}, bf16[256,128]{1,0:T(8,128)(2,1)}, bf1...) custom-call(bf16[512,1024]{1,0:T(8,128)(2,1)S(1)} %collective-permut, ...), custom_call_target="tpu_custom_call" | custom-call | flops 262144 | bytes 262144 | tf_op jit(solution)/shard_map/project_finish/pallas_call | solution.py:456
  32.1 1.9 %collective-permute-start.7 = (bf16[256,128]{1,0:T(8,128)(2,1)}, bf16[256,128]{1,0:T(8,128)(2,1)S(1)}, u32[]{:S(2)}, u32[]{:S(2)}) collective-permute-start(bf16[256,128]{1,0:T(8,128)(2,1)} %get-tuple-element.53), channel_id=1, source_target_pairs={{0,8},{4,12},{8,0},{12,4},{16,24},{20,28},{24,16},{28,20},{1,9},{5... | collective-permute-start | bytes 196616 | tf_op jit(solution)/shard_map/ppermute | solution.py:335
  34.0 3.4 %collective-permute-start.6 = (bf16[256,128]{1,0:T(8,128)(2,1)}, bf16[256,128]{1,0:T(8,128)(2,1)S(1)}, u32[]{:S(2)}, u32[]{:S(2)}) collective-permute-start(bf16[256,128]{1,0:T(8,128)(2,1)} %get-tuple-element.49), channel_id=1, source_target_pairs={{0,28},{4,24},{8,20},{12,16},{16,12},{20,8},{24,4},{28,0},{1,29},{... | collective-permute-start | bytes 196616 | tf_op jit(solution)/shard_map/ppermute | solution.py:335
  37.4 2.9 %collective-permute-start.4 = (bf16[256,128]{1,0:T(8,128)(2,1)}, bf16[256,128]{1,0:T(8,128)(2,1)S(1)}, u32[]{:S(2)}, u32[]{:S(2)}) collective-permute-start(bf16[256,128]{1,0:T(8,128)(2,1)} %get-tuple-element.46), channel_id=1, source_target_pairs={{0,20},{4,16},{8,28},{12,24},{16,4},{20,0},{24,12},{28,8},{1,21},{... | collective-permute-start | bytes 196616 | tf_op jit(solution)/shard_map/ppermute | solution.py:335
  43.2 5.2 %filter_spectrum.1 = (f32[9,2,256,128]{3,2,1,0:T(8,128)}, bf16[8,256,128]{2,1,0:T(8,128)(2,1)}, bf16[8,16,128]{2,1,0:T(8,128)(2,1)}) custom-call(bf16[8,528,128]{2,1,0:T(8,128)(2,1)} %all-to-all-done.xh_at, bf16[512,256]{1,0:T(8,128)(2,1)} %constant.6.clone.dft_at.refs_11_, f32[9,2,256,128]{3,2,1,0:T(8,128)} %constant.7.clone.tw_at.refs_12_, ...), custom_call_target="tpu_custom_call" | custom-call | flops 6039797760 | bytes 4718592 | tf_op jit(solution)/shard_map/filter_spectrum/pallas_call | solution.py:816
  48.5 6.5 %collective-permute-start.10 = (bf16[256,512]{1,0:T(8,128)(2,1)S(1)}, bf16[256,512]{1,0:T(8,128)(2,1)S(1)}, u32[]{:S(2)}, u32[]{:S(2)}) collective-permute-start(bf16[256,512]{1,0:T(8,128)(2,1)S(1)} %copy-done.12), channel_id=1, source_target_pairs={{0,16},{4,20},{8,24},{12,28},{16,0},{20,4},{24,8},{28,12},{1,17},{... | collective-permute-start | bytes 786440 | tf_op jit(solution)/shard_map/ppermute | solution.py:475
  55.7 8.8 %token_products.1 = (f32[9,2,256,128]{3,2,1,0:T(8,128)}, bf16[8,512,128]{2,1,0:T(8,128)(2,1)}) custom-call(bf16[256,128]{1,0:T(8,128)(2,1)} %copy-done.15, bf16[256,128]{1,0:T(8,128)(2,1)} %copy-done.16, bf16[256,128]{1,0:T(8,128)(2,1)} %copy-done.17, bf16[256,128]{1,0:T(8,128)(2,1)} %copy-done.14, bf16[256,128]{1,0:T(8,128)(2,1)} %get-tuple-element.51.refs_4_, ...), custom_call_target="tpu_custom_call" | custom-call | flops 12079595520 | bytes 7077888 | tf_op jit(solution)/shard_map/token_products/pallas_call | solution.py:845
  64.5 3.8 %all-to-all-start.1 = ((bf16[8,512,128]{2,1,0:T(8,128)(2,1)}), bf16[8,512,128]{2,1,0:T(8,128)(2,1)S(1)}, u32[]{:S(2)}, u32[]{:S(2)}) async-start(bf16[8,512,128]{2,1,0:T(8,128)(2,1)} %get-tuple-element.74), calls=%async_computation.1 | async-start | bytes 2097152 | tf_op jit(solution)/shard_map/all_to_all | solution.py:783
  68.2 9.9 %conv_and_filter.1 = (bf16[4,4,64,128]{3,2,1,0:T(8,128)(2,1)}, bf16[4,4,64,128]{3,2,1,0:T(8,128)(2,1)}, bf16[4,4,64,128]{3,2,1,0:T(8,128)(2,1)}, bf16[4,4,64,128...) custom-call(bf16[8,256,128]{2,1,0:T(8,128)(2,1)} %get-tuple-element., ...), custom_call_target="tpu_custom_call" | custom-call | flops 1811939328 | bytes 9437184 | tf_op jit(solution)/shard_map/conv_and_filter/pallas_call | solution.py:875
  78.2 1.8 %collective-permute-start.11 = (bf16[4,4,64,128]{3,2,1,0:T(8,128)(2,1)}, bf16[4,4,64,128]{3,2,1,0:T(8,128)(2,1)S(1)}, u32[]{:S(2)}, u32[]{:S(2)}) collective-permute-start(bf16[4,4,64,128]{3,2,1,0:T(8,128)(2,1)} %get-tuple-element.66), channel_id=1, source_target_pairs={{0,8},{4,12},{8,0},{12,4},{16,24},{20,28},{24,16},{28,20},{1,9},{5... | collective-permute-start | bytes 786440 | tf_op jit(solution)/shard_map/ppermute | solution.py:335
  80.0 2.4 %collective-permute-start.14 = (bf16[2,4,64,128]{3,2,1,0:T(8,128)(2,1)}, bf16[2,4,64,128]{3,2,1,0:T(8,128)(2,1)S(1)}, u32[]{:S(2)}, u32[]{:S(2)}) collective-permute-start(bf16[2,4,64,128]{3,2,1,0:T(8,128)(2,1)} %get-tuple-element.70), channel_id=1, source_target_pairs={{0,16},{4,20},{8,24},{12,28},{16,0},{20,4},{24,8},{28,12},{1,17},{... | collective-permute-start | bytes 393224 | tf_op jit(solution)/shard_map/ppermute | solution.py:335
  83.8 10.4 %collective-permute-done.11.refs_2_ = bf16[4,4,64,128]{3,2,1,0:T(8,128)(2,1)S(1)} collective-permute-done((bf16[4,4,64,128]{3,2,1,0:T(8,128)(2,1)}, bf16[4,4,64,128]{3,2,1,0:T(8,128)(2,1)S(1)}, u32[]{:S(2)}, u32[]{:S(2)}) %collective-permute-start.11) | collective-permute-done | bytes 262176 | tf_op jit(solution)/shard_map/ppermute | solution.py:335
  95.3 2.8 %collective-permute-start.15 = (bf16[2,4,64,128]{3,2,1,0:T(8,128)(2,1)}, bf16[2,4,64,128]{3,2,1,0:T(8,128)(2,1)S(1)}, u32[]{:S(2)}, u32[]{:S(2)}) collective-permute-start(bf16[2,4,64,128]{3,2,1,0:T(8,128)(2,1)} %get-tuple-element.71), channel_id=1, source_target_pairs={{0,20},{4,16},{8,28},{12,24},{16,4},{20,0},{24,12},{28,8},{1,21},{... | collective-permute-start | bytes 393224 | tf_op jit(solution)/shard_map/ppermute | solution.py:335
  99.8 2.4 %collective-permute-done.14.refs_4_ = bf16[2,4,64,128]{3,2,1,0:T(8,128)(2,1)S(1)} collective-permute-done((bf16[2,4,64,128]{3,2,1,0:T(8,128)(2,1)}, bf16[2,4,64,128]{3,2,1,0:T(8,128)(2,1)S(1)}, u32[]{:S(2)}, u32[]{:S(2)}) %collective-permute-start.14) | collective-permute-done | bytes 131104 | tf_op jit(solution)/shard_map/ppermute | solution.py:335
  102.2 2.2 %collective-permute-start.17 = (bf16[2,4,64,128]{3,2,1,0:T(8,128)(2,1)}, bf16[2,4,64,128]{3,2,1,0:T(8,128)(2,1)S(1)}, u32[]{:S(2)}, u32[]{:S(2)}) collective-permute-start(bf16[2,4,64,128]{3,2,1,0:T(8,128)(2,1)} %get-tuple-element.75), channel_id=1, source_target_pairs={{0,28},{4,24},{8,20},{12,16},{16,12},{20,8},{24,4},{28,0},{1,29},{... | collective-permute-start | bytes 393224 | tf_op jit(solution)/shard_map/ppermute | solution.py:335
  104.4 4.0 %collective-permute-done.15.refs_5_ = bf16[2,4,64,128]{3,2,1,0:T(8,128)(2,1)S(1)} collective-permute-done((bf16[2,4,64,128]{3,2,1,0:T(8,128)(2,1)}, bf16[2,4,64,128]{3,2,1,0:T(8,128)(2,1)S(1)}, u32[]{:S(2)}, u32[]{:S(2)}) %collective-permute-start.15) | collective-permute-done | bytes 131104 | tf_op jit(solution)/shard_map/ppermute | solution.py:335
  108.5 1.7 %collective-permute-done.17.refs_7_ = bf16[2,4,64,128]{3,2,1,0:T(8,128)(2,1)S(1)} collective-permute-done((bf16[2,4,64,128]{3,2,1,0:T(8,128)(2,1)}, bf16[2,4,64,128]{3,2,1,0:T(8,128)(2,1)S(1)}, u32[]{:S(2)}, u32[]{:S(2)}) %collective-permute-start.17) | collective-permute-done | bytes 131104 | tf_op jit(solution)/shard_map/ppermute | solution.py:335
  110.8 2.9 %columns.1 = (bf16[8,64,512]{2,1,0:T(8,128)(2,1)}, f32[8,64,512]{2,1,0:T(8,128)}) custom-call(bf16[4,4,64,128]{3,2,1,0:T(8,128)(2,1)} %get-tuple-element.64.refs_0_, bf16[4,4,64,128]{3,2,1,0:T(8,128)(2,1)} %copy-done.6, bf16[4,4,64,128]{3,2,1,0:T(8,128)(2,1)} %copy-done.4, bf16[4,4,64,128]{3,2,1,0:T(8,128)(2,1)} %copy-done.5, ...), custom_call_target="tpu_custom_call" | custom-call | flops 2097152 | bytes 3145728 | tf_op jit(solution)/shard_map/columns/pallas_call | solution.py:759
  (66 shorter events, 11.6 us)
Async XLA Ops:
  0.6 11.2 %copy-start.2 = (bf16[512,1024]{1,0:T(8,128)(2,1)S(1)}, bf16[512,1024]{1,0:T(8,128)(2,1)}, u32[]{:S(2)}) copy-start(bf16[512,1024]{1,0:T(8,128)(2,1)} %refs_0_.3) | copy-start | bytes 3145732
  0.6 26.4 %collective-permute-start = (bf16[512,1024]{1,0:T(8,128)(2,1)}, bf16[512,1024]{1,0:T(8,128)(2,1)S(1)}, u32[]{:S(2)}, u32[]{:S(2)}) collective-permute-start(bf16[512,1024]{1,0:T(8,128)(2,1)} %refs_0_.3), channel_id=1, source_target_pairs={{0,2},{1,3},{2,0},{3,1},{4,6},{5,7},{6,4},{7,5},{8,10},{9,11},{10,... | collective-permute-start | bytes 3145736 | tf_op jit(solution)/shard_map/ppermute | solution.py:802
  6.0 37.2 %all-to-all-start = ((bf16[8,528,128]{2,1,0:T(8,128)(2,1)}), bf16[8,528,128]{2,1,0:T(8,128)(2,1)}, u32[]{:S(2)}, u32[]{:S(2)}) async-start(bf16[8,528,128]{2,1,0:T(8,128)(2,1)} %pack_channels.1), calls=%async_computation | async-start | bytes 2162688 | tf_op jit(solution)/shard_map/all_to_all | solution.py:783
  11.9 15.1 %collective-permute-start.2 = (bf16[512,1024]{1,0:T(8,128)(2,1)S(1)}, bf16[512,1024]{1,0:T(8,128)(2,1)S(1)}, u32[]{:S(2)}, u32[]{:S(2)}) collective-permute-start(bf16[512,1024]{1,0:T(8,128)(2,1)S(1)} %copy-done.2), channel_id=1, source_target_pairs={{0,1},{1,0},{2,3},{3,2},{4,5},{5,4},{6,7},{7,6},{8,9},{9,8},{10,11... | collective-permute-start | bytes 3145736 | tf_op jit(solution)/shard_map/ppermute | solution.py:803
  15.5 11.6 %copy-start.1 = (bf16[512,4096]{1,0:T(8,128)(2,1)S(1)}, bf16[512,4096]{1,0:T(8,128)(2,1)}, u32[]{:S(2)}) copy-start(bf16[512,4096]{1,0:T(8,128)(2,1)} %refs_1_.5) | copy-start | bytes 12582916
  16.6 13.1 %copy-start.3 = (bf16[512,512]{1,0:T(8,128)(2,1)S(1)}, bf16[512,512]{1,0:T(8,128)(2,1)}, u32[]{:S(2)}) copy-start(bf16[512,512]{1,0:T(8,128)(2,1)} %refs_3_.3) | copy-start | bytes 1572868
  27.0 2.7 %collective-permute-start.1 = (bf16[512,1024]{1,0:T(8,128)(2,1)S(1)}, bf16[512,1024]{1,0:T(8,128)(2,1)S(1)}, u32[]{:S(2)}, u32[]{:S(2)}) collective-permute-start(bf16[512,1024]{1,0:T(8,128)(2,1)S(1)} %collective-permute-done.refs_1_), channel_id=1, source_target_pairs={{0,1},{1,0},{2,3},{3,2},{4,5},{5,4},{6,7},{7,6},{8,9},{9,8},{10,11... | collective-permute-start | bytes 3145736 | tf_op jit(solution)/shard_map/ppermute | solution.py:807
  32.1 9.5 %collective-permute-start.7 = (bf16[256,128]{1,0:T(8,128)(2,1)}, bf16[256,128]{1,0:T(8,128)(2,1)S(1)}, u32[]{:S(2)}, u32[]{:S(2)}) collective-permute-start(bf16[256,128]{1,0:T(8,128)(2,1)} %get-tuple-element.53), channel_id=1, source_target_pairs={{0,8},{4,12},{8,0},{12,4},{16,24},{20,28},{24,16},{28,20},{1,9},{5... | collective-permute-start | bytes 196616 | tf_op jit(solution)/shard_map/ppermute | solution.py:335
  34.0 8.0 %collective-permute-start.6 = (bf16[256,128]{1,0:T(8,128)(2,1)}, bf16[256,128]{1,0:T(8,128)(2,1)S(1)}, u32[]{:S(2)}, u32[]{:S(2)}) collective-permute-start(bf16[256,128]{1,0:T(8,128)(2,1)} %get-tuple-element.49), channel_id=1, source_target_pairs={{0,28},{4,24},{8,20},{12,16},{16,12},{20,8},{24,4},{28,0},{1,29},{... | collective-permute-start | bytes 196616 | tf_op jit(solution)/shard_map/ppermute | solution.py:335
  37.4 11.0 %collective-permute-start.3 = (bf16[256,128]{1,0:T(8,128)(2,1)}, bf16[256,128]{1,0:T(8,128)(2,1)S(1)}, u32[]{:S(2)}, u32[]{:S(2)}) collective-permute-start(bf16[256,128]{1,0:T(8,128)(2,1)} %get-tuple-element.45), channel_id=1, source_target_pairs={{0,16},{4,20},{8,24},{12,28},{16,0},{20,4},{24,8},{28,12},{1,17},{... | collective-permute-start | bytes 196616 | tf_op jit(solution)/shard_map/ppermute | solution.py:335
  37.4 17.6 %collective-permute-start.4 = (bf16[256,128]{1,0:T(8,128)(2,1)}, bf16[256,128]{1,0:T(8,128)(2,1)S(1)}, u32[]{:S(2)}, u32[]{:S(2)}) collective-permute-start(bf16[256,128]{1,0:T(8,128)(2,1)} %get-tuple-element.46), channel_id=1, source_target_pairs={{0,20},{4,16},{8,28},{12,24},{16,4},{20,0},{24,12},{28,8},{1,21},{... | collective-permute-start | bytes 196616 | tf_op jit(solution)/shard_map/ppermute | solution.py:335
  40.3 14.7 %collective-permute-start.5 = (bf16[256,128]{1,0:T(8,128)(2,1)}, bf16[256,128]{1,0:T(8,128)(2,1)S(1)}, u32[]{:S(2)}, u32[]{:S(2)}) collective-permute-start(bf16[256,128]{1,0:T(8,128)(2,1)} %get-tuple-element.47), channel_id=1, source_target_pairs={{0,24},{4,28},{8,16},{12,20},{16,8},{20,12},{24,0},{28,4},{1,25},{... | collective-permute-start | bytes 196616 | tf_op jit(solution)/shard_map/ppermute | solution.py:335
  41.6 13.4 %collective-permute-start.8 = (bf16[256,128]{1,0:T(8,128)(2,1)}, bf16[256,128]{1,0:T(8,128)(2,1)S(1)}, u32[]{:S(2)}, u32[]{:S(2)}) collective-permute-start(bf16[256,128]{1,0:T(8,128)(2,1)} %get-tuple-element.55), channel_id=1, source_target_pairs={{0,12},{4,8},{8,4},{12,0},{16,28},{20,24},{24,20},{28,16},{1,13},{... | collective-permute-start | bytes 196616 | tf_op jit(solution)/shard_map/ppermute | solution.py:335
  42.0 13.0 %collective-permute-start.9 = (bf16[256,128]{1,0:T(8,128)(2,1)}, bf16[256,128]{1,0:T(8,128)(2,1)S(1)}, u32[]{:S(2)}, u32[]{:S(2)}) collective-permute-start(bf16[256,128]{1,0:T(8,128)(2,1)} %get-tuple-element.56), channel_id=1, source_target_pairs={{0,4},{4,0},{8,12},{12,8},{16,20},{20,16},{24,28},{28,24},{1,5},{5... | collective-permute-start | bytes 196616 | tf_op jit(solution)/shard_map/ppermute | solution.py:335
  48.5 16.0 %collective-permute-start.10 = (bf16[256,512]{1,0:T(8,128)(2,1)S(1)}, bf16[256,512]{1,0:T(8,128)(2,1)S(1)}, u32[]{:S(2)}, u32[]{:S(2)}) collective-permute-start(bf16[256,512]{1,0:T(8,128)(2,1)S(1)} %copy-done.12), channel_id=1, source_target_pairs={{0,16},{4,20},{8,24},{12,28},{16,0},{20,4},{24,8},{28,12},{1,17},{... | collective-permute-start | bytes 786440 | tf_op jit(solution)/shard_map/ppermute | solution.py:475
  64.5 33.9 %all-to-all-start.1 = ((bf16[8,512,128]{2,1,0:T(8,128)(2,1)}), bf16[8,512,128]{2,1,0:T(8,128)(2,1)S(1)}, u32[]{:S(2)}, u32[]{:S(2)}) async-start(bf16[8,512,128]{2,1,0:T(8,128)(2,1)} %get-tuple-element.74), calls=%async_computation.1 | async-start | bytes 2097152 | tf_op jit(solution)/shard_map/all_to_all | solution.py:783
  78.2 16.0 %collective-permute-start.11 = (bf16[4,4,64,128]{3,2,1,0:T(8,128)(2,1)}, bf16[4,4,64,128]{3,2,1,0:T(8,128)(2,1)S(1)}, u32[]{:S(2)}, u32[]{:S(2)}) collective-permute-start(bf16[4,4,64,128]{3,2,1,0:T(8,128)(2,1)} %get-tuple-element.66), channel_id=1, source_target_pairs={{0,8},{4,12},{8,0},{12,4},{16,24},{20,28},{24,16},{28,20},{1,9},{5... | collective-permute-start | bytes 786440 | tf_op jit(solution)/shard_map/ppermute | solution.py:335
  80.0 22.2 %collective-permute-start.14 = (bf16[2,4,64,128]{3,2,1,0:T(8,128)(2,1)}, bf16[2,4,64,128]{3,2,1,0:T(8,128)(2,1)S(1)}, u32[]{:S(2)}, u32[]{:S(2)}) collective-permute-start(bf16[2,4,64,128]{3,2,1,0:T(8,128)(2,1)} %get-tuple-element.70), channel_id=1, source_target_pairs={{0,16},{4,20},{8,24},{12,28},{16,0},{20,4},{24,8},{28,12},{1,17},{... | collective-permute-start | bytes 393224 | tf_op jit(solution)/shard_map/ppermute | solution.py:335
  82.3 26.1 %collective-permute-start.13 = (bf16[4,4,64,128]{3,2,1,0:T(8,128)(2,1)}, bf16[4,4,64,128]{3,2,1,0:T(8,128)(2,1)S(1)}, u32[]{:S(2)}, u32[]{:S(2)}) collective-permute-start(bf16[4,4,64,128]{3,2,1,0:T(8,128)(2,1)} %get-tuple-element.69), channel_id=1, source_target_pairs={{0,12},{4,8},{8,4},{12,0},{16,28},{20,24},{24,20},{28,16},{1,13},{... | collective-permute-start | bytes 786440 | tf_op jit(solution)/shard_map/ppermute | solution.py:335
  94.2 16.0 %copy-start.4 = (bf16[4,4,64,128]{3,2,1,0:T(8,128)(2,1)}, bf16[4,4,64,128]{3,2,1,0:T(8,128)(2,1)S(1)}, u32[]{:S(2)}) copy-start(bf16[4,4,64,128]{3,2,1,0:T(8,128)(2,1)S(1)} %collective-permute-done.11.refs_2_) | copy-start | bytes 786436
  94.2 14.3 %collective-permute-start.12 = (bf16[4,4,64,128]{3,2,1,0:T(8,128)(2,1)}, bf16[4,4,64,128]{3,2,1,0:T(8,128)(2,1)S(1)}, u32[]{:S(2)}, u32[]{:S(2)}) collective-permute-start(bf16[4,4,64,128]{3,2,1,0:T(8,128)(2,1)} %get-tuple-element.67), channel_id=1, source_target_pairs={{0,4},{4,0},{8,12},{12,8},{16,20},{20,16},{24,28},{28,24},{1,5},{5... | collective-permute-start | bytes 786440 | tf_op jit(solution)/shard_map/ppermute | solution.py:335
  95.3 13.1 %collective-permute-start.15 = (bf16[2,4,64,128]{3,2,1,0:T(8,128)(2,1)}, bf16[2,4,64,128]{3,2,1,0:T(8,128)(2,1)S(1)}, u32[]{:S(2)}, u32[]{:S(2)}) collective-permute-start(bf16[2,4,64,128]{3,2,1,0:T(8,128)(2,1)} %get-tuple-element.71), channel_id=1, source_target_pairs={{0,20},{4,16},{8,28},{12,24},{16,4},{20,0},{24,12},{28,8},{1,21},{... | collective-permute-start | bytes 393224 | tf_op jit(solution)/shard_map/ppermute | solution.py:335
  98.2 10.3 %collective-permute-start.16 = (bf16[2,4,64,128]{3,2,1,0:T(8,128)(2,1)}, bf16[2,4,64,128]{3,2,1,0:T(8,128)(2,1)S(1)}, u32[]{:S(2)}, u32[]{:S(2)}) collective-permute-start(bf16[2,4,64,128]{3,2,1,0:T(8,128)(2,1)} %get-tuple-element.72), channel_id=1, source_target_pairs={{0,24},{4,28},{8,16},{12,20},{16,8},{20,12},{24,0},{28,4},{1,25},{... | collective-permute-start | bytes 393224 | tf_op jit(solution)/shard_map/ppermute | solution.py:335
  102.2 8.0 %collective-permute-start.17 = (bf16[2,4,64,128]{3,2,1,0:T(8,128)(2,1)}, bf16[2,4,64,128]{3,2,1,0:T(8,128)(2,1)S(1)}, u32[]{:S(2)}, u32[]{:S(2)}) collective-permute-start(bf16[2,4,64,128]{3,2,1,0:T(8,128)(2,1)} %get-tuple-element.75), channel_id=1, source_target_pairs={{0,28},{4,24},{8,20},{12,16},{16,12},{20,8},{24,4},{28,0},{1,29},{... | collective-permute-start | bytes 393224 | tf_op jit(solution)/shard_map/ppermute | solution.py:335
  (16 other events, 50.6 us)
